TPU v7x, 32 devices: a whole 2x2x4 slice. The times are simulated.
32 devices in a mesh: grp: 2 (over y), blk: 16 (over z, x, core).
Axes of the slice: x: 2, y: 2, z: 4, core: 2. Of those that a mesh axis runs over, the one named last changes fastest.
Arguments:
- tokens: bfloat16 [4096, 2048], P(('grp', 'blk')), may hold values from -6 to 6
- d_out: bfloat16 [4096, 2048], P(('grp', 'blk')), may hold values from -6 to 6
- expert_ids: int32 [4096, 6], P(('grp', 'blk')), may hold values from 0 to 15, all different within a row; in each aligned block of 128 rows (0 to 127, 128 to 255, ...) at most 52 rows name the same one
- gate_values: bfloat16 [4096, 6], P(('grp', 'blk')), may hold values from 0.049804688 to 0.44921875
- saved_gate_pre: bfloat16 [4096, 6, 704], P(('grp', 'blk')), may hold values from -6 to 6
- saved_up_pre: bfloat16 [4096, 6, 704], P(('grp', 'blk')), may hold values from -6 to 6
- w_gate: bfloat16 [16, 2048, 704], P('blk'), may hold values from -0.125 to 0.125
- w_up: bfloat16 [16, 2048, 704], P('blk'), may hold values from -0.125 to 0.125
- w_down: bfloat16 [16, 704, 2048], P('blk'), may hold values from -0.21875 to 0.21875
Outputs:
- d_tokens: bfloat16 [4096, 2048], P(('grp', 'blk'))
- d_w_gate: bfloat16 [16, 2048, 704], P('blk', 'grp')
- d_w_up: bfloat16 [16, 2048, 704], P('blk', 'grp')
- d_w_down: bfloat16 [16, 704, 2048], P('blk', None, 'grp')
Inputs may be any that keep to these rules, and one draw needn't show every extreme that they name: `expert_ids`: within the 128 rows of one device no expert is named more than 52 times, a bound that some block reaches; the 6 ids of a token differ.
All inputs are finite; a program needn't handle non-finite values.
Results may differ from a plain program's by a relative error of at most 0.0057.
Values may be sent and summed in bfloat16 or wider, within the bound.
No kernel may reach another device: no remote copies, remote signals or barrier semaphores. Data moves between devices by JAX's collectives and lax.ppermute only.
A program may use at most 192 MiB of HBM per device.

v0:
```python
import jax
import jax.numpy as jnp
from jax import lax
from jax.sharding import PartitionSpec as P


def expert_side(cotangents, weights, gate_pre, up_pre, w_gate, w_up, w_down):
    sigmoid_gate = jax.nn.sigmoid(gate_pre)
    active = gate_pre * sigmoid_gate
    scale_col = weights[:, :, None]
    scaled_hidden = (scale_col * active * up_pre).astype(jnp.bfloat16)
    back_hidden = scale_col * jnp.einsum(
        "erd,efd->erf", cotangents, w_down, preferred_element_type=jnp.float32
    )
    grad_gate = (
        back_hidden * up_pre * sigmoid_gate * (1.0 + gate_pre * (1.0 - sigmoid_gate))
    ).astype(jnp.bfloat16)
    grad_up = (back_hidden * active).astype(jnp.bfloat16)
    route_grad = (
        jnp.einsum("erf,edf->erd", grad_gate, w_gate, preferred_element_type=jnp.float32)
        + jnp.einsum("erf,edf->erd", grad_up, w_up, preferred_element_type=jnp.float32)
    ).astype(jnp.bfloat16)
    return (route_grad, grad_gate, grad_up, scaled_hidden)


def per_device(
    tokens, d_out, expert_ids, gate_values, saved_gate_pre, saved_up_pre, w_gate, w_up, w_down
):
    tok_dev, model_width = tokens.shape
    top_count = expert_ids.shape[1]
    ffw_width = saved_gate_pre.shape[2]
    blk_count = lax.axis_size("blk")
    exp_dev = w_gate.shape[0]
    expert_count = exp_dev * blk_count
    slot_count = 13 * tok_dev // (2 * expert_count)
    buffer_rows = expert_count * slot_count
    route_count = tok_dev * top_count
    flat_ids = expert_ids.reshape(-1)
    onehot = (flat_ids[:, None] == jnp.arange(expert_count, dtype=jnp.int32)[None, :]).astype(
        jnp.int32
    )
    before = jnp.cumsum(onehot, axis=0) - onehot
    slot_index = jnp.sum(before * onehot, axis=1)
    target = flat_ids * slot_count + slot_index
    slot_route = (
        jnp.zeros((buffer_rows,), jnp.int32)
        .at[target]
        .set(jnp.arange(route_count, dtype=jnp.int32))
    )
    filled = jnp.zeros((buffer_rows,), jnp.bool_).at[target].set(True)
    token_row = slot_route // top_count

    def pick(table, rows):
        taken = table[rows]
        return jnp.where(
            filled.reshape((buffer_rows,) + (1,) * (taken.ndim - 1)), taken, jnp.zeros_like(taken)
        )

    send_inputs = pick(tokens, token_row)
    send_grads = pick(d_out, token_row)
    send_gate_pre = pick(saved_gate_pre.reshape(route_count, ffw_width), slot_route)
    send_up_pre = pick(saved_up_pre.reshape(route_count, ffw_width), slot_route)
    send_gate = pick(gate_values.reshape(-1), slot_route)
    per_peer = exp_dev * slot_count
    recv_inputs, recv_grads, recv_gpre, recv_upre, recv_gate = (
        lax.all_to_all(
            send_inputs.reshape(blk_count, per_peer, model_width),
            "blk",
            split_axis=0,
            concat_axis=0,
            tiled=True,
        ),
        lax.all_to_all(
            send_grads.reshape(blk_count, per_peer, model_width),
            "blk",
            split_axis=0,
            concat_axis=0,
            tiled=True,
        ),
        lax.all_to_all(
            send_gate_pre.reshape(blk_count, per_peer, ffw_width),
            "blk",
            split_axis=0,
            concat_axis=0,
            tiled=True,
        ),
        lax.all_to_all(
            send_up_pre.reshape(blk_count, per_peer, ffw_width),
            "blk",
            split_axis=0,
            concat_axis=0,
            tiled=True,
        ),
        lax.all_to_all(
            send_gate.reshape(blk_count, per_peer), "blk", split_axis=0, concat_axis=0, tiled=True
        ),
    )
    local_rows = blk_count * slot_count

    def to_expert(array):
        shaped = array.reshape((blk_count, exp_dev, slot_count) + array.shape[2:])
        moved = jnp.swapaxes(shaped, 0, 1)
        return moved.reshape((exp_dev, local_rows) + array.shape[2:])

    inputs = to_expert(recv_inputs)
    cotangents = to_expert(recv_grads)
    gate_pre = to_expert(recv_gpre).astype(jnp.float32)
    up_pre = to_expert(recv_upre).astype(jnp.float32)
    weights = to_expert(recv_gate).astype(jnp.float32)
    route_grad, grad_gate, grad_up, scaled_hidden = expert_side(
        cotangents, weights, gate_pre, up_pre, w_gate, w_up, w_down
    )
    back_shaped = jnp.swapaxes(
        route_grad.reshape(exp_dev, blk_count, slot_count, model_width), 0, 1
    )
    returned = lax.all_to_all(
        back_shaped.reshape(blk_count, per_peer, model_width),
        "blk",
        split_axis=0,
        concat_axis=0,
        tiled=True,
    )
    by_route = returned.reshape(buffer_rows, model_width)[target].reshape(
        tok_dev, top_count, model_width
    )
    d_tokens = jnp.sum(by_route.astype(jnp.float32), axis=1).astype(jnp.bfloat16)
    term_gate = jnp.einsum("erd,erf->edf", inputs, grad_gate, preferred_element_type=jnp.float32)
    term_up = jnp.einsum("erd,erf->edf", inputs, grad_up, preferred_element_type=jnp.float32)
    term_down = jnp.einsum(
        "erf,erd->efd", scaled_hidden, cotangents, preferred_element_type=jnp.float32
    )
    sum_gate, sum_up, sum_down = (
        lax.psum_scatter(term_gate, "grp", scatter_dimension=1, tiled=True),
        lax.psum_scatter(term_up, "grp", scatter_dimension=1, tiled=True),
        lax.psum_scatter(term_down, "grp", scatter_dimension=2, tiled=True),
    )
    return (
        d_tokens,
        sum_gate.astype(jnp.bfloat16),
        sum_up.astype(jnp.bfloat16),
        sum_down.astype(jnp.bfloat16),
    )


def solution(mesh):
    return jax.shard_map(
        per_device,
        mesh=mesh,
        in_specs=(
            P(("grp", "blk"), None),
            P(("grp", "blk"), None),
            P(("grp", "blk"), None),
            P(("grp", "blk"), None),
            P(("grp", "blk"), None, None),
            P(("grp", "blk"), None, None),
            P("blk", None, None),
            P("blk", None, None),
            P("blk", None, None),
        ),
        out_specs=(
            P(("grp", "blk"), None),
            P("blk", "grp", None),
            P("blk", "grp", None),
            P("blk", None, "grp"),
        ),
        check_vma=False,
    )
```

profile of v0, /device:TPU:10, one launch (start us, length us, event | category | flops | bytes accessed | tf_op | source)
XLA Modules:
  0.0 554.2 jit_solution(5815670729238916260)
XLA Ops:
  7.2 0.9 copy.29
  8.1 0.1 eq.29
  8.3 0.1 eq.25
  8.4 0.7 broadcast_multiply_fusion
  9.1 1.7 reduce-window.6
  10.8 0.3 slice_reduce_fusion
  11.1 0.1 copy.28
  11.2 0.1 mul.114
  11.4 0.1 fusion.9
  11.5 3.4 scatter_custom_fusion.1
  14.9 0.8 copy.32
  15.7 0.2 reshape.268
  15.9 3.4 scatter_custom_fusion
  19.3 5.4 gather_fusion
  24.7 0.7 all_to_all.28
  25.4 6.2 %all-to-all-start = ((bf16[16,1,52]{2,1,0:T(2,128)(2,1)}), bf16[16,1,52]{2,1,0:T(2,128)(2,1)S(1)}, u32[]{:S(2)}, u32[]{:S(2)}) async-start(bf16[16,1,52]{2,1,0:T(2,128)(2,1)} %all_to_all.28), calls=%async_computation | async-start | bytes 16384 | tf_op jit(solution)/shard_map/all_to_all | solution.py:94
  31.7 0.1 broadcast_in_dim.51
  31.8 2.9 copy.36
  34.7 3.3 reshape.272
  38.1 6.2 %gather_fusion.3 = bf16[832,704]{1,0:T(8,128)(2,1)} fusion(bf16[768,704]{1,0:T(8,128)(2,1)} %reshape.272, s32[1024]{0:T(1024)S(1)} %get-tuple-element.13), kind=kCustom, calls=%fused_computation.3 | custom fusion | bytes 2346240 | tf_op jit(solution)/shard_map/gather | solution.py:54
  44.3 2.3 gather.32
  46.6 2.9 copy.34
  49.5 3.3 reshape.271
  52.8 6.2 %gather_fusion.2 = bf16[832,704]{1,0:T(8,128)(2,1)} fusion(bf16[768,704]{1,0:T(8,128)(2,1)} %reshape.271, s32[1024]{0:T(1024)S(1)} %get-tuple-element.13), kind=kCustom, calls=%fused_computation.2 | custom fusion | bytes 2346240 | tf_op jit(solution)/shard_map/gather | solution.py:54
  59.0 2.3 gather.30
  61.3 3.5 broadcast_select_fusion.3
  64.9 38.0 %all_to_all.35 = bf16[16,52,704]{2,1,0:T(8,128)(2,1)} all-to-all(bf16[16,52,704]{2,1,0:T(8,128)(2,1)} %get-tuple-element.10), channel_id=1, replica_groups=mesh['grp'=2,'blk'=16] {'blk'}, dimensions={0} | all-to-all | bytes 2342912 | tf_op jit(solution)/shard_map/all_to_all | solution.py:87
  102.8 5.5 all-to-all-start.3
  108.4 4.9 gather_fusion.1
  113.3 4.7 gather.28
  117.9 4.9 gather_fusion.5
  122.8 4.6 gather.35
  127.4 5.4 broadcast_select_fusion
  132.8 7.4 %all-to-all-done.3 = bf16[16,52,704]{2,1,0:T(8,128)(2,1)} async-done(((bf16[16,52,704]{2,1,0:T(8,128)(2,1)}), bf16[16,52,704]{2,1,0:T(8,128)(2,1)}, u32[]{:S(2)}, u32[]{:S(2)}) %all-to-all-start.3) | async-done | bytes 1171488 | tf_op jit(solution)/shard_map/all_to_all | solution.py:80
  140.2 85.9 %all_to_all.36 = bf16[16,52,2048]{2,1,0:T(8,128)(2,1)} all-to-all(bf16[16,52,2048]{2,1,0:T(8,128)(2,1)} %get-tuple-element.9), channel_id=1, replica_groups=mesh['grp'=2,'blk'=16] {'blk'}, dimensions={0} | all-to-all | bytes 6815744 | tf_op jit(solution)/shard_map/all_to_all | solution.py:73
  226.1 5.4 all-to-all-start.5
  231.6 0.1 reshape.278
  231.7 2.8 reshape.279
  234.4 3.2 copy.35
  237.7 2.7 reshape.280
  240.4 3.2 copy.37
  243.6 4.6 reshape.269
  248.2 9.6 %multiply_convert_fusion.1 = (bf16[832,704]{0,1:T(8,128)(2,1)}, bf16[832,704]{0,1:T(8,128)(2,1)}) fusion(f32[832,704]{0,1:T(8,128)} %copy.37, f32[832]{0:T(1024)S(1)} %reshape.278, f32[832,704]{0,1:T(8,128)} %copy.35, bf16[832,2048]{1,0:T(8,128)(2,1)} %reshape.269, bf16[1,704,2048]{2,1,0:T(8,128)(2,1)} %param.17), kind=kOutput, calls=%fused_computation.20 | convolution fusion | flops 2407342080 | bytes 13323520 | tf_op jit(solution)/shard_map/erd,efd->erf/dot_general | solution.py:12
  257.8 54.8 %all-to-all-done.5 = bf16[16,52,2048]{2,1,0:T(8,128)(2,1)} async-done(((bf16[16,52,2048]{2,1,0:T(8,128)(2,1)}), bf16[16,52,2048]{2,1,0:T(8,128)(2,1)}, u32[]{:S(2)}, u32[]{:S(2)}) %all-to-all-start.5) | async-done | bytes 3407904 | tf_op jit(solution)/shard_map/all_to_all | solution.py:66
  312.6 4.6 reshape.277
  317.1 7.9 %convolution_bitcast_fusion.1 = f32[1,2048,704]{1,2,0:T(8,128)} fusion(bf16[832,704]{0,1:T(8,128)(2,1)} %get-tuple-element.5, bf16[832,2048]{1,0:T(8,128)(2,1)} %reshape.277), kind=kOutput, calls=%fused_computation.12 | convolution fusion | flops 2399141888 | bytes 10346496 | tf_op jit(solution)/shard_map/erd,erf->edf/dot_general | solution.py:127
  325.1 0.3 reduce-scatter.6.cloned.1.call-start
  325.4 8.2 %convolution_bitcast_fusion = f32[1,2048,704]{1,2,0:T(8,128)} fusion(bf16[832,704]{0,1:T(8,128)(2,1)} %get-tuple-element.4, bf16[832,2048]{1,0:T(8,128)(2,1)} %reshape.277), kind=kOutput, calls=%fused_computation.11 | convolution fusion | flops 2399141888 | bytes 10346496 | tf_op jit(solution)/shard_map/erd,erf->edf/dot_general | solution.py:128
  333.6 2.8 reshape.281
  336.4 2.8 reshape.282
  339.2 9.4 %convolution_bitcast_fusion.2 = f32[1,704,2048]{2,1,0:T(8,128)} fusion(bf16[832,2048]{1,0:T(8,128)(2,1)} %reshape.269, f32[1,832,1,1,1,1,704]{6,1,5,4,3,2,0:T(8,128)} %reshape.282, f32[1,832,1,1,1,1,704]{6,1,5,4,3,2,0:T(8,128)} %reshape.281, f32[832]{0:T(1024)S(1)} %reshape.278), kind=kOutput, calls=%fused_computation.13 | convolution fusion | flops 2403241984 | bytes 13864192 | tf_op jit(solution)/shard_map/erf,erd->efd/dot_general | solution.py:129
  348.6 4.3 fusion.1
  353.0 4.5 add_convert_fusion
  357.6 4.7 reshape_transpose_reshape.2
  362.2 5.5 %all-to-all-start.4 = ((bf16[16,52,2048]{2,1,0:T(8,128)(2,1)}), bf16[16,52,2048]{2,1,0:T(8,128)(2,1)}, u32[]{:S(2)}, u32[]{:S(2)}) async-start(bf16[16,52,2048]{2,1,0:T(8,128)(2,1)} %reshape_transpose_reshape.2), calls=%async_computation.4 | async-start | bytes 7340032 | tf_op jit(solution)/shard_map/all_to_all | solution.py:116
  367.8 80.9 %all-to-all-done.4 = bf16[16,52,2048]{2,1,0:T(8,128)(2,1)} async-done(((bf16[16,52,2048]{2,1,0:T(8,128)(2,1)}), bf16[16,52,2048]{2,1,0:T(8,128)(2,1)}, u32[]{:S(2)}, u32[]{:S(2)}) %all-to-all-start.4) | async-done | bytes 3407904 | tf_op jit(solution)/shard_map/all_to_all | solution.py:116
  448.7 4.6 reshape.275
  453.4 9.6 %gather_fusion.4 = bf16[768,2048]{1,0:T(8,128)(2,1)} fusion(bf16[832,2048]{1,0:T(8,128)(2,1)} %reshape.275, s32[1024]{0:T(1024)S(1)} %pad_clamp_fusion), kind=kCustom, calls=%fused_computation.4 | custom fusion | bytes 6294528 | tf_op jit(solution)/shard_map/gather | solution.py:123
  462.9 6.3 %reshape.276 = bf16[128,6,2048]{2,1,0:T(8,128)(2,1)} reshape(bf16[768,2048]{1,0:T(8,128)(2,1)} %gather_fusion.4) | data formatting | bytes 6291456 | tf_op jit(solution)/shard_map/reshape | solution.py:123
  469.2 5.8 %reduce_sum.25 = bf16[128,2048]{1,0:T(8,128)(2,1)} reduce(bf16[128,6,2048]{2,1,0:T(8,128)(2,1)} %reshape.276, bf16[]{:T(256)} %constant.18.clone.1), dimensions={1}, to_apply=%region_5.6 | reduce | flops 1310720 | bytes 3670018 | tf_op jit(solution)/shard_map/reduce_sum | solution.py:126
  475.0 3.1 convert_element_type.128
  478.1 3.9 convert_element_type.129
  482.1 62.1 %reduce-scatter.8.cloned.1.call-done = f32[1,704,1024]{2,1,0:T(8,128)} async-done(((f32[1,704,2048]{2,1,0:T(8,128)}), f32[1,704,1024]{2,1,0:T(8,128)}) %reduce-scatter.8.cloned.1.call-update) | async-done | bytes 2883600 | tf_op jit(solution)/shard_map/reduce_scatter | solution.py:135
  544.1 3.1 convert_element_type.136
  (28 shorter events, 0.3 us)
Async XLA Ops:
  7.2 341.4 %copy-start = (bf16[1,2048,704]{1,2,0:T(8,128)(2,1)S(1)}, bf16[1,2048,704]{1,2,0:T(8,128)(2,1)}, u32[]{:S(2)}) copy-start(bf16[1,2048,704]{1,2,0:T(8,128)(2,1)} %param.15) | copy-start | bytes 8650756
  25.4 39.4 %all-to-all-start = ((bf16[16,1,52]{2,1,0:T(2,128)(2,1)}), bf16[16,1,52]{2,1,0:T(2,128)(2,1)S(1)}, u32[]{:S(2)}, u32[]{:S(2)}) async-start(bf16[16,1,52]{2,1,0:T(2,128)(2,1)} %all_to_all.28), calls=%async_computation | async-start | bytes 16384 | tf_op jit(solution)/shard_map/all_to_all | solution.py:94
  64.9 43.5 %copy-start.1 = (bf16[128,2048]{1,0:T(8,128)(2,1)S(1)}, bf16[128,2048]{1,0:T(8,128)(2,1)}, u32[]{:S(2)}) copy-start(bf16[128,2048]{1,0:T(8,128)(2,1)} %param.10) | copy-start | bytes 1572868
  102.8 37.3 %all-to-all-start.3 = ((bf16[16,52,704]{2,1,0:T(8,128)(2,1)}), bf16[16,52,704]{2,1,0:T(8,128)(2,1)}, u32[]{:S(2)}, u32[]{:S(2)}) async-start(bf16[16,52,704]{2,1,0:T(8,128)(2,1)} %get-tuple-element.11), calls=%async_computation.3 | async-start | bytes 2752512 | tf_op jit(solution)/shard_map/all_to_all | solution.py:80
  113.3 4.7 copy-start.2
  226.1 86.5 %all-to-all-start.5 = ((bf16[16,52,2048]{2,1,0:T(8,128)(2,1)}), bf16[16,52,2048]{2,1,0:T(8,128)(2,1)}, u32[]{:S(2)}, u32[]{:S(2)}) async-start(bf16[16,52,2048]{2,1,0:T(8,128)(2,1)} %get-tuple-element.8), calls=%async_computation.5 | async-start | bytes 7340032 | tf_op jit(solution)/shard_map/all_to_all | solution.py:66
  231.5 243.5 %reduce-scatter.4.cloned.1.call-start = ((), (), s32[]{:S(2)}) async-start(), calls=%async_computation.9 | async-start | bytes 8650752 | tf_op jit(solution)/shard_map/reduce_scatter | solution.py:133
  325.1 153.0 %reduce-scatter.6.cloned.1.call-start = ((), (), s32[]{:S(2)}) async-start(), calls=%async_computation.10 | async-start | bytes 8650752 | tf_op jit(solution)/shard_map/reduce_scatter | solution.py:134
  333.6 210.5 %reduce-scatter.8.cloned.1.call-start = ((), (), s32[]{:S(2)}) async-start(), calls=%async_computation.11 | async-start | bytes 8650752 | tf_op jit(solution)/shard_map/reduce_scatter | solution.py:135
  348.6 4.4 copy-start.3
  348.6 4.4 copy-start.4
  362.2 86.5 %all-to-all-start.4 = ((bf16[16,52,2048]{2,1,0:T(8,128)(2,1)}), bf16[16,52,2048]{2,1,0:T(8,128)(2,1)}, u32[]{:S(2)}, u32[]{:S(2)}) async-start(bf16[16,52,2048]{2,1,0:T(8,128)(2,1)} %reshape_transpose_reshape.2), calls=%async_computation.4 | async-start | bytes 7340032 | tf_op jit(solution)/shard_map/all_to_all | solution.py:116
Sparse Core Ops, SparseCore 0:
  325.2 71.3 reduce-scatter.3
  399.0 71.3 reduce-scatter.5
  472.7 71.3 reduce-scatter.7
where the time goes:
time: 565 us; the launch traced here: 554 us
  waiting for transfers between devices  205 us (36%)
  blocking collectives  124 us (22%)
  local copies, waits for them, and re-layouts  116 us (21%)
  matrix products  44 us (8%)
  other arithmetic  27.5 us (5%)
  starting transfers between devices  23 us (4%)
  between operations  14.4 us (3%)
    all_to_all x1, blocking collectives, per_device(): lax.all_to_all(send_grads.reshape(blk_count, per_peer, model_width), 'blk...  85.9 us
    all_to_all x1, waiting for transfers between devices, per_device(): lax.all_to_all(back_shaped.reshape(blk_count, per_peer, model_width), 'bl...  80.9 us
    reduce_scatter x1, waiting for transfers between devices, per_device(): lax.psum_scatter(term_down, 'grp', scatter_dimension=2, tiled=True)  62.1 us
    all_to_all x1, waiting for transfers between devices, per_device(): lax.all_to_all(send_inputs.reshape(blk_count, per_peer, model_width), 'bl...  54.8 us
    gather x9, local copies, waits for them, and re-layouts, pick(): taken = table[rows]  41.5 us
    all_to_all x1, blocking collectives, per_device(): lax.all_to_all(send_up_pre.reshape(blk_count, per_peer, ffw_width), 'blk'...  38 us
  transfers between devices with their start and end apart: 7, of which 4 were waited for; matrix products, arithmetic and copies ran while one was open for 28% of the time, Pallas kernels for 0%

commit v1 on v0

v1 whole, which is shorter than its diff:
```python
import functools

import jax
import jax.numpy as jnp
from jax import lax
from jax.experimental import pallas as pl
from jax.experimental.pallas import tpu as pltpu
from jax.sharding import PartitionSpec as P

BF16 = jnp.bfloat16
F32 = jnp.float32
VMEM_BYTES = 56 * 1024 * 1024
NT = (((1,), (1,)), ((), ()))
TN = (((0,), (0,)), ((), ()))


def params():
    return pltpu.CompilerParams(vmem_limit_bytes=VMEM_BYTES)


def cost(flops, moved):
    return pl.CostEstimate(flops=int(flops), bytes_accessed=int(moved), transcendentals=0)


def dot(a, b):
    return jnp.dot(a, b, preferred_element_type=F32)


def before_matrix(size):
    row = lax.broadcasted_iota(jnp.int32, (size, size), 0)
    col = lax.broadcasted_iota(jnp.int32, (size, size), 1)
    return jnp.where(row < col, 1.0, 0.0).astype(BF16)


def expert_hits(meta, top, expert):
    hits = jnp.where(meta[:top] == expert, 1.0, 0.0)
    return jnp.sum(hits, axis=0, keepdims=True), jnp.sum(hits * meta[top:], axis=0, keepdims=True)


def chip_slots(own, sib, core, before):
    rows = jnp.broadcast_to(own, (8, own.shape[1])), jnp.broadcast_to(sib, (8, sib.shape[1]))
    own_before = dot(rows[0].astype(BF16), before)[:1]
    sib_before = dot(rows[1].astype(BF16), before)[:1]
    own_total = jnp.sum(own, axis=1, keepdims=True)
    sib_total = jnp.sum(sib, axis=1, keepdims=True)
    core_f = core.astype(F32)
    own_slot = jnp.where(own > 0, own_before + core_f * sib_total, -1.0)
    sib_slot = jnp.where(sib > 0, sib_before + (1.0 - core_f) * own_total, -1.0)
    return own_slot, sib_slot


def slot_rows(slot, count):
    row = lax.broadcasted_iota(jnp.int32, (count, slot.shape[1]), 0).astype(F32)
    return jnp.where(row == slot, 1.0, 0.0)


def pack_kernel(zn, top, chip_rows, sc, meta_own, meta_sib, *refs):
    srcs, outs, (cat, sem) = refs[:4], refs[4 : 4 + 2 * zn], refs[4 + 2 * zn :]
    ffw, tok = srcs[0].shape[1:]
    copies = []
    for part in range(2):
        for core in range(2):
            for k in range(top):
                copies.append(
                    pltpu.make_async_copy(
                        srcs[2 * core + part].at[k],
                        cat.at[pl.ds(part * ffw, ffw), pl.ds((2 * k + core) * tok, tok)],
                        sem.at[len(copies)],
                    )
                )
    for copy in copies:
        copy.start()
    z, x, c = sc[0], sc[1], sc[2]
    q = lax.broadcasted_iota(jnp.int32, (2 * zn, 1), 0)
    plane = z + lax.shift_right_logical(q, 1)
    plane = jnp.where(plane >= zn, plane - zn, plane)
    experts = (plane * 4 + lax.bitwise_and(x + q, 1) * 2 + c).astype(F32)
    own = meta_own[...].astype(F32)
    sib = meta_sib[...].astype(F32)
    base = q.astype(F32) * chip_rows + 1.0
    before = before_matrix(tok)
    hits = [[jnp.where(m[k : k + 1] == experts, 1.0, 0.0) for k in range(top)] for m in (own, sib)]
    mask = [sum(h) for h in hits]
    total = [jnp.sum(m, axis=1, keepdims=True) for m in mask]
    core_f = c.astype(F32)
    slot = [dot(m.astype(BF16), before) for m in mask]
    slot = [slot[0] + core_f * total[1] + base, slot[1] + (1.0 - core_f) * total[0] + base]
    targets = []
    for k in range(top):
        for core in range(2):
            targets.append(jnp.sum(hits[core][k] * slot[core], axis=0, keepdims=True) - 1.0)
    target = jnp.concatenate(targets, axis=1)
    for copy in copies:
        copy.wait()
    table = cat[...]
    for j in range(zn):
        row = lax.broadcasted_iota(jnp.int32, (2 * chip_rows, target.shape[1]), 0) + 2 * j * chip_rows
        pick = jnp.where(row.astype(F32) == target, 1.0, 0.0).astype(BF16)
        packed = lax.dot_general(pick, table, NT, preferred_element_type=F32)
        outs[2 * j][...] = packed[:chip_rows].astype(BF16)
        outs[2 * j + 1][...] = packed[chip_rows:].astype(BF16)


def expert_kernel(
    zn, nb, top, chip_rows, j, sc, meta, d00, d01, d10, d11, pre0, pre1, w_gate, w_up, w_down,
    grads_out, hidden_out, rows_out, back0, back1,
):
    z, x, c, g = sc[0], sc[1], sc[2], sc[3]
    expert = (z * 4 + x * 2 + c).astype(F32)
    source = z - j + jnp.where(z < j, zn, 0)
    before = before_matrix(d00.shape[0])
    picked, weights = [], []
    for xr, (own_ref, sib_ref) in enumerate(((d00, d01), (d10, d11))):
        at = g * nb + source * 4 + lax.bitwise_and(x + xr, 1) * 2
        own, own_gate = expert_hits(meta[at + c].astype(F32), top, expert)
        sib, sib_gate = expert_hits(meta[at + 1 - c].astype(F32), top, expert)
        slot = jnp.concatenate(chip_slots(own, sib, c, before), axis=1)
        pick = slot_rows(slot, chip_rows)
        gates = jnp.concatenate([own_gate, sib_gate], axis=1)
        weights.append(jnp.sum(pick * gates, axis=1, keepdims=True))
        both = jnp.concatenate([own_ref[...], sib_ref[...]], axis=0)
        picked.append(dot(pick.astype(BF16), both))
    weight = jnp.concatenate(weights, axis=0)
    rows = jnp.concatenate(picked, axis=0).astype(BF16)
    rows_out[...] = rows
    ffw = w_down.shape[0]
    down = w_down[...]
    back = lax.dot_general(rows, jnp.concatenate([down, down], axis=0), NT, preferred_element_type=F32)
    pre = jnp.concatenate([pre0[...].astype(F32), pre1[...].astype(F32)], axis=0)
    swapped = pltpu.roll(pre, ffw, axis=1)
    first = lax.broadcasted_iota(jnp.int32, pre.shape, 1) < ffw
    gate_pre = jnp.where(first, pre, swapped)
    up_pre = jnp.where(first, swapped, pre)
    sig = jax.nn.sigmoid(gate_pre)
    active = gate_pre * sig
    slope = jnp.where(first, up_pre * sig * (1.0 + gate_pre * (1.0 - sig)), active)
    grads = (weight * back * slope).astype(BF16)
    grads_out[...] = grads
    hidden_out[...] = (weight * active * up_pre)[:, :ffw].astype(BF16)
    route = dot(grads, jnp.concatenate([w_gate[...], w_up[...]], axis=0))
    back0[...] = route[:chip_rows].astype(BF16)
    back1[...] = route[chip_rows:].astype(BF16)


def combine_kernel(zn, nb, top, chip_rows, j, sc, meta, r00, r01, r10, r11, out):
    z, x, c, g = sc[0], sc[1], sc[2], sc[3]
    source = z - j + jnp.where(z < j, zn, 0)
    at = g * nb + source * 4 + x * 2
    own_meta = meta[at + c].astype(F32)
    sib_meta = meta[at + 1 - c].astype(F32)
    before = before_matrix(out.shape[0])
    total = jnp.zeros(out.shape, F32)
    for n, ref in enumerate((r00, r01, r10, r11)):
        xr, cr = n // 2, n % 2
        expert = z * 4 + lax.bitwise_and(x + xr, 1) * 2 + lax.bitwise_and(c + cr, 1)
        own, _ = expert_hits(own_meta, top, expert.astype(F32))
        sib, _ = expert_hits(sib_meta, top, expert.astype(F32))
        slot, _ = chip_slots(own, sib, c, before)
        pick = slot_rows(slot, chip_rows).astype(BF16)
        total = total + lax.dot_general(pick, ref[...], TN, preferred_element_type=F32)
    out[...] = total.astype(BF16)


def inner_kernel(zn, nb, ng, top, chip_rows, sc, meta, *refs):
    n_x, n_g = 4 * zn, zn * ng
    xs, gs = refs[:n_x], refs[n_x : n_x + n_g]
    gate_out, up_out, table, grads, grads_t, rows, sem_x, sem_g = refs[n_x + n_g :]
    tok = xs[0].shape[0] // ng
    ffw, width = gate_out.shape
    quad = 2 * chip_rows
    copies = []
    for j in range(zn):
        for n in range(4):
            for r in range(ng):
                copies.append(
                    pltpu.make_async_copy(
                        xs[4 * j + n].at[pl.ds(r * tok, tok)],
                        table.at[j * ng + r, n // 2, pl.ds((n % 2) * tok, tok)],
                        sem_x.at[len(copies)],
                    )
                )
    for u in range(n_g):
        copies.append(pltpu.make_async_copy(gs[u], grads.at[pl.ds(u * quad, quad)], sem_g.at[u]))
    for copy in copies:
        copy.start()
    z, x, c, g = sc[0], sc[1], sc[2], sc[3]
    expert = (z * 4 + x * 2 + c).astype(F32)
    before = before_matrix(tok)
    for copy in copies:
        copy.wait()

    def pick_rows(u, carry):
        j, r = u // ng, u % ng
        source = lax.rem(z - j + zn, zn)
        group = lax.rem(g - r + ng, ng)
        picked = []
        for xr in range(2):
            at = group * nb + source * 4 + lax.bitwise_and(x + xr, 1) * 2
            own, _ = expert_hits(meta[at + c].astype(F32), top, expert)
            sib, _ = expert_hits(meta[at + 1 - c].astype(F32), top, expert)
            slot = jnp.concatenate(chip_slots(own, sib, c, before), axis=1)
            picked.append(dot(slot_rows(slot, chip_rows).astype(BF16), table[u, xr]))
        rows[pl.ds(pl.multiple_of(u * quad, 16), quad), :] = jnp.concatenate(picked, axis=0).astype(BF16)
        return carry

    lax.fori_loop(0, n_g, pick_rows, 0)
    total = n_g * quad
    step = 128
    for i in range(0, total, step):
        grads_t[:, i : i + step] = grads[i : i + step, :].T
    chunk = min(256, width)

    def product(n, carry):
        cols = pl.ds(pl.multiple_of(n * chunk, chunk), chunk)
        both = dot(grads_t[...], rows[:, cols])
        gate_out[:, cols] = both[:ffw].astype(BF16)
        up_out[:, cols] = both[ffw:].astype(BF16)
        return carry

    lax.fori_loop(0, width // chunk, product, 0)


def outer_kernel(zn, ng, sc, *refs):
    hs, ds = refs[:zn], refs[zn : 2 * zn]
    own, sent, hidden, rows, sem = refs[2 * zn :]
    quad = hs[0].shape[0]
    copies = []
    for j in range(zn):
        copies.append(pltpu.make_async_copy(hs[j], hidden.at[pl.ds(j * quad, quad)], sem.at[2 * j]))
        copies.append(pltpu.make_async_copy(ds[j], rows.at[pl.ds(j * quad, quad)], sem.at[2 * j + 1]))
    for copy in copies:
        copy.start()
    for copy in copies:
        copy.wait()
    g = sc[3]
    width = own.shape[1]
    chunk = min(256, width)
    hidden_t = hidden[...].T

    for r in range(ng):
        base = lax.rem(g + r, ng) * width

        def product(n, carry):
            cols = pl.ds(pl.multiple_of(base + n * chunk, chunk), chunk)
            value = dot(hidden_t, rows[:, cols])
            to = pl.ds(pl.multiple_of(n * chunk, chunk), chunk)
            if r == 0:
                own[:, to] = value
            else:
                sent[r - 1, :, to] = value.astype(BF16)
            return carry

        lax.fori_loop(0, width // chunk, product, 0)


def per_device(
    tokens, d_out, expert_ids, gate_values, saved_gate_pre, saved_up_pre, w_gate, w_up, w_down
):
    tok, width = tokens.shape
    top = expert_ids.shape[1]
    ffw = saved_gate_pre.shape[2]
    nb, ng = lax.axis_size("blk"), lax.axis_size("grp")
    zn = nb // 4
    experts = w_gate.shape[0] * nb
    slots = 13 * tok // (2 * experts)
    chip_rows = -(-2 * slots // 8) * 8
    quad = 2 * chip_rows
    part = width // ng
    me, g = lax.axis_index("blk"), lax.axis_index("grp")
    z, x, c = me // 4, (me // 2) % 2, me % 2
    sc = jnp.stack([z, x, c, g]).astype(jnp.int32)

    def shift(value, n):
        return lax.ppermute(value, "blk", [(b, (b + 4 * n) % nb) for b in range(nb)])

    def over_x(value):
        return lax.ppermute(value, "blk", [(b, b ^ 2) for b in range(nb)])

    def over_core(value):
        return lax.ppermute(value, "blk", [(b, b ^ 1) for b in range(nb)])

    def over_groups(value, n):
        return lax.ppermute(value, "grp", [(b, (b + n) % ng) for b in range(ng)])

    def gathered(block):
        out = []
        for j in range(zn):
            if j:
                block = shift(block, 1)
            hop = over_x(block)
            out.append((block, over_core(block), hop, over_core(hop)))
        return out

    smem = pl.BlockSpec(memory_space=pltpu.SMEM)
    vmem = pl.BlockSpec(memory_space=pltpu.VMEM)
    anywhere = pl.BlockSpec(memory_space=pl.ANY)

    def shape(*dims, dtype=BF16):
        return jax.ShapeDtypeStruct(dims, dtype)

    meta = jnp.concatenate([expert_ids.T.astype(BF16), gate_values.T], axis=0)
    meta_all = lax.all_gather(meta, ("grp", "blk"))
    meta_sib = over_core(meta)
    pre = [saved_gate_pre.transpose(1, 2, 0), saved_up_pre.transpose(1, 2, 0)]
    pre_sib = [over_core(p) for p in pre]
    grads_in = gathered(d_out)

    packed = pl.pallas_call(
        functools.partial(pack_kernel, zn, top, chip_rows),
        out_shape=[shape(chip_rows, 2 * ffw)] * (2 * zn),
        in_specs=[smem, vmem, vmem] + [anywhere] * 4,
        out_specs=[vmem] * (2 * zn),
        scratch_shapes=[
            pltpu.VMEM((2 * ffw, 2 * top * tok), BF16),
            pltpu.SemaphoreType.DMA((4 * top,)),
        ],
        compiler_params=params(),
        cost_estimate=cost(2 * zn * quad * 2 * top * tok * 2 * ffw, 8 * top * tok * ffw * 2),
        name="pack",
    )(sc, meta, meta_sib, *pre, *pre_sib)
    arrived = []
    for j in range(zn):
        near, far = packed[2 * j], over_x(packed[2 * j + 1])
        arrived.append((shift(near, j), shift(far, j)) if j else (near, far))

    weights = (w_gate[0].T, w_up[0].T, w_down[0])
    done = []
    for j in range(zn):
        done.append(
            pl.pallas_call(
                functools.partial(expert_kernel, zn, nb, top, chip_rows, j),
                out_shape=[
                    shape(quad, 2 * ffw),
                    shape(quad, ffw),
                    shape(quad, width),
                    shape(chip_rows, width),
                    shape(chip_rows, width),
                ],
                in_specs=[smem] + [vmem] * 10,
                out_specs=[vmem] * 5,
                compiler_params=params(),
                cost_estimate=cost(2 * quad * width * ffw * 4 + 2 * quad * tok * 2 * width, 16e6),
                name="expert",
            )(sc, meta_all, *grads_in[j], *arrived[j], *weights)
        )

    partials = []
    for j in range(zn):
        near, far = done[j][3], over_x(done[j][4])
        partials.append(
            pl.pallas_call(
                functools.partial(combine_kernel, zn, nb, top, chip_rows, j),
                out_shape=shape(tok, width),
                in_specs=[smem] + [vmem] * 5,
                out_specs=vmem,
                compiler_params=params(),
                cost_estimate=cost(2 * 4 * tok * chip_rows * width, 3e6),
                name="combine",
            )(sc, meta_all, near, over_core(near), far, over_core(far))
        )
    d_tokens = partials[0].astype(F32)
    for j in range(1, zn):
        d_tokens = d_tokens + shift(partials[j], -j).astype(F32)

    down_own, down_sent = pl.pallas_call(
        functools.partial(outer_kernel, zn, ng),
        out_shape=[shape(ffw, part, dtype=F32), shape(max(ng - 1, 1), ffw, part)],
        in_specs=[smem] + [anywhere] * (2 * zn),
        out_specs=[vmem, vmem],
        scratch_shapes=[
            pltpu.VMEM((zn * quad, ffw), BF16),
            pltpu.VMEM((zn * quad, width), BF16),
            pltpu.SemaphoreType.DMA((2 * zn,)),
        ],
        compiler_params=params(),
        cost_estimate=cost(2 * zn * quad * ffw * width, 10e6),
        name="outer",
    )(sc, *[d[1] for d in done], *[d[2] for d in done])
    d_down = down_own
    for r in range(1, ng):
        d_down = d_down + over_groups(down_sent[r - 1], r).astype(F32)

    own_part = lax.dynamic_slice(tokens, (0, g * part), (tok, part))
    pieces = [own_part]
    for r in range(1, ng):
        there = lax.dynamic_slice(tokens, (0, ((g + r) % ng) * part), (tok, part))
        pieces.append(over_groups(there, r))
    inputs = gathered(jnp.concatenate(pieces, axis=0))
    grads = []
    for j in range(zn):
        grads.append(done[j][0])
        for r in range(1, ng):
            grads.append(over_groups(done[j][0], r))
    units = zn * ng
    d_gate, d_up = pl.pallas_call(
        functools.partial(inner_kernel, zn, nb, ng, top, chip_rows),
        out_shape=[shape(ffw, part)] * 2,
        in_specs=[smem, vmem] + [anywhere] * (4 * zn + units),
        out_specs=[vmem, vmem],
        scratch_shapes=[
            pltpu.VMEM((units, 2, 2 * tok, part), BF16),
            pltpu.VMEM((units * quad, 2 * ffw), BF16),
            pltpu.VMEM((2 * ffw, units * quad), BF16),
            pltpu.VMEM((units * quad, part), BF16),
            pltpu.SemaphoreType.DMA((4 * units,)),
            pltpu.SemaphoreType.DMA((units,)),
        ],
        compiler_params=params(),
        cost_estimate=cost(2 * units * quad * 2 * ffw * part, 20e6),
        name="inner",
    )(sc, meta_all, *[block for plane in inputs for block in plane], *grads)
    return (
        d_tokens.astype(BF16),
        d_gate.T[None],
        d_up.T[None],
        d_down.astype(BF16)[None],
    )


def solution(mesh):
    return jax.shard_map(
        per_device,
        mesh=mesh,
        in_specs=(
            P(("grp", "blk"), None),
            P(("grp", "blk"), None),
            P(("grp", "blk"), None),
            P(("grp", "blk"), None),
            P(("grp", "blk"), None, None),
            P(("grp", "blk"), None, None),
            P("blk", None, None),
            P("blk", None, None),
            P("blk", None, None),
        ),
        out_specs=(
            P(("grp", "blk"), None),
            P("blk", "grp", None),
            P("blk", "grp", None),
            P("blk", None, "grp"),
        ),
        check_vma=False,
    )
```

time: 565 us -> 317 us (0.56)
  the two profiles are of different devices: /device:TPU:10 before, /device:TPU:0 now
where the time goes in v1:
time: 317 us; the launch traced here: 316 us
  waiting for transfers between devices  126 us (40%)
  Pallas kernels  89.7 us (28%)
  blocking collectives  48.4 us (15%)
  starting transfers between devices  44.5 us (14%)
  other arithmetic  4.77 us (2%)
    ppermute x15, waiting for transfers between devices, shift(): lax.ppermute(value, 'blk', [(b, (b + 4 * n) % nb) for b in range(nb)])  80.8 us
    all_gather x1, blocking collectives, per_device(): meta_all = lax.all_gather(meta, ('grp', 'blk'))  48.4 us
    ppermute x16, waiting for transfers between devices, over_x(): return lax.ppermute(value, 'blk', [(b, b ^ 2) for b in range(nb)])  39.9 us
    pallas_call x4, Pallas kernels, per_device(): pl.pallas_call(functools.partial(expert_kernel, zn, nb, top, chip_rows, j...  37.8 us
    pallas_call x1, Pallas kernels, per_device(): pl.pallas_call(functools.partial(inner_kernel, zn, nb, ng, top, chip_rows...  19 us
    ppermute x16, starting transfers between devices, over_x(): return lax.ppermute(value, 'blk', [(b, b ^ 2) for b in range(nb)])  16.9 us
    ppermute x15, starting transfers between devices, shift(): lax.ppermute(value, 'blk', [(b, (b + 4 * n) % nb) for b in range(nb)])  16.4 us
    pallas_call x4, Pallas kernels, per_device(): pl.pallas_call(functools.partial(combine_kernel, zn, nb, top, chip_rows,...  14 us
  transfers between devices with their start and end apart: 64, of which 17 were waited for; matrix products, arithmetic and copies ran while one was open for 1% of the time, Pallas kernels for 28%

profile of v1, /device:TPU:0, one launch (start us, length us, event | category | flops | bytes accessed | tf_op | source)
XLA Modules:
  0.0 316.3 jit_solution(12246770914508309286)
XLA Ops:
  0.6 3.1 collective-permute-start.10
  3.7 1.5 collective-permute-start.1
  5.2 1.1 constant_dynamic-slice_fusion.1
  6.3 1.6 collective-permute-start.43
  7.9 0.7 convert_bitcast_fusion
  8.5 0.7 pad_maximum_fusion.1
  9.5 5.5 %collective-permute-done.43 = bf16[128,1024]{1,0:T(8,128)(2,1)S(1)} collective-permute-done((bf16[128,1024]{1,0:T(8,128)(2,1)S(1)}, bf16[128,1024]{1,0:T(8,128)(2,1)S(1)}, u32[]{:S(2)}, u32[]{:S(2)}) %collective-permute-start.43) | collective-permute-done | bytes 262176 | tf_op jit(solution)/shard_map/ppermute | solution.py:283
  15.1 1.6 collective-permute-start.47
  16.7 0.5 collective-permute-start.45
  17.3 0.6 collective-permute-done.10.d00
  18.5 12.1 %collective-permute-done.47.refs_4_ = bf16[256,1024]{1,0:T(8,128)(2,1)} collective-permute-done((bf16[256,1024]{1,0:T(8,128)(2,1)S(1)}, bf16[256,1024]{1,0:T(8,128)(2,1)}, u32[]{:S(2)}, u32[]{:S(2)}) %collective-permute-start.47) | collective-permute-done | bytes 524320 | tf_op jit(solution)/shard_map/ppermute | solution.py:274
  30.6 0.5 collective-permute-start.12
  31.2 13.9 %collective-permute-done.21.d00 = bf16[128,2048]{1,0:T(8,128)(2,1)S(1)} collective-permute-done((bf16[128,2048]{1,0:T(8,128)(2,1)S(1)}, bf16[128,2048]{1,0:T(8,128)(2,1)S(1)}, u32[]{:S(2)}, u32[]{:S(2)}) %collective-permute-start.21) | collective-permute-done | bytes 524320 | tf_op jit(solution)/shard_map/ppermute | solution.py:274
  45.2 0.6 collective-permute-start.49
  45.8 0.6 pad_add_fusion.sc
  46.9 9.4 %pack.1 = (bf16[104,1408]{1,0:T(8,128)(2,1)}, bf16[104,1408]{1,0:T(8,128)(2,1)}, bf16[104,1408]{1,0:T(8,128)(2,1)}, bf16[104,1408]{1,0:T(8,128)(2,1)}, bf16[104,...) custom-call(s32[4]{0:T(128)} %pad_add_fusion.sc, ...), custom_call_target="tpu_custom_call" | custom-call | flops 3598712832 | bytes 8650752 | tf_op jit(solution)/shard_map/pack/pallas_call | solution.py:308
  56.4 1.6 collective-permute-start.26
  58.0 3.5 %collective-permute-done.51.refs_8_ = bf16[256,1024]{1,0:T(8,128)(2,1)} collective-permute-done((bf16[256,1024]{1,0:T(8,128)(2,1)}, bf16[256,1024]{1,0:T(8,128)(2,1)}, u32[]{:S(2)}, u32[]{:S(2)}) %collective-permute-start.51) | collective-permute-done | bytes 524320 | tf_op jit(solution)/shard_map/ppermute | solution.py:274
  61.5 0.5 collective-permute-start.15
  62.1 0.8 collective-permute-start.14
  62.9 1.5 collective-permute-start.6
  64.4 2.1 collective-permute-done.26
  66.5 1.5 collective-permute-start.23
  68.0 13.8 %collective-permute-done.25.pre0 = bf16[104,1408]{1,0:T(8,128)(2,1)S(1)} collective-permute-done((bf16[104,1408]{1,0:T(8,128)(2,1)}, bf16[104,1408]{1,0:T(8,128)(2,1)S(1)}, u32[]{:S(2)}, u32[]{:S(2)}) %collective-permute-start.25) | collective-permute-done | bytes 292896 | tf_op jit(solution)/shard_map/ppermute | solution.py:274
  81.9 0.6 collective-permute-start.37
  82.7 13.3 %collective-permute-done.37 = bf16[104,1408]{1,0:T(8,128)(2,1)S(1)} collective-permute-done((bf16[104,1408]{1,0:T(8,128)(2,1)}, bf16[104,1408]{1,0:T(8,128)(2,1)S(1)}, u32[]{:S(2)}, u32[]{:S(2)}) %collective-permute-start.37) | collective-permute-done | bytes 292896 | tf_op jit(solution)/shard_map/ppermute | solution.py:277
  96.6 48.4 %all-gather.1.meta = bf16[32,12,128]{2,1,0:T(8,128)(2,1)} all-gather(bf16[1,12,128]{2,1,0:T(8,128)(2,1)S(1)} %get-tuple-element.71), channel_id=2, replica_groups=mesh['grp'=2,'blk'=16] {'grp','blk'}, dimensions={0}, use_global_device_ids=true | all-gather | bytes 101376 | tf_op jit(solution)/shard_map/all_gather | solution.py:302
  145.2 3.8 %collective-permute-start.38 = (bf16[104,1408]{1,0:T(8,128)(2,1)S(1)}, bf16[104,1408]{1,0:T(8,128)(2,1)S(1)}, u32[]{:S(2)}, u32[]{:S(2)}) collective-permute-start(bf16[104,1408]{1,0:T(8,128)(2,1)S(1)} %collective-permute-done.37), channel_id=1, source_target_pairs={{0,12},{1,13},{2,14},{3,15},{4,0},{5,1},{6,2},{7,3},{8,4},{9,5},{1... | collective-permute-start | bytes 878600 | tf_op jit(solution)/shard_map/ppermute | solution.py:274
  149.0 9.4 %expert.4 = (bf16[208,1408]{1,0:T(8,128)(2,1)}, bf16[208,704]{1,0:T(8,128)(2,1)}, bf16[208,2048]{1,0:T(8,128)(2,1)}, bf16[104,2048]{1,0:T(8,128)(2,1)}, bf16[104,2048]{1,0:T(8,128)(2,1)}) custom-call(s32[4]{0:T(128)} %pad_add_fusion.sc, bf16[32,12,128]{2,1,0:T(8,128)(2,1)} %all-gather.1.meta, bf16[128,2048]{1,0:T(8,128)(2,1)} %d00.1, ...), custom_call_target="tpu_custom_call" | custom-call | flops 2617245696 | bytes 16000000 | tf_op jit(solution)/shard_map/expert/pallas_call | solution.py:330
  158.5 1.3 collective-permute-start.8
  159.7 5.4 %collective-permute-done.27.pre1 = bf16[104,1408]{1,0:T(8,128)(2,1)S(1)} collective-permute-done((bf16[104,1408]{1,0:T(8,128)(2,1)S(1)}, bf16[104,1408]{1,0:T(8,128)(2,1)S(1)}, u32[]{:S(2)}, u32[]{:S(2)}) %collective-permute-start.27) | collective-permute-done | bytes 292896 | tf_op jit(solution)/shard_map/ppermute | solution.py:274
  165.2 1.3 collective-permute-start.53
  166.4 1.6 collective-permute-done.38.pre1
  168.0 3.4 %collective-permute-done.8.r10 = bf16[104,2048]{1,0:T(8,128)(2,1)S(1)} collective-permute-done((bf16[104,2048]{1,0:T(8,128)(2,1)}, bf16[104,2048]{1,0:T(8,128)(2,1)S(1)}, u32[]{:S(2)}, u32[]{:S(2)}) %collective-permute-start.8) | collective-permute-done | bytes 426016 | tf_op jit(solution)/shard_map/ppermute | solution.py:277
  171.4 1.5 collective-permute-start.59
  173.0 8.1 %collective-permute-done.55.refs_12_ = bf16[256,1024]{1,0:T(8,128)(2,1)S(1)} collective-permute-done((bf16[256,1024]{1,0:T(8,128)(2,1)}, bf16[256,1024]{1,0:T(8,128)(2,1)S(1)}, u32[]{:S(2)}, u32[]{:S(2)}) %collective-permute-start.55) | collective-permute-done | bytes 524320 | tf_op jit(solution)/shard_map/ppermute | solution.py:274
  181.1 1.2 collective-permute-start.34
  182.8 9.5 %expert.5 = (bf16[208,1408]{1,0:T(8,128)(2,1)}, bf16[208,704]{1,0:T(8,128)(2,1)}, bf16[208,2048]{1,0:T(8,128)(2,1)}, bf16[104,2048]{1,0:T(8,128)(2,1)}, bf16[104,2048]{1,0:T(8,128)(2,1)}) custom-call(s32[4]{0:T(128)} %pad_add_fusion.sc, bf16[32,12,128]{2,1,0:T(8,128)(2,1)} %all-gather.1.meta, bf16[128,2048]{1,0:T(8,128)(2,1)} %copy-done.2, ...), custom_call_target="tpu_custom_call" | custom-call | flops 2617245696 | bytes 16000000 | tf_op jit(solution)/shard_map/expert/pallas_call | solution.py:330
  192.3 0.9 collective-permute-start.18
  193.2 0.8 collective-permute-done.34.d10
  194.0 10.4 %collective-permute-done.18.r10 = bf16[104,2048]{1,0:T(8,128)(2,1)S(1)} collective-permute-done((bf16[104,2048]{1,0:T(8,128)(2,1)}, bf16[104,2048]{1,0:T(8,128)(2,1)S(1)}, u32[]{:S(2)}, u32[]{:S(2)}) %collective-permute-start.18) | collective-permute-done | bytes 426016 | tf_op jit(solution)/shard_map/ppermute | solution.py:277
  204.4 1.2 collective-permute-start.60
  205.7 1.2 collective-permute-start.57
  207.2 9.5 %expert.6 = (bf16[208,1408]{1,0:T(8,128)(2,1)}, bf16[208,704]{1,0:T(8,128)(2,1)}, bf16[208,2048]{1,0:T(8,128)(2,1)}, bf16[104,2048]{1,0:T(8,128)(2,1)}, bf16[104,2048]{1,0:T(8,128)(2,1)}) custom-call(s32[4]{0:T(128)} %pad_add_fusion.sc, bf16[32,12,128]{2,1,0:T(8,128)(2,1)} %all-gather.1.meta, bf16[128,2048]{1,0:T(8,128)(2,1)} %copy-done.3, ...), custom_call_target="tpu_custom_call" | custom-call | flops 2617245696 | bytes 16000000 | tf_op jit(solution)/shard_map/expert/pallas_call | solution.py:330
  216.7 0.9 collective-permute-start.29
  217.6 9.4 %expert.7 = (bf16[208,1408]{1,0:T(8,128)(2,1)}, bf16[208,704]{1,0:T(8,128)(2,1)}, bf16[208,2048]{1,0:T(8,128)(2,1)}, bf16[104,2048]{1,0:T(8,128)(2,1)}, bf16[104,2048]{1,0:T(8,128)(2,1)}) custom-call(s32[4]{0:T(128)} %pad_add_fusion.sc, bf16[32,12,128]{2,1,0:T(8,128)(2,1)} %all-gather.1.meta, bf16[128,2048]{1,0:T(8,128)(2,1)} %copy-done.10, ...), custom_call_target="tpu_custom_call" | custom-call | flops 2617245696 | bytes 16000000 | tf_op jit(solution)/shard_map/expert/pallas_call | solution.py:330
  227.1 1.2 collective-permute-start.40
  229.7 9.6 %collective-permute-done.40.r10 = bf16[104,2048]{1,0:T(8,128)(2,1)S(1)} collective-permute-done((bf16[104,2048]{1,0:T(8,128)(2,1)}, bf16[104,2048]{1,0:T(8,128)(2,1)S(1)}, u32[]{:S(2)}, u32[]{:S(2)}) %collective-permute-start.40) | collective-permute-done | bytes 426016 | tf_op jit(solution)/shard_map/ppermute | solution.py:277
  239.3 0.6 collective-permute-start.56
  239.9 0.8 collective-permute-start.61
  240.7 1.4 collective-permute-start.62
  242.1 9.4 %outer.1 = (f32[704,1024]{1,0:T(8,128)}, bf16[1,704,1024]{2,1,0:T(8,128)(2,1)}) custom-call(s32[4]{0:T(128)} %pad_add_fusion.sc, bf16[208,704]{1,0:T(8,128)(2,1)} %get-tuple-element.58.refs_0_, bf16[208,704]{1,0:T(8,128)(2,1)} %get-tuple-element.59.refs_1_, bf16[208,704]{1,0:T(8,128)(2,1)} %get-tuple-element.60.refs_2_, ...), custom_call_target="tpu_custom_call" | custom-call | flops 2399141888 | bytes 10000000 | tf_op jit(solution)/shard_map/outer/pallas_call | solution.py:365
  251.5 0.8 collective-permute-start.63
  252.3 3.5 %combine.5 = bf16[128,2048]{1,0:T(8,128)(2,1)} custom-call(s32[4]{0:T(128)} %pad_add_fusion.sc, bf16[32,12,128]{2,1,0:T(8,128)(2,1)} %all-gather.1.meta, bf16[104,2048]{1,0:T(8,128)(2,1)} %get-tuple-element.42.r00, bf16[104,2048]{1,0:T(8,128)(2,1)} %copy-done.23, bf16[104,2048]{1,0:T(8,128)(2,1)} %copy-done.22, bf16[104,2048]{1,0:T(8,128)(2,1)} %copy-done.27), custom_call_target="tpu_custom_call" | custom-call | flops 218103808 | bytes 3000000 | tf_op jit(solution)/shard_map/combine/pallas_call | solution.py:351
  255.8 3.5 %combine.6 = bf16[128,2048]{1,0:T(8,128)(2,1)} custom-call(s32[4]{0:T(128)} %pad_add_fusion.sc, bf16[32,12,128]{2,1,0:T(8,128)(2,1)} %all-gather.1.meta, bf16[104,2048]{1,0:T(8,128)(2,1)} %get-tuple-element.46.r00, bf16[104,2048]{1,0:T(8,128)(2,1)} %copy-done.28, bf16[104,2048]{1,0:T(8,128)(2,1)} %copy-done.25, bf16[104,2048]{1,0:T(8,128)(2,1)} %copy-done.29), custom_call_target="tpu_custom_call" | custom-call | flops 218103808 | bytes 3000000 | tf_op jit(solution)/shard_map/combine/pallas_call | solution.py:351
  259.3 3.6 %combine.7 = bf16[128,2048]{1,0:T(8,128)(2,1)} custom-call(s32[4]{0:T(128)} %pad_add_fusion.sc, bf16[32,12,128]{2,1,0:T(8,128)(2,1)} %all-gather.1.meta, bf16[104,2048]{1,0:T(8,128)(2,1)} %get-tuple-element.50.r00, bf16[104,2048]{1,0:T(8,128)(2,1)} %copy-done.30, bf16[104,2048]{1,0:T(8,128)(2,1)} %copy-done.26, bf16[104,2048]{1,0:T(8,128)(2,1)} %copy-done.31), custom_call_target="tpu_custom_call" | custom-call | flops 218103808 | bytes 3000000 | tf_op jit(solution)/shard_map/combine/pallas_call | solution.py:351
  262.9 0.7 collective-permute-start.20
  263.5 4.7 %collective-permute-start.31 = (bf16[128,2048]{1,0:T(8,128)(2,1)S(1)}, bf16[128,2048]{1,0:T(8,128)(2,1)S(1)}, u32[]{:S(2)}, u32[]{:S(2)}) collective-permute-start(bf16[128,2048]{1,0:T(8,128)(2,1)S(1)} %copy-done.16), channel_id=1, source_target_pairs={{0,8},{1,9},{2,10},{3,11},{4,12},{5,13},{6,14},{7,15},{8,0},{9,1},... | collective-permute-start | bytes 1572872 | tf_op jit(solution)/shard_map/ppermute | solution.py:274
  268.3 1.0 collective-permute-start.42
  269.3 3.5 %combine.4 = bf16[128,2048]{1,0:T(8,128)(2,1)} custom-call(s32[4]{0:T(128)} %pad_add_fusion.sc, bf16[32,12,128]{2,1,0:T(8,128)(2,1)} %all-gather.1.meta, bf16[104,2048]{1,0:T(8,128)(2,1)} %get-tuple-element.38.r00, bf16[104,2048]{1,0:T(8,128)(2,1)} %copy-done.20, bf16[104,2048]{1,0:T(8,128)(2,1)} %copy-done.19, bf16[104,2048]{1,0:T(8,128)(2,1)} %copy-done.21), custom_call_target="tpu_custom_call" | custom-call | flops 218103808 | bytes 3000000 | tf_op jit(solution)/shard_map/combine/pallas_call | solution.py:351
  272.8 19.0 %inner.1 = (bf16[704,1024]{1,0:T(8,128)(2,1)}, bf16[704,1024]{1,0:T(8,128)(2,1)}) custom-call(s32[4]{0:T(128)} %pad_add_fusion.sc, bf16[32,12,128]{2,1,0:T(8,128)(2,1)} %all-gather.1.meta, bf16[256,1024]{1,0:T(8,128)(2,1)} %copy-done.18, bf16[256,1024]{1,0:T(8,128)(2,1)} %copy-done.44, bf16[256,1024]{1,0:T(8,128)(2,1)} %collective-permute-done.45.refs_2_, ...), custom_call_target="tpu_custom_call" | custom-call | flops 4798283776 | bytes 20000000 | tf_op jit(solution)/shard_map/inner/pallas_call | solution.py:395
  291.9 21.7 %collective-permute-done.31 = bf16[128,2048]{1,0:T(8,128)(2,1)S(1)} collective-permute-done((bf16[128,2048]{1,0:T(8,128)(2,1)S(1)}, bf16[128,2048]{1,0:T(8,128)(2,1)S(1)}, u32[]{:S(2)}, u32[]{:S(2)}) %collective-permute-start.31) | collective-permute-done | bytes 524320 | tf_op jit(solution)/shard_map/ppermute | solution.py:274
  313.6 1.1 add_convert_fusion.1
  314.7 1.6 fusion
  (191 shorter events, 4.8 us)
Async XLA Ops:
  0.6 17.2 %collective-permute-start.10 = (bf16[128,2048]{1,0:T(8,128)(2,1)}, bf16[128,2048]{1,0:T(8,128)(2,1)S(1)}, u32[]{:S(2)}, u32[]{:S(2)}) collective-permute-start(bf16[128,2048]{1,0:T(8,128)(2,1)} %d00.1), channel_id=1, source_target_pairs={{0,4},{1,5},{2,6},{3,7},{4,8},{5,9},{6,10},{7,11},{8,12},{9,13},{1... | collective-permute-start | bytes 1572872 | tf_op jit(solution)/shard_map/ppermute | solution.py:274
  3.7 14.2 %collective-permute-start.1 = (bf16[128,2048]{1,0:T(8,128)(2,1)}, bf16[128,2048]{1,0:T(8,128)(2,1)S(1)}, u32[]{:S(2)}, u32[]{:S(2)}) collective-permute-start(bf16[128,2048]{1,0:T(8,128)(2,1)} %d00.1), channel_id=1, source_target_pairs={{0,2},{1,3},{2,0},{3,1},{4,6},{5,7},{6,4},{7,5},{8,10},{9,11},{10,... | collective-permute-start | bytes 1572872 | tf_op jit(solution)/shard_map/ppermute | solution.py:277
  5.2 13.2 %collective-permute-start = (bf16[128,2048]{1,0:T(8,128)(2,1)}, bf16[128,2048]{1,0:T(8,128)(2,1)S(1)}, u32[]{:S(2)}, u32[]{:S(2)}) collective-permute-start(bf16[128,2048]{1,0:T(8,128)(2,1)} %d00.1), channel_id=1, source_target_pairs={{0,1},{1,0},{2,3},{3,2},{4,5},{5,4},{6,7},{7,6},{8,9},{9,8},{10,11... | collective-permute-start | bytes 1572872 | tf_op jit(solution)/shard_map/ppermute | solution.py:280
  6.3 8.8 %collective-permute-start.43 = (bf16[128,1024]{1,0:T(8,128)(2,1)S(1)}, bf16[128,1024]{1,0:T(8,128)(2,1)S(1)}, u32[]{:S(2)}, u32[]{:S(2)}) collective-permute-start(bf16[128,1024]{1,0:T(8,128)(2,1)S(1)} %get-tuple-element.69), channel_id=1, source_target_pairs={{0,16},{16,0},{1,17},{17,1},{2,18},{18,2},{3,19},{19,3},{4,20},{20... | collective-permute-start | bytes 786440 | tf_op jit(solution)/shard_map/ppermute | solution.py:283
  9.2 7.5 %collective-permute-start.3 = (bf16[12,128]{1,0:T(8,128)(2,1)S(1)}, bf16[12,128]{1,0:T(8,128)(2,1)S(1)}, u32[]{:S(2)}, u32[]{:S(2)}) collective-permute-start(bf16[12,128]{1,0:T(8,128)(2,1)S(1)} %get-tuple-element.70.meta_own), channel_id=1, source_target_pairs={{0,1},{1,0},{2,3},{3,2},{4,5},{5,4},{6,7},{7,6},{8,9},{9,8},{10,11... | collective-permute-start | bytes 9224 | tf_op jit(solution)/shard_map/ppermute | solution.py:280
  15.1 15.5 %collective-permute-start.47 = (bf16[256,1024]{1,0:T(8,128)(2,1)S(1)}, bf16[256,1024]{1,0:T(8,128)(2,1)}, u32[]{:S(2)}, u32[]{:S(2)}) collective-permute-start(bf16[256,1024]{1,0:T(8,128)(2,1)S(1)} %pad_maximum_fusion.refs_0_), channel_id=1, source_target_pairs={{0,4},{1,5},{2,6},{3,7},{4,8},{5,9},{6,10},{7,11},{8,12},{9,13},{1... | collective-permute-start | bytes 1572872 | tf_op jit(solution)/shard_map/ppermute | solution.py:274
  16.7 13.9 %collective-permute-start.45 = (bf16[256,1024]{1,0:T(8,128)(2,1)S(1)}, bf16[256,1024]{1,0:T(8,128)(2,1)}, u32[]{:S(2)}, u32[]{:S(2)}) collective-permute-start(bf16[256,1024]{1,0:T(8,128)(2,1)S(1)} %pad_maximum_fusion.refs_0_), channel_id=1, source_target_pairs={{0,2},{1,3},{2,0},{3,1},{4,6},{5,7},{6,4},{7,5},{8,10},{9,11},{10,... | collective-permute-start | bytes 1572872 | tf_op jit(solution)/shard_map/ppermute | solution.py:277
  17.9 13.3 %collective-permute-start.44 = (bf16[256,1024]{1,0:T(8,128)(2,1)S(1)}, bf16[256,1024]{1,0:T(8,128)(2,1)S(1)}, u32[]{:S(2)}, u32[]{:S(2)}) collective-permute-start(bf16[256,1024]{1,0:T(8,128)(2,1)S(1)} %pad_maximum_fusion.refs_0_), channel_id=1, source_target_pairs={{0,1},{1,0},{2,3},{3,2},{4,5},{5,4},{6,7},{7,6},{8,9},{9,8},{10,11... | collective-permute-start | bytes 1572872 | tf_op jit(solution)/shard_map/ppermute | solution.py:280
  17.9 28.5 %collective-permute-start.4 = (bf16[6,704,128]{2,1,0:T(8,128)(2,1)}, bf16[6,704,128]{2,1,0:T(8,128)(2,1)}, u32[]{:S(2)}, u32[]{:S(2)}) collective-permute-start(bf16[6,704,128]{2,1,0:T(8,128)(2,1)} %bitcast.7.refs_0_), channel_id=1, source_target_pairs={{0,1},{1,0},{2,3},{3,2},{4,5},{5,4},{6,7},{7,6},{8,9},{9,8},{10,11... | collective-permute-start | bytes 3244040 | tf_op jit(solution)/shard_map/ppermute | solution.py:280
  18.4 28.2 %collective-permute-start.5 = (bf16[6,704,128]{2,1,0:T(8,128)(2,1)}, bf16[6,704,128]{2,1,0:T(8,128)(2,1)}, u32[]{:S(2)}, u32[]{:S(2)}) collective-permute-start(bf16[6,704,128]{2,1,0:T(8,128)(2,1)} %bitcast.8.refs_1_), channel_id=1, source_target_pairs={{0,1},{1,0},{2,3},{3,2},{4,5},{5,4},{6,7},{7,6},{8,9},{9,8},{10,11... | collective-permute-start | bytes 3244040 | tf_op jit(solution)/shard_map/ppermute | solution.py:280
  30.6 14.5 %collective-permute-start.21 = (bf16[128,2048]{1,0:T(8,128)(2,1)S(1)}, bf16[128,2048]{1,0:T(8,128)(2,1)S(1)}, u32[]{:S(2)}, u32[]{:S(2)}) collective-permute-start(bf16[128,2048]{1,0:T(8,128)(2,1)S(1)} %collective-permute-done.10.d00), channel_id=1, source_target_pairs={{0,4},{1,5},{2,6},{3,7},{4,8},{5,9},{6,10},{7,11},{8,12},{9,13},{1... | collective-permute-start | bytes 1572872 | tf_op jit(solution)/shard_map/ppermute | solution.py:274
  30.6 14.5 %collective-permute-start.12 = (bf16[128,2048]{1,0:T(8,128)(2,1)S(1)}, bf16[128,2048]{1,0:T(8,128)(2,1)S(1)}, u32[]{:S(2)}, u32[]{:S(2)}) collective-permute-start(bf16[128,2048]{1,0:T(8,128)(2,1)S(1)} %collective-permute-done.10.d00), channel_id=1, source_target_pairs={{0,2},{1,3},{2,0},{3,1},{4,6},{5,7},{6,4},{7,5},{8,10},{9,11},{10,... | collective-permute-start | bytes 1572872 | tf_op jit(solution)/shard_map/ppermute | solution.py:277
  31.2 14.0 %collective-permute-start.11 = (bf16[128,2048]{1,0:T(8,128)(2,1)S(1)}, bf16[128,2048]{1,0:T(8,128)(2,1)S(1)}, u32[]{:S(2)}, u32[]{:S(2)}) collective-permute-start(bf16[128,2048]{1,0:T(8,128)(2,1)S(1)} %collective-permute-done.10.d00), channel_id=1, source_target_pairs={{0,1},{1,0},{2,3},{3,2},{4,5},{5,4},{6,7},{7,6},{8,9},{9,8},{10,11... | collective-permute-start | bytes 1572872 | tf_op jit(solution)/shard_map/ppermute | solution.py:280
  45.1 11.3 %collective-permute-start.2 = (bf16[128,2048]{1,0:T(8,128)(2,1)S(1)}, bf16[128,2048]{1,0:T(8,128)(2,1)}, u32[]{:S(2)}, u32[]{:S(2)}) collective-permute-start(bf16[128,2048]{1,0:T(8,128)(2,1)S(1)} %collective-permute-done.1.d10), channel_id=1, source_target_pairs={{0,1},{1,0},{2,3},{3,2},{4,5},{5,4},{6,7},{7,6},{8,9},{9,8},{10,11... | collective-permute-start | bytes 1572872 | tf_op jit(solution)/shard_map/ppermute | solution.py:280
  45.1 16.4 %collective-permute-start.51 = (bf16[256,1024]{1,0:T(8,128)(2,1)}, bf16[256,1024]{1,0:T(8,128)(2,1)}, u32[]{:S(2)}, u32[]{:S(2)}) collective-permute-start(bf16[256,1024]{1,0:T(8,128)(2,1)} %collective-permute-done.47.refs_4_), channel_id=1, source_target_pairs={{0,4},{1,5},{2,6},{3,7},{4,8},{5,9},{6,10},{7,11},{8,12},{9,13},{1... | collective-permute-start | bytes 1572872 | tf_op jit(solution)/shard_map/ppermute | solution.py:274
  45.2 16.3 %collective-permute-start.49 = (bf16[256,1024]{1,0:T(8,128)(2,1)}, bf16[256,1024]{1,0:T(8,128)(2,1)}, u32[]{:S(2)}, u32[]{:S(2)}) collective-permute-start(bf16[256,1024]{1,0:T(8,128)(2,1)} %collective-permute-done.47.refs_4_), channel_id=1, source_target_pairs={{0,2},{1,3},{2,0},{3,1},{4,6},{5,7},{6,4},{7,5},{8,10},{9,11},{10,... | collective-permute-start | bytes 1572872 | tf_op jit(solution)/shard_map/ppermute | solution.py:277
  46.4 16.5 %collective-permute-start.48 = (bf16[256,1024]{1,0:T(8,128)(2,1)}, bf16[256,1024]{1,0:T(8,128)(2,1)S(1)}, u32[]{:S(2)}, u32[]{:S(2)}) collective-permute-start(bf16[256,1024]{1,0:T(8,128)(2,1)} %collective-permute-done.47.refs_4_), channel_id=1, source_target_pairs={{0,1},{1,0},{2,3},{3,2},{4,5},{5,4},{6,7},{7,6},{8,9},{9,8},{10,11... | collective-permute-start | bytes 1572872 | tf_op jit(solution)/shard_map/ppermute | solution.py:280
  46.6 15.5 %collective-permute-start.46 = (bf16[256,1024]{1,0:T(8,128)(2,1)}, bf16[256,1024]{1,0:T(8,128)(2,1)S(1)}, u32[]{:S(2)}, u32[]{:S(2)}) collective-permute-start(bf16[256,1024]{1,0:T(8,128)(2,1)} %collective-permute-done.45.refs_2_), channel_id=1, source_target_pairs={{0,1},{1,0},{2,3},{3,2},{4,5},{5,4},{6,7},{7,6},{8,9},{9,8},{10,11... | collective-permute-start | bytes 1572872 | tf_op jit(solution)/shard_map/ppermute | solution.py:280
  56.4 10.1 %collective-permute-start.26 = (bf16[104,1408]{1,0:T(8,128)(2,1)}, bf16[104,1408]{1,0:T(8,128)(2,1)S(1)}, u32[]{:S(2)}, u32[]{:S(2)}) collective-permute-start(bf16[104,1408]{1,0:T(8,128)(2,1)} %get-tuple-element.45), channel_id=1, source_target_pairs={{0,2},{1,3},{2,0},{3,1},{4,6},{5,7},{6,4},{7,5},{8,10},{9,11},{10,... | collective-permute-start | bytes 878600 | tf_op jit(solution)/shard_map/ppermute | solution.py:277
  61.5 20.3 %collective-permute-start.25 = (bf16[104,1408]{1,0:T(8,128)(2,1)}, bf16[104,1408]{1,0:T(8,128)(2,1)S(1)}, u32[]{:S(2)}, u32[]{:S(2)}) collective-permute-start(bf16[104,1408]{1,0:T(8,128)(2,1)} %get-tuple-element.44), channel_id=1, source_target_pairs={{0,8},{1,9},{2,10},{3,11},{4,12},{5,13},{6,14},{7,15},{8,0},{9,1},... | collective-permute-start | bytes 878600 | tf_op jit(solution)/shard_map/ppermute | solution.py:274
  61.5 20.3 %collective-permute-start.15 = (bf16[104,1408]{1,0:T(8,128)(2,1)}, bf16[104,1408]{1,0:T(8,128)(2,1)S(1)}, u32[]{:S(2)}, u32[]{:S(2)}) collective-permute-start(bf16[104,1408]{1,0:T(8,128)(2,1)} %get-tuple-element.41), channel_id=1, source_target_pairs={{0,2},{1,3},{2,0},{3,1},{4,6},{5,7},{6,4},{7,5},{8,10},{9,11},{10,... | collective-permute-start | bytes 878600 | tf_op jit(solution)/shard_map/ppermute | solution.py:277
  62.1 20.4 %collective-permute-start.14 = (bf16[104,1408]{1,0:T(8,128)(2,1)}, bf16[104,1408]{1,0:T(8,128)(2,1)S(1)}, u32[]{:S(2)}, u32[]{:S(2)}) collective-permute-start(bf16[104,1408]{1,0:T(8,128)(2,1)} %get-tuple-element.40), channel_id=1, source_target_pairs={{0,4},{1,5},{2,6},{3,7},{4,8},{5,9},{6,10},{7,11},{8,12},{9,13},{1... | collective-permute-start | bytes 878600 | tf_op jit(solution)/shard_map/ppermute | solution.py:274
  62.9 19.6 %collective-permute-start.6 = (bf16[104,1408]{1,0:T(8,128)(2,1)}, bf16[104,1408]{1,0:T(8,128)(2,1)S(1)}, u32[]{:S(2)}, u32[]{:S(2)}) collective-permute-start(bf16[104,1408]{1,0:T(8,128)(2,1)} %get-tuple-element.37), channel_id=1, source_target_pairs={{0,2},{1,3},{2,0},{3,1},{4,6},{5,7},{6,4},{7,5},{8,10},{9,11},{10,... | collective-permute-start | bytes 878600 | tf_op jit(solution)/shard_map/ppermute | solution.py:277
  66.5 78.5 %collective-permute-start.23 = (bf16[128,2048]{1,0:T(8,128)(2,1)S(1)}, bf16[128,2048]{1,0:T(8,128)(2,1)S(1)}, u32[]{:S(2)}, u32[]{:S(2)}) collective-permute-start(bf16[128,2048]{1,0:T(8,128)(2,1)S(1)} %collective-permute-done.21.d00), channel_id=1, source_target_pairs={{0,2},{1,3},{2,0},{3,1},{4,6},{5,7},{6,4},{7,5},{8,10},{9,11},{10,... | collective-permute-start | bytes 1572872 | tf_op jit(solution)/shard_map/ppermute | solution.py:277
  81.9 63.3 %collective-permute-start.22 = (bf16[128,2048]{1,0:T(8,128)(2,1)S(1)}, bf16[128,2048]{1,0:T(8,128)(2,1)S(1)}, u32[]{:S(2)}, u32[]{:S(2)}) collective-permute-start(bf16[128,2048]{1,0:T(8,128)(2,1)S(1)} %collective-permute-done.21.d00), channel_id=1, source_target_pairs={{0,1},{1,0},{2,3},{3,2},{4,5},{5,4},{6,7},{7,6},{8,9},{9,8},{10,11... | collective-permute-start | bytes 1572872 | tf_op jit(solution)/shard_map/ppermute | solution.py:280
  81.9 14.2 %collective-permute-start.37 = (bf16[104,1408]{1,0:T(8,128)(2,1)}, bf16[104,1408]{1,0:T(8,128)(2,1)S(1)}, u32[]{:S(2)}, u32[]{:S(2)}) collective-permute-start(bf16[104,1408]{1,0:T(8,128)(2,1)} %get-tuple-element.49), channel_id=1, source_target_pairs={{0,2},{1,3},{2,0},{3,1},{4,6},{5,7},{6,4},{7,5},{8,10},{9,11},{10,... | collective-permute-start | bytes 878600 | tf_op jit(solution)/shard_map/ppermute | solution.py:277
  82.5 62.6 %collective-permute-start.36 = (bf16[104,1408]{1,0:T(8,128)(2,1)}, bf16[104,1408]{1,0:T(8,128)(2,1)S(1)}, u32[]{:S(2)}, u32[]{:S(2)}) collective-permute-start(bf16[104,1408]{1,0:T(8,128)(2,1)} %get-tuple-element.48), channel_id=1, source_target_pairs={{0,12},{1,13},{2,14},{3,15},{4,0},{5,1},{6,2},{7,3},{8,4},{9,5},{1... | collective-permute-start | bytes 878600 | tf_op jit(solution)/shard_map/ppermute | solution.py:274
  82.5 75.9 %collective-permute-start.13 = (bf16[128,2048]{1,0:T(8,128)(2,1)S(1)}, bf16[128,2048]{1,0:T(8,128)(2,1)S(1)}, u32[]{:S(2)}, u32[]{:S(2)}) collective-permute-start(bf16[128,2048]{1,0:T(8,128)(2,1)S(1)} %collective-permute-done.12.d10), channel_id=1, source_target_pairs={{0,1},{1,0},{2,3},{3,2},{4,5},{5,4},{6,7},{7,6},{8,9},{9,8},{10,11... | collective-permute-start | bytes 1572872 | tf_op jit(solution)/shard_map/ppermute | solution.py:280
  96.1 63.6 %collective-permute-start.32 = (bf16[128,2048]{1,0:T(8,128)(2,1)S(1)}, bf16[128,2048]{1,0:T(8,128)(2,1)S(1)}, u32[]{:S(2)}, u32[]{:S(2)}) collective-permute-start(bf16[128,2048]{1,0:T(8,128)(2,1)S(1)} %collective-permute-done.21.d00), channel_id=1, source_target_pairs={{0,4},{1,5},{2,6},{3,7},{4,8},{5,9},{6,10},{7,11},{8,12},{9,13},{1... | collective-permute-start | bytes 1572872 | tf_op jit(solution)/shard_map/ppermute | solution.py:274
  145.1 20.1 %collective-permute-start.27 = (bf16[104,1408]{1,0:T(8,128)(2,1)S(1)}, bf16[104,1408]{1,0:T(8,128)(2,1)S(1)}, u32[]{:S(2)}, u32[]{:S(2)}) collective-permute-start(bf16[104,1408]{1,0:T(8,128)(2,1)S(1)} %collective-permute-done.26), channel_id=1, source_target_pairs={{0,8},{1,9},{2,10},{3,11},{4,12},{5,13},{6,14},{7,15},{8,0},{9,1},... | collective-permute-start | bytes 878600 | tf_op jit(solution)/shard_map/ppermute | solution.py:274
  145.1 20.1 %collective-permute-start.16 = (bf16[104,1408]{1,0:T(8,128)(2,1)S(1)}, bf16[104,1408]{1,0:T(8,128)(2,1)S(1)}, u32[]{:S(2)}, u32[]{:S(2)}) collective-permute-start(bf16[104,1408]{1,0:T(8,128)(2,1)S(1)} %collective-permute-done.15), channel_id=1, source_target_pairs={{0,4},{1,5},{2,6},{3,7},{4,8},{5,9},{6,10},{7,11},{8,12},{9,13},{1... | collective-permute-start | bytes 878600 | tf_op jit(solution)/shard_map/ppermute | solution.py:274
  145.2 22.8 %collective-permute-start.38 = (bf16[104,1408]{1,0:T(8,128)(2,1)S(1)}, bf16[104,1408]{1,0:T(8,128)(2,1)S(1)}, u32[]{:S(2)}, u32[]{:S(2)}) collective-permute-start(bf16[104,1408]{1,0:T(8,128)(2,1)S(1)} %collective-permute-done.37), channel_id=1, source_target_pairs={{0,12},{1,13},{2,14},{3,15},{4,0},{5,1},{6,2},{7,3},{8,4},{9,5},{1... | collective-permute-start | bytes 878600 | tf_op jit(solution)/shard_map/ppermute | solution.py:274
  158.5 13.0 %collective-permute-start.8 = (bf16[104,2048]{1,0:T(8,128)(2,1)}, bf16[104,2048]{1,0:T(8,128)(2,1)S(1)}, u32[]{:S(2)}, u32[]{:S(2)}) collective-permute-start(bf16[104,2048]{1,0:T(8,128)(2,1)} %get-tuple-element.39), channel_id=1, source_target_pairs={{0,2},{1,3},{2,0},{3,1},{4,6},{5,7},{6,4},{7,5},{8,10},{9,11},{10,... | collective-permute-start | bytes 1277960 | tf_op jit(solution)/shard_map/ppermute | solution.py:277
  159.7 13.2 %collective-permute-start.7 = (bf16[104,2048]{1,0:T(8,128)(2,1)}, bf16[104,2048]{1,0:T(8,128)(2,1)S(1)}, u32[]{:S(2)}, u32[]{:S(2)}) collective-permute-start(bf16[104,2048]{1,0:T(8,128)(2,1)} %get-tuple-element.38.r00), channel_id=1, source_target_pairs={{0,1},{1,0},{2,3},{3,2},{4,5},{5,4},{6,7},{7,6},{8,9},{9,8},{10,11... | collective-permute-start | bytes 1277960 | tf_op jit(solution)/shard_map/ppermute | solution.py:280
  165.1 15.9 %collective-permute-start.55 = (bf16[256,1024]{1,0:T(8,128)(2,1)}, bf16[256,1024]{1,0:T(8,128)(2,1)S(1)}, u32[]{:S(2)}, u32[]{:S(2)}) collective-permute-start(bf16[256,1024]{1,0:T(8,128)(2,1)} %collective-permute-done.51.refs_8_), channel_id=1, source_target_pairs={{0,4},{1,5},{2,6},{3,7},{4,8},{5,9},{6,10},{7,11},{8,12},{9,13},{1... | collective-permute-start | bytes 1572872 | tf_op jit(solution)/shard_map/ppermute | solution.py:274
  165.2 17.1 %collective-permute-start.53 = (bf16[256,1024]{1,0:T(8,128)(2,1)}, bf16[256,1024]{1,0:T(8,128)(2,1)S(1)}, u32[]{:S(2)}, u32[]{:S(2)}) collective-permute-start(bf16[256,1024]{1,0:T(8,128)(2,1)} %collective-permute-done.51.refs_8_), channel_id=1, source_target_pairs={{0,2},{1,3},{2,0},{3,1},{4,6},{5,7},{6,4},{7,5},{8,10},{9,11},{10,... | collective-permute-start | bytes 1572872 | tf_op jit(solution)/shard_map/ppermute | solution.py:277
  168.0 14.3 %collective-permute-start.50 = (bf16[256,1024]{1,0:T(8,128)(2,1)}, bf16[256,1024]{1,0:T(8,128)(2,1)}, u32[]{:S(2)}, u32[]{:S(2)}) collective-permute-start(bf16[256,1024]{1,0:T(8,128)(2,1)} %collective-permute-done.49.refs_6_), channel_id=1, source_target_pairs={{0,1},{1,0},{2,3},{3,2},{4,5},{5,4},{6,7},{7,6},{8,9},{9,8},{10,11... | collective-permute-start | bytes 1572872 | tf_op jit(solution)/shard_map/ppermute | solution.py:280
  171.4 21.8 %collective-permute-start.59 = (bf16[208,1408]{1,0:T(8,128)(2,1)}, bf16[208,1408]{1,0:T(8,128)(2,1)S(1)}, u32[]{:S(2)}, u32[]{:S(2)}) collective-permute-start(bf16[208,1408]{1,0:T(8,128)(2,1)} %get-tuple-element.52.refs_16_), channel_id=1, source_target_pairs={{0,16},{16,0},{1,17},{17,1},{2,18},{18,2},{3,19},{19,3},{4,20},{20... | collective-permute-start | bytes 1757192 | tf_op jit(solution)/shard_map/ppermute | solution.py:283
  173.0 19.4 %collective-permute-start.52 = (bf16[256,1024]{1,0:T(8,128)(2,1)}, bf16[256,1024]{1,0:T(8,128)(2,1)S(1)}, u32[]{:S(2)}, u32[]{:S(2)}) collective-permute-start(bf16[256,1024]{1,0:T(8,128)(2,1)} %collective-permute-done.51.refs_8_), channel_id=1, source_target_pairs={{0,1},{1,0},{2,3},{3,2},{4,5},{5,4},{6,7},{7,6},{8,9},{9,8},{10,11... | collective-permute-start | bytes 1572872 | tf_op jit(solution)/shard_map/ppermute | solution.py:280
  181.1 12.9 %collective-permute-start.34 = (bf16[128,2048]{1,0:T(8,128)(2,1)S(1)}, bf16[128,2048]{1,0:T(8,128)(2,1)S(1)}, u32[]{:S(2)}, u32[]{:S(2)}) collective-permute-start(bf16[128,2048]{1,0:T(8,128)(2,1)S(1)} %collective-permute-done.32.d00), channel_id=1, source_target_pairs={{0,2},{1,3},{2,0},{3,1},{4,6},{5,7},{6,4},{7,5},{8,10},{9,11},{10,... | collective-permute-start | bytes 1572872 | tf_op jit(solution)/shard_map/ppermute | solution.py:277
  182.3 24.7 %collective-permute-start.33 = (bf16[128,2048]{1,0:T(8,128)(2,1)S(1)}, bf16[128,2048]{1,0:T(8,128)(2,1)S(1)}, u32[]{:S(2)}, u32[]{:S(2)}) collective-permute-start(bf16[128,2048]{1,0:T(8,128)(2,1)S(1)} %collective-permute-done.32.d00), channel_id=1, source_target_pairs={{0,1},{1,0},{2,3},{3,2},{4,5},{5,4},{6,7},{7,6},{8,9},{9,8},{10,11... | collective-permute-start | bytes 1572872 | tf_op jit(solution)/shard_map/ppermute | solution.py:280
  182.3 23.4 %collective-permute-start.24 = (bf16[128,2048]{1,0:T(8,128)(2,1)S(1)}, bf16[128,2048]{1,0:T(8,128)(2,1)S(1)}, u32[]{:S(2)}, u32[]{:S(2)}) collective-permute-start(bf16[128,2048]{1,0:T(8,128)(2,1)S(1)} %collective-permute-done.23.d10), channel_id=1, source_target_pairs={{0,1},{1,0},{2,3},{3,2},{4,5},{5,4},{6,7},{7,6},{8,9},{9,8},{10,11... | collective-permute-start | bytes 1572872 | tf_op jit(solution)/shard_map/ppermute | solution.py:280
  192.3 12.1 %collective-permute-start.18 = (bf16[104,2048]{1,0:T(8,128)(2,1)}, bf16[104,2048]{1,0:T(8,128)(2,1)S(1)}, u32[]{:S(2)}, u32[]{:S(2)}) collective-permute-start(bf16[104,2048]{1,0:T(8,128)(2,1)} %get-tuple-element.43), channel_id=1, source_target_pairs={{0,2},{1,3},{2,0},{3,1},{4,6},{5,7},{6,4},{7,5},{8,10},{9,11},{10,... | collective-permute-start | bytes 1277960 | tf_op jit(solution)/shard_map/ppermute | solution.py:277
  193.2 12.4 %collective-permute-start.17 = (bf16[104,2048]{1,0:T(8,128)(2,1)}, bf16[104,2048]{1,0:T(8,128)(2,1)S(1)}, u32[]{:S(2)}, u32[]{:S(2)}) collective-permute-start(bf16[104,2048]{1,0:T(8,128)(2,1)} %get-tuple-element.42.r00), channel_id=1, source_target_pairs={{0,1},{1,0},{2,3},{3,2},{4,5},{5,4},{6,7},{7,6},{8,9},{9,8},{10,11... | collective-permute-start | bytes 1277960 | tf_op jit(solution)/shard_map/ppermute | solution.py:280
  194.0 22.7 %collective-permute-start.35 = (bf16[128,2048]{1,0:T(8,128)(2,1)S(1)}, bf16[128,2048]{1,0:T(8,128)(2,1)S(1)}, u32[]{:S(2)}, u32[]{:S(2)}) collective-permute-start(bf16[128,2048]{1,0:T(8,128)(2,1)S(1)} %collective-permute-done.34.d10), channel_id=1, source_target_pairs={{0,1},{1,0},{2,3},{3,2},{4,5},{5,4},{6,7},{7,6},{8,9},{9,8},{10,11... | collective-permute-start | bytes 1572872 | tf_op jit(solution)/shard_map/ppermute | solution.py:280
  204.4 23.9 %collective-permute-start.60 = (bf16[208,1408]{1,0:T(8,128)(2,1)}, bf16[208,1408]{1,0:T(8,128)(2,1)S(1)}, u32[]{:S(2)}, u32[]{:S(2)}) collective-permute-start(bf16[208,1408]{1,0:T(8,128)(2,1)} %get-tuple-element.53.refs_18_), channel_id=1, source_target_pairs={{0,16},{16,0},{1,17},{17,1},{2,18},{18,2},{3,19},{19,3},{4,20},{20... | collective-permute-start | bytes 1757192 | tf_op jit(solution)/shard_map/ppermute | solution.py:283
  205.6 21.5 %collective-permute-start.9 = (bf16[104,2048]{1,0:T(8,128)(2,1)S(1)}, bf16[104,2048]{1,0:T(8,128)(2,1)S(1)}, u32[]{:S(2)}, u32[]{:S(2)}) collective-permute-start(bf16[104,2048]{1,0:T(8,128)(2,1)S(1)} %collective-permute-done.8.r10), channel_id=1, source_target_pairs={{0,1},{1,0},{2,3},{3,2},{4,5},{5,4},{6,7},{7,6},{8,9},{9,8},{10,11... | collective-permute-start | bytes 1277960 | tf_op jit(solution)/shard_map/ppermute | solution.py:280
  205.7 22.7 %collective-permute-start.57 = (bf16[256,1024]{1,0:T(8,128)(2,1)S(1)}, bf16[256,1024]{1,0:T(8,128)(2,1)S(1)}, u32[]{:S(2)}, u32[]{:S(2)}) collective-permute-start(bf16[256,1024]{1,0:T(8,128)(2,1)S(1)} %collective-permute-done.55.refs_12_), channel_id=1, source_target_pairs={{0,2},{1,3},{2,0},{3,1},{4,6},{5,7},{6,4},{7,5},{8,10},{9,11},{10,... | collective-permute-start | bytes 1572872 | tf_op jit(solution)/shard_map/ppermute | solution.py:277
  206.9 22.2 %collective-permute-start.54 = (bf16[256,1024]{1,0:T(8,128)(2,1)S(1)}, bf16[256,1024]{1,0:T(8,128)(2,1)}, u32[]{:S(2)}, u32[]{:S(2)}) collective-permute-start(bf16[256,1024]{1,0:T(8,128)(2,1)S(1)} %collective-permute-done.53.refs_10_), channel_id=1, source_target_pairs={{0,1},{1,0},{2,3},{3,2},{4,5},{5,4},{6,7},{7,6},{8,9},{9,8},{10,11... | collective-permute-start | bytes 1572872 | tf_op jit(solution)/shard_map/ppermute | solution.py:280
  216.7 12.5 %collective-permute-start.29 = (bf16[104,2048]{1,0:T(8,128)(2,1)}, bf16[104,2048]{1,0:T(8,128)(2,1)S(1)}, u32[]{:S(2)}, u32[]{:S(2)}) collective-permute-start(bf16[104,2048]{1,0:T(8,128)(2,1)} %get-tuple-element.47), channel_id=1, source_target_pairs={{0,2},{1,3},{2,0},{3,1},{4,6},{5,7},{6,4},{7,5},{8,10},{9,11},{10,... | collective-permute-start | bytes 1277960 | tf_op jit(solution)/shard_map/ppermute | solution.py:277
  227.1 12.2 %collective-permute-start.40 = (bf16[104,2048]{1,0:T(8,128)(2,1)}, bf16[104,2048]{1,0:T(8,128)(2,1)S(1)}, u32[]{:S(2)}, u32[]{:S(2)}) collective-permute-start(bf16[104,2048]{1,0:T(8,128)(2,1)} %get-tuple-element.51), channel_id=1, source_target_pairs={{0,2},{1,3},{2,0},{3,1},{4,6},{5,7},{6,4},{7,5},{8,10},{9,11},{10,... | collective-permute-start | bytes 1277960 | tf_op jit(solution)/shard_map/ppermute | solution.py:277
  228.3 11.0 %collective-permute-start.19 = (bf16[104,2048]{1,0:T(8,128)(2,1)S(1)}, bf16[104,2048]{1,0:T(8,128)(2,1)S(1)}, u32[]{:S(2)}, u32[]{:S(2)}) collective-permute-start(bf16[104,2048]{1,0:T(8,128)(2,1)S(1)} %collective-permute-done.18.r10), channel_id=1, source_target_pairs={{0,1},{1,0},{2,3},{3,2},{4,5},{5,4},{6,7},{7,6},{8,9},{9,8},{10,11... | collective-permute-start | bytes 1277960 | tf_op jit(solution)/shard_map/ppermute | solution.py:280
  228.4 11.4 %collective-permute-start.28 = (bf16[104,2048]{1,0:T(8,128)(2,1)S(1)}, bf16[104,2048]{1,0:T(8,128)(2,1)S(1)}, u32[]{:S(2)}, u32[]{:S(2)}) collective-permute-start(bf16[104,2048]{1,0:T(8,128)(2,1)S(1)} %copy-done.24), channel_id=1, source_target_pairs={{0,1},{1,0},{2,3},{3,2},{4,5},{5,4},{6,7},{7,6},{8,9},{9,8},{10,11... | collective-permute-start | bytes 1277960 | tf_op jit(solution)/shard_map/ppermute | solution.py:280
  229.2 11.5 %collective-permute-start.30 = (bf16[104,2048]{1,0:T(8,128)(2,1)S(1)}, bf16[104,2048]{1,0:T(8,128)(2,1)S(1)}, u32[]{:S(2)}, u32[]{:S(2)}) collective-permute-start(bf16[104,2048]{1,0:T(8,128)(2,1)S(1)} %collective-permute-done.29.r10), channel_id=1, source_target_pairs={{0,1},{1,0},{2,3},{3,2},{4,5},{5,4},{6,7},{7,6},{8,9},{9,8},{10,11... | collective-permute-start | bytes 1277960 | tf_op jit(solution)/shard_map/ppermute | solution.py:280
  229.2 11.5 %collective-permute-start.39 = (bf16[104,2048]{1,0:T(8,128)(2,1)}, bf16[104,2048]{1,0:T(8,128)(2,1)S(1)}, u32[]{:S(2)}, u32[]{:S(2)}) collective-permute-start(bf16[104,2048]{1,0:T(8,128)(2,1)} %get-tuple-element.50.r00), channel_id=1, source_target_pairs={{0,1},{1,0},{2,3},{3,2},{4,5},{5,4},{6,7},{7,6},{8,9},{9,8},{10,11... | collective-permute-start | bytes 1277960 | tf_op jit(solution)/shard_map/ppermute | solution.py:280
  239.3 12.2 %collective-permute-start.41 = (bf16[104,2048]{1,0:T(8,128)(2,1)S(1)}, bf16[104,2048]{1,0:T(8,128)(2,1)S(1)}, u32[]{:S(2)}, u32[]{:S(2)}) collective-permute-start(bf16[104,2048]{1,0:T(8,128)(2,1)S(1)} %collective-permute-done.40.r10), channel_id=1, source_target_pairs={{0,1},{1,0},{2,3},{3,2},{4,5},{5,4},{6,7},{7,6},{8,9},{9,8},{10,11... | collective-permute-start | bytes 1277960 | tf_op jit(solution)/shard_map/ppermute | solution.py:280
  239.3 23.6 %collective-permute-start.56 = (bf16[256,1024]{1,0:T(8,128)(2,1)S(1)}, bf16[256,1024]{1,0:T(8,128)(2,1)S(1)}, u32[]{:S(2)}, u32[]{:S(2)}) collective-permute-start(bf16[256,1024]{1,0:T(8,128)(2,1)S(1)} %collective-permute-done.55.refs_12_), channel_id=1, source_target_pairs={{0,1},{1,0},{2,3},{3,2},{4,5},{5,4},{6,7},{7,6},{8,9},{9,8},{10,11... | collective-permute-start | bytes 1572872 | tf_op jit(solution)/shard_map/ppermute | solution.py:280
  239.9 23.7 %collective-permute-start.61 = (bf16[208,1408]{1,0:T(8,128)(2,1)S(1)}, bf16[208,1408]{1,0:T(8,128)(2,1)S(1)}, u32[]{:S(2)}, u32[]{:S(2)}) collective-permute-start(bf16[208,1408]{1,0:T(8,128)(2,1)S(1)} %copy-done.42), channel_id=1, source_target_pairs={{0,16},{16,0},{1,17},{17,1},{2,18},{18,2},{3,19},{19,3},{4,20},{20... | collective-permute-start | bytes 1757192 | tf_op jit(solution)/shard_map/ppermute | solution.py:283
  240.7 27.6 %collective-permute-start.58 = (bf16[256,1024]{1,0:T(8,128)(2,1)S(1)}, bf16[256,1024]{1,0:T(8,128)(2,1)S(1)}, u32[]{:S(2)}, u32[]{:S(2)}) collective-permute-start(bf16[256,1024]{1,0:T(8,128)(2,1)S(1)} %collective-permute-done.57.refs_14_), channel_id=1, source_target_pairs={{0,1},{1,0},{2,3},{3,2},{4,5},{5,4},{6,7},{7,6},{8,9},{9,8},{10,11... | collective-permute-start | bytes 1572872 | tf_op jit(solution)/shard_map/ppermute | solution.py:280
  240.7 32.1 %collective-permute-start.62 = (bf16[208,1408]{1,0:T(8,128)(2,1)}, bf16[208,1408]{1,0:T(8,128)(2,1)}, u32[]{:S(2)}, u32[]{:S(2)}) collective-permute-start(bf16[208,1408]{1,0:T(8,128)(2,1)} %get-tuple-element.55.refs_22_), channel_id=1, source_target_pairs={{0,16},{16,0},{1,17},{17,1},{2,18},{18,2},{3,19},{19,3},{4,20},{20... | collective-permute-start | bytes 1757192 | tf_op jit(solution)/shard_map/ppermute | solution.py:283
  251.5 63.2 %collective-permute-start.63 = (bf16[704,1024]{1,0:T(8,128)(2,1)}, bf16[704,1024]{1,0:T(8,128)(2,1)S(1)}, u32[]{:S(2)}, u32[]{:S(2)}) collective-permute-start(bf16[704,1024]{1,0:T(8,128)(2,1)} %bitcast.40), channel_id=1, source_target_pairs={{0,16},{16,0},{1,17},{17,1},{2,18},{18,2},{3,19},{19,3},{4,20},{20... | collective-permute-start | bytes 4325384 | tf_op jit(solution)/shard_map/ppermute | solution.py:283
  262.9 29.0 %collective-permute-start.20 = (bf16[128,2048]{1,0:T(8,128)(2,1)S(1)}, bf16[128,2048]{1,0:T(8,128)(2,1)S(1)}, u32[]{:S(2)}, u32[]{:S(2)}) collective-permute-start(bf16[128,2048]{1,0:T(8,128)(2,1)S(1)} %copy-done.15), channel_id=1, source_target_pairs={{0,12},{1,13},{2,14},{3,15},{4,0},{5,1},{6,2},{7,3},{8,4},{9,5},{1... | collective-permute-start | bytes 1572872 | tf_op jit(solution)/shard_map/ppermute | solution.py:274
  263.5 50.0 %collective-permute-start.31 = (bf16[128,2048]{1,0:T(8,128)(2,1)S(1)}, bf16[128,2048]{1,0:T(8,128)(2,1)S(1)}, u32[]{:S(2)}, u32[]{:S(2)}) collective-permute-start(bf16[128,2048]{1,0:T(8,128)(2,1)S(1)} %copy-done.16), channel_id=1, source_target_pairs={{0,8},{1,9},{2,10},{3,11},{4,12},{5,13},{6,14},{7,15},{8,0},{9,1},... | collective-permute-start | bytes 1572872 | tf_op jit(solution)/shard_map/ppermute | solution.py:274
  268.3 45.3 %collective-permute-start.42 = (bf16[128,2048]{1,0:T(8,128)(2,1)}, bf16[128,2048]{1,0:T(8,128)(2,1)S(1)}, u32[]{:S(2)}, u32[]{:S(2)}) collective-permute-start(bf16[128,2048]{1,0:T(8,128)(2,1)} %combine.7), channel_id=1, source_target_pairs={{0,4},{1,5},{2,6},{3,7},{4,8},{5,9},{6,10},{7,11},{8,12},{9,13},{1... | collective-permute-start | bytes 1572872 | tf_op jit(solution)/shard_map/ppermute | solution.py:274
  (54 other events, 1302.0 us)

commit v2 on v1

--- a/solution.py
+++ b/solution.py
@@ -9,13 +9,13 @@
 
 BF16 = jnp.bfloat16
 F32 = jnp.float32
-VMEM_BYTES = 56 * 1024 * 1024
+MIB = 1024 * 1024
 NT = (((1,), (1,)), ((), ()))
 TN = (((0,), (0,)), ((), ()))
 
 
-def params():
-    return pltpu.CompilerParams(vmem_limit_bytes=VMEM_BYTES)
+def params(mib):
+    return pltpu.CompilerParams(vmem_limit_bytes=mib * MIB)
 
 
 def cost(flops, moved):
@@ -102,18 +102,25 @@
 
 
 def expert_kernel(
-    zn, nb, top, chip_rows, j, sc, meta, d00, d01, d10, d11, pre0, pre1, w_gate, w_up, w_down,
-    grads_out, hidden_out, rows_out, back0, back1,
+    top, chip_rows, sc, meta, d00, d01, d10, d11, pre0, pre1, w_gate, w_up, w_down,
+    grads_out, hidden_out, rows_out, back0, back1, down_at, both_at, sem,
 ):
-    z, x, c, g = sc[0], sc[1], sc[2], sc[3]
+    z, x, c = sc[0], sc[1], sc[2]
+    ffw = w_down.shape[0]
+    copies = [
+        pltpu.make_async_copy(w_down, down_at.at[pl.ds(0, ffw)], sem.at[0]),
+        pltpu.make_async_copy(w_down, down_at.at[pl.ds(ffw, ffw)], sem.at[1]),
+        pltpu.make_async_copy(w_gate, both_at.at[pl.ds(0, ffw)], sem.at[2]),
+        pltpu.make_async_copy(w_up, both_at.at[pl.ds(ffw, ffw)], sem.at[3]),
+    ]
+    for copy in copies:
+        copy.start()
     expert = (z * 4 + x * 2 + c).astype(F32)
-    source = z - j + jnp.where(z < j, zn, 0)
     before = before_matrix(d00.shape[0])
     picked, weights = [], []
     for xr, (own_ref, sib_ref) in enumerate(((d00, d01), (d10, d11))):
-        at = g * nb + source * 4 + lax.bitwise_and(x + xr, 1) * 2
-        own, own_gate = expert_hits(meta[at + c].astype(F32), top, expert)
-        sib, sib_gate = expert_hits(meta[at + 1 - c].astype(F32), top, expert)
+        own, own_gate = expert_hits(meta[0, xr, 0].astype(F32), top, expert)
+        sib, sib_gate = expert_hits(meta[0, xr, 1].astype(F32), top, expert)
         slot = jnp.concatenate(chip_slots(own, sib, c, before), axis=1)
         pick = slot_rows(slot, chip_rows)
         gates = jnp.concatenate([own_gate, sib_gate], axis=1)
@@ -123,9 +130,9 @@
     weight = jnp.concatenate(weights, axis=0)
     rows = jnp.concatenate(picked, axis=0).astype(BF16)
     rows_out[...] = rows
-    ffw = w_down.shape[0]
-    down = w_down[...]
-    back = lax.dot_general(rows, jnp.concatenate([down, down], axis=0), NT, preferred_element_type=F32)
+    copies[0].wait()
+    copies[1].wait()
+    back = lax.dot_general(rows, down_at[...], NT, preferred_element_type=F32)
     pre = jnp.concatenate([pre0[...].astype(F32), pre1[...].astype(F32)], axis=0)
     swapped = pltpu.roll(pre, ffw, axis=1)
     first = lax.broadcasted_iota(jnp.int32, pre.shape, 1) < ffw
@@ -137,17 +144,17 @@
     grads = (weight * back * slope).astype(BF16)
     grads_out[...] = grads
     hidden_out[...] = (weight * active * up_pre)[:, :ffw].astype(BF16)
-    route = dot(grads, jnp.concatenate([w_gate[...], w_up[...]], axis=0))
+    copies[2].wait()
+    copies[3].wait()
+    route = dot(grads, both_at[...])
     back0[...] = route[:chip_rows].astype(BF16)
     back1[...] = route[chip_rows:].astype(BF16)
 
 
-def combine_kernel(zn, nb, top, chip_rows, j, sc, meta, r00, r01, r10, r11, out):
-    z, x, c, g = sc[0], sc[1], sc[2], sc[3]
-    source = z - j + jnp.where(z < j, zn, 0)
-    at = g * nb + source * 4 + x * 2
-    own_meta = meta[at + c].astype(F32)
-    sib_meta = meta[at + 1 - c].astype(F32)
+def combine_kernel(top, chip_rows, sc, meta, r00, r01, r10, r11, out):
+    z, x, c = sc[0], sc[1], sc[2]
+    own_meta = meta[0, 0, 0].astype(F32)
+    sib_meta = meta[0, 0, 1].astype(F32)
     before = before_matrix(out.shape[0])
     total = jnp.zeros(out.shape, F32)
     for n, ref in enumerate((r00, r01, r10, r11)):
@@ -161,49 +168,43 @@
     out[...] = total.astype(BF16)
 
 
-def inner_kernel(zn, nb, ng, top, chip_rows, sc, meta, *refs):
+def inner_kernel(zn, ng, top, chip_rows, sc, *refs):
     n_x, n_g = 4 * zn, zn * ng
-    xs, gs = refs[:n_x], refs[n_x : n_x + n_g]
-    gate_out, up_out, table, grads, grads_t, rows, sem_x, sem_g = refs[n_x + n_g :]
+    metas, xs, gs = refs[:zn], refs[zn : zn + n_x], refs[zn + n_x : zn + n_x + n_g]
+    gate_out, up_out, table, grads, grads_t, rows, sem_x, sem_g = refs[zn + n_x + n_g :]
     tok = xs[0].shape[0] // ng
     ffw, width = gate_out.shape
     quad = 2 * chip_rows
     copies = []
-    for j in range(zn):
-        for n in range(4):
-            for r in range(ng):
-                copies.append(
-                    pltpu.make_async_copy(
-                        xs[4 * j + n].at[pl.ds(r * tok, tok)],
-                        table.at[j * ng + r, n // 2, pl.ds((n % 2) * tok, tok)],
-                        sem_x.at[len(copies)],
-                    )
-                )
     for u in range(n_g):
-        copies.append(pltpu.make_async_copy(gs[u], grads.at[pl.ds(u * quad, quad)], sem_g.at[u]))
-    for copy in copies:
-        copy.start()
-    z, x, c, g = sc[0], sc[1], sc[2], sc[3]
+        j, r = u // ng, u % ng
+        mine = [
+            pltpu.make_async_copy(
+                xs[4 * j + n].at[pl.ds(r * tok, tok)],
+                table.at[u, n // 2, pl.ds((n % 2) * tok, tok)],
+                sem_x.at[4 * u + n],
+            )
+            for n in range(4)
+        ]
+        mine.append(pltpu.make_async_copy(gs[u], grads.at[pl.ds(u * quad, quad)], sem_g.at[u]))
+        copies.append(mine)
+        for copy in mine:
+            copy.start()
+    z, x, c = sc[0], sc[1], sc[2]
     expert = (z * 4 + x * 2 + c).astype(F32)
     before = before_matrix(tok)
-    for copy in copies:
-        copy.wait()
-
-    def pick_rows(u, carry):
+    for u in range(n_g):
         j, r = u // ng, u % ng
-        source = lax.rem(z - j + zn, zn)
-        group = lax.rem(g - r + ng, ng)
-        picked = []
+        picks = []
         for xr in range(2):
-            at = group * nb + source * 4 + lax.bitwise_and(x + xr, 1) * 2
-            own, _ = expert_hits(meta[at + c].astype(F32), top, expert)
-            sib, _ = expert_hits(meta[at + 1 - c].astype(F32), top, expert)
+            own, _ = expert_hits(metas[j][r, xr, 0].astype(F32), top, expert)
+            sib, _ = expert_hits(metas[j][r, xr, 1].astype(F32), top, expert)
             slot = jnp.concatenate(chip_slots(own, sib, c, before), axis=1)
-            picked.append(dot(slot_rows(slot, chip_rows).astype(BF16), table[u, xr]))
-        rows[pl.ds(pl.multiple_of(u * quad, 16), quad), :] = jnp.concatenate(picked, axis=0).astype(BF16)
-        return carry
-
-    lax.fori_loop(0, n_g, pick_rows, 0)
+            picks.append(slot_rows(slot, chip_rows).astype(BF16))
+        for copy in copies[u]:
+            copy.wait()
+        picked = [dot(pick, table[u, xr]) for xr, pick in enumerate(picks)]
+        rows[u * quad : (u + 1) * quad, :] = jnp.concatenate(picked, axis=0).astype(BF16)
     total = n_g * quad
     step = 128
     for i in range(0, total, step):
@@ -299,8 +300,11 @@
         return jax.ShapeDtypeStruct(dims, dtype)
 
     meta = jnp.concatenate([expert_ids.T.astype(BF16), gate_values.T], axis=0)
-    meta_all = lax.all_gather(meta, ("grp", "blk"))
     meta_sib = over_core(meta)
+    chip_meta = jnp.stack([meta, meta_sib])
+    plane_meta = jnp.stack([chip_meta, over_x(chip_meta)])
+    all_meta = jnp.stack([plane_meta] + [over_groups(plane_meta, r) for r in range(1, ng)])
+    metas = [all_meta] + [shift(all_meta, j) for j in range(1, zn)]
     pre = [saved_gate_pre.transpose(1, 2, 0), saved_up_pre.transpose(1, 2, 0)]
     pre_sib = [over_core(p) for p in pre]
     grads_in = gathered(d_out)
@@ -314,7 +318,7 @@
             pltpu.VMEM((2 * ffw, 2 * top * tok), BF16),
             pltpu.SemaphoreType.DMA((4 * top,)),
         ],
-        compiler_params=params(),
+        compiler_params=params(24),
         cost_estimate=cost(2 * zn * quad * 2 * top * tok * 2 * ffw, 8 * top * tok * ffw * 2),
         name="pack",
     )(sc, meta, meta_sib, *pre, *pre_sib)
@@ -328,7 +332,7 @@
     for j in range(zn):
         done.append(
             pl.pallas_call(
-                functools.partial(expert_kernel, zn, nb, top, chip_rows, j),
+                functools.partial(expert_kernel, top, chip_rows),
                 out_shape=[
                     shape(quad, 2 * ffw),
                     shape(quad, ffw),
@@ -336,12 +340,17 @@
                     shape(chip_rows, width),
                     shape(chip_rows, width),
                 ],
-                in_specs=[smem] + [vmem] * 10,
+                in_specs=[smem] + [vmem] * 7 + [anywhere] * 3,
                 out_specs=[vmem] * 5,
-                compiler_params=params(),
+                scratch_shapes=[
+                    pltpu.VMEM((2 * ffw, width), BF16),
+                    pltpu.VMEM((2 * ffw, width), BF16),
+                    pltpu.SemaphoreType.DMA((4,)),
+                ],
+                compiler_params=params(32),
                 cost_estimate=cost(2 * quad * width * ffw * 4 + 2 * quad * tok * 2 * width, 16e6),
                 name="expert",
-            )(sc, meta_all, *grads_in[j], *arrived[j], *weights)
+            )(sc, metas[j], *grads_in[j], *arrived[j], *weights)
         )
 
     partials = []
@@ -349,14 +358,14 @@
         near, far = done[j][3], over_x(done[j][4])
         partials.append(
             pl.pallas_call(
-                functools.partial(combine_kernel, zn, nb, top, chip_rows, j),
+                functools.partial(combine_kernel, top, chip_rows),
                 out_shape=shape(tok, width),
                 in_specs=[smem] + [vmem] * 5,
                 out_specs=vmem,
-                compiler_params=params(),
+                compiler_params=params(12),
                 cost_estimate=cost(2 * 4 * tok * chip_rows * width, 3e6),
                 name="combine",
-            )(sc, meta_all, near, over_core(near), far, over_core(far))
+            )(sc, metas[j], near, over_core(near), far, over_core(far))
         )
     d_tokens = partials[0].astype(F32)
     for j in range(1, zn):
@@ -372,7 +381,7 @@
             pltpu.VMEM((zn * quad, width), BF16),
             pltpu.SemaphoreType.DMA((2 * zn,)),
         ],
-        compiler_params=params(),
+        compiler_params=params(24),
         cost_estimate=cost(2 * zn * quad * ffw * width, 10e6),
         name="outer",
     )(sc, *[d[1] for d in done], *[d[2] for d in done])
@@ -385,7 +394,8 @@
     for r in range(1, ng):
         there = lax.dynamic_slice(tokens, (0, ((g + r) % ng) * part), (tok, part))
         pieces.append(over_groups(there, r))
-    inputs = gathered(jnp.concatenate(pieces, axis=0))
+    block, _ = lax.optimization_barrier((jnp.concatenate(pieces, axis=0), packed[0]))
+    inputs = gathered(block)
     grads = []
     for j in range(zn):
         grads.append(done[j][0])
@@ -393,9 +403,9 @@
             grads.append(over_groups(done[j][0], r))
     units = zn * ng
     d_gate, d_up = pl.pallas_call(
-        functools.partial(inner_kernel, zn, nb, ng, top, chip_rows),
+        functools.partial(inner_kernel, zn, ng, top, chip_rows),
         out_shape=[shape(ffw, part)] * 2,
-        in_specs=[smem, vmem] + [anywhere] * (4 * zn + units),
+        in_specs=[smem] + [vmem] * zn + [anywhere] * (4 * zn + units),
         out_specs=[vmem, vmem],
         scratch_shapes=[
             pltpu.VMEM((units, 2, 2 * tok, part), BF16),
@@ -405,10 +415,10 @@
             pltpu.SemaphoreType.DMA((4 * units,)),
             pltpu.SemaphoreType.DMA((units,)),
         ],
-        compiler_params=params(),
+        compiler_params=params(40 if units <= 16 else 56),
         cost_estimate=cost(2 * units * quad * 2 * ffw * part, 20e6),
         name="inner",
-    )(sc, meta_all, *[block for plane in inputs for block in plane], *grads)
+    )(sc, *metas, *[block for plane in inputs for block in plane], *grads)
     return (
         d_tokens.astype(BF16),
         d_gate.T[None],

time: 317 us -> 292 us (0.921)
  the two profiles are of different devices: /device:TPU:0 before, /device:TPU:10 now
where the time goes in v2:
time: 292 us; the launch traced here: 289 us
  waiting for transfers between devices  146 us (50%)
  starting transfers between devices  59.9 us (21%)
  Pallas kernels  58.9 us (20%)
  local copies, waits for them, and re-layouts  18.9 us (6%)
  other arithmetic  4.29 us (1%)
    ppermute x18, waiting for transfers between devices, shift(): lax.ppermute(value, 'blk', [(b, (b + 4 * n) % nb) for b in range(nb)])  98.7 us
    ppermute x17, waiting for transfers between devices, over_x(): return lax.ppermute(value, 'blk', [(b, b ^ 2) for b in range(nb)])  37.2 us
    ppermute x18, starting transfers between devices, shift(): lax.ppermute(value, 'blk', [(b, (b + 4 * n) % nb) for b in range(nb)])  27.1 us
    pallas_call x4, Pallas kernels, per_device(): pl.pallas_call(functools.partial(expert_kernel, top, chip_rows), out_shap...  23.3 us
    ppermute x17, starting transfers between devices, over_x(): return lax.ppermute(value, 'blk', [(b, b ^ 2) for b in range(nb)])  18.9 us
    unnamed x92, local copies, waits for them, and re-layouts  17.8 us
    pallas_call x1, Pallas kernels, per_device(): pl.pallas_call(functools.partial(inner_kernel, zn, ng, top, chip_rows), o...  13.6 us
    ppermute x7, starting transfers between devices, over_groups(): return lax.ppermute(value, 'grp', [(b, (b + n) % ng) for b in range(ng)])  9.25 us
  transfers between devices with their start and end apart: 69, of which 23 were waited for; matrix products, arithmetic and copies ran while one was open for 1% of the time, Pallas kernels for 20%

profile of v2, /device:TPU:10, one launch (start us, length us, event | category | flops | bytes accessed | tf_op | source)
XLA Modules:
  0.0 289.4 jit_solution(15715261664111957793)
XLA Ops:
  2.7 1.9 collective-permute-done.meta_sib
  5.1 3.1 %collective-permute-done.1 = bf16[2,12,128]{2,1,0:T(8,128)(2,1)S(1)} collective-permute-done((bf16[2,12,128]{2,1,0:T(8,128)(2,1)S(1)}, bf16[2,12,128]{2,1,0:T(8,128)(2,1)S(1)}, u32[]{:S(2)}, u32[]{:S(2)}) %collective-permute-start.1) | collective-permute-done | bytes 6176 | tf_op jit(solution)/shard_map/ppermute | solution.py:278
  8.3 1.6 collective-permute-start.2
  10.4 1.6 collective-permute-start.13
  12.6 12.2 %collective-permute-done.36.meta.refs_3_ = bf16[2,2,2,12,128]{4,3,2,1,0:T(8,128)(2,1)S(1)} collective-permute-done((bf16[2,2,2,12,128]{4,3,2,1,0:T(8,128)(2,1)S(1)}, bf16[2,2,2,12,128]{4,3,2,1,0:T(8,128)(2,1)S(1)}, u32[]{:S(2)}, u32[]{:S(2)}) %collective-permute-start.36) | collective-permute-done | bytes 24608 | tf_op jit(solution)/shard_map/ppermute | solution.py:275
  24.8 1.5 collective-permute-start.24
  26.3 3.4 %collective-permute-done.24.meta.refs_2_ = bf16[2,2,2,12,128]{4,3,2,1,0:T(8,128)(2,1)S(1)} collective-permute-done((bf16[2,2,2,12,128]{4,3,2,1,0:T(8,128)(2,1)S(1)}, bf16[2,2,2,12,128]{4,3,2,1,0:T(8,128)(2,1)S(1)}, u32[]{:S(2)}, u32[]{:S(2)}) %collective-permute-start.24) | collective-permute-done | bytes 24608 | tf_op jit(solution)/shard_map/ppermute | solution.py:275
  31.2 2.4 collective-permute-done.12.meta.refs_1_
  33.9 6.0 %collective-permute-done.48 = bf16[128,1024]{1,0:T(8,128)(2,1)S(1)} collective-permute-done((bf16[128,1024]{1,0:T(8,128)(2,1)S(1)}, bf16[128,1024]{1,0:T(8,128)(2,1)S(1)}, u32[]{:S(2)}, u32[]{:S(2)}) %collective-permute-start.48) | collective-permute-done | bytes 262176 | tf_op jit(solution)/shard_map/ppermute | solution.py:284
  41.0 1.5 collective-permute-start.15
  42.6 1.2 copy-done.4
  43.8 1.2 copy-done.5
  45.1 8.6 %pack.1 = (bf16[104,1408]{1,0:T(8,128)(2,1)S(1)}, bf16[104,1408]{1,0:T(8,128)(2,1)S(1)}, bf16[104,1408]{1,0:T(8,128)(2,1)S(1)}, bf16[104,1408]{1,0:T(8,128)(2,1)...) custom-call(s32[4]{0:T(128)S(1)} %pad_add_fusion.sc, ...), custom_call_target="tpu_custom_call" | custom-call | flops 3598712832 | bytes 8650752 | tf_op jit(solution)/shard_map/pack/pallas_call | solution.py:312
  54.3 1.8 collective-permute-start.17
  56.1 1.5 collective-permute-start.18
  57.6 2.1 collective-permute-start.29
  60.2 3.3 %collective-permute-done.8.pre1 = bf16[104,1408]{1,0:T(8,128)(2,1)S(1)} collective-permute-done((bf16[104,1408]{1,0:T(8,128)(2,1)S(1)}, bf16[104,1408]{1,0:T(8,128)(2,1)S(1)}, u32[]{:S(2)}, u32[]{:S(2)}) %collective-permute-start.8) | collective-permute-done | bytes 292896 | tf_op jit(solution)/shard_map/ppermute | solution.py:278
  63.5 1.5 collective-permute-start.41
  65.0 10.7 %collective-permute-done.17.pre0 = bf16[104,1408]{1,0:T(8,128)(2,1)S(1)} collective-permute-done((bf16[104,1408]{1,0:T(8,128)(2,1)S(1)}, bf16[104,1408]{1,0:T(8,128)(2,1)S(1)}, u32[]{:S(2)}, u32[]{:S(2)}) %collective-permute-start.17) | collective-permute-done | bytes 292896 | tf_op jit(solution)/shard_map/ppermute | solution.py:275
  75.7 2.7 collective-permute-start.37
  78.4 1.5 collective-permute-start.27
  79.9 2.3 collective-permute-done.29.pre0
  82.2 1.5 collective-permute-start.42
  83.7 11.8 %collective-permute-done.41.pre0 = bf16[104,1408]{1,0:T(8,128)(2,1)S(1)} collective-permute-done((bf16[104,1408]{1,0:T(8,128)(2,1)S(1)}, bf16[104,1408]{1,0:T(8,128)(2,1)S(1)}, u32[]{:S(2)}, u32[]{:S(2)}) %collective-permute-start.41) | collective-permute-done | bytes 292896 | tf_op jit(solution)/shard_map/ppermute | solution.py:275
  95.6 1.3 collective-permute-start.50
  98.1 3.2 %collective-permute-start.31 = (bf16[104,1408]{1,0:T(8,128)(2,1)S(1)}, bf16[104,1408]{1,0:T(8,128)(2,1)S(1)}, u32[]{:S(2)}, u32[]{:S(2)}) collective-permute-start(bf16[104,1408]{1,0:T(8,128)(2,1)S(1)} %collective-permute-done.30), channel_id=1, source_target_pairs={{0,8},{1,9},{2,10},{3,11},{4,12},{5,13},{6,14},{7,15},{8,0},{9,1},... | collective-permute-start | bytes 878600 | tf_op jit(solution)/shard_map/ppermute | solution.py:275
  101.4 5.8 %expert.4 = (bf16[208,1408]{1,0:T(8,128)(2,1)S(1)}, bf16[208,704]{1,0:T(8,128)(2,1)S(1)}, bf16[208,2048]{1,0:T(8,128)(2,1)S(1)}, bf16[104,2048]{1,0:T(8,128)(2,1)S(1)}, bf16[104,2048]{1,0:T(8,128)(2,1)S(1)}) custom-call(s32[4]{0:T(128)S(1)} %pad_add_fusion.sc, bf16[2,2,2,12,128]{4,3,2,1,0:T(8,128)(2,1)S(1)} %pad_maximum_fusion.1.meta.refs_0_, ...), custom_call_target="tpu_custom_call" | custom-call | flops 2617245696 | bytes 16000000 | tf_op jit(solution)/shard_map/expert/pallas_call | solution.py:334
  107.9 2.4 collective-permute-done.52.refs_8_
  110.3 1.3 collective-permute-start.10
  111.9 4.7 %collective-permute-done.19.pre1 = bf16[104,1408]{1,0:T(8,128)(2,1)S(1)} collective-permute-done((bf16[104,1408]{1,0:T(8,128)(2,1)S(1)}, bf16[104,1408]{1,0:T(8,128)(2,1)S(1)}, u32[]{:S(2)}, u32[]{:S(2)}) %collective-permute-start.19) | collective-permute-done | bytes 292896 | tf_op jit(solution)/shard_map/ppermute | solution.py:275
  116.6 2.0 collective-permute-start.64
  118.6 14.3 %collective-permute-done.31.pre1 = bf16[104,1408]{1,0:T(8,128)(2,1)S(1)} collective-permute-done((bf16[104,1408]{1,0:T(8,128)(2,1)S(1)}, bf16[104,1408]{1,0:T(8,128)(2,1)S(1)}, u32[]{:S(2)}, u32[]{:S(2)}) %collective-permute-start.31) | collective-permute-done | bytes 292896 | tf_op jit(solution)/shard_map/ppermute | solution.py:275
  132.9 1.3 collective-permute-start.39
  134.1 5.8 %expert.5 = (bf16[208,1408]{1,0:T(8,128)(2,1)S(1)}, bf16[208,704]{1,0:T(8,128)(2,1)S(1)}, bf16[208,2048]{1,0:T(8,128)(2,1)S(1)}, bf16[104,2048]{1,0:T(8,128)(2,1)S(1)}, bf16[104,2048]{1,0:T(8,128)(2,1)S(1)}) custom-call(s32[4]{0:T(128)S(1)} %pad_add_fusion.sc, bf16[2,2,2,12,128]{4,3,2,1,0:T(8,128)(2,1)S(1)} %collective-permute-done.12.meta.refs_1_, ...), custom_call_target="tpu_custom_call" | custom-call | flops 2617245696 | bytes 16000000 | tf_op jit(solution)/shard_map/expert/pallas_call | solution.py:334
  142.0 13.7 %collective-permute-done.21.r10 = bf16[104,2048]{1,0:T(8,128)(2,1)S(1)} collective-permute-done((bf16[104,2048]{1,0:T(8,128)(2,1)S(1)}, bf16[104,2048]{1,0:T(8,128)(2,1)S(1)}, u32[]{:S(2)}, u32[]{:S(2)}) %collective-permute-start.21) | collective-permute-done | bytes 426016 | tf_op jit(solution)/shard_map/ppermute | solution.py:278
  155.7 1.3 collective-permute-start.54
  157.5 1.1 collective-permute-start.65
  158.6 10.0 %collective-permute-done.56.refs_12_ = bf16[256,1024]{1,0:T(8,128)(2,1)S(1)} collective-permute-done((bf16[256,1024]{1,0:T(8,128)(2,1)S(1)}, bf16[256,1024]{1,0:T(8,128)(2,1)S(1)}, u32[]{:S(2)}, u32[]{:S(2)}) %collective-permute-start.56) | collective-permute-done | bytes 524320 | tf_op jit(solution)/shard_map/ppermute | solution.py:275
  170.1 5.8 %expert.6 = (bf16[208,1408]{1,0:T(8,128)(2,1)S(1)}, bf16[208,704]{1,0:T(8,128)(2,1)S(1)}, bf16[208,2048]{1,0:T(8,128)(2,1)S(1)}, bf16[104,2048]{1,0:T(8,128)(2,1)S(1)}, bf16[104,2048]{1,0:T(8,128)(2,1)S(1)}) custom-call(s32[4]{0:T(128)S(1)} %pad_add_fusion.sc, bf16[2,2,2,12,128]{4,3,2,1,0:T(8,128)(2,1)S(1)} %collective-permute-done.24.meta.refs_2_, ...), custom_call_target="tpu_custom_call" | custom-call | flops 2617245696 | bytes 16000000 | tf_op jit(solution)/shard_map/expert/pallas_call | solution.py:334
  177.5 1.3 collective-permute-start.33
  178.8 3.5 %collective-permute-start.60 = (bf16[256,1024]{1,0:T(8,128)(2,1)S(1)}, bf16[256,1024]{1,0:T(8,128)(2,1)S(1)}, u32[]{:S(2)}, u32[]{:S(2)}) collective-permute-start(bf16[256,1024]{1,0:T(8,128)(2,1)S(1)} %collective-permute-done.56.refs_12_), channel_id=1, source_target_pairs={{0,4},{1,5},{2,6},{3,7},{4,8},{5,9},{6,10},{7,11},{8,12},{9,13},{1... | collective-permute-start | bytes 1572872 | tf_op jit(solution)/shard_map/ppermute | solution.py:275
  183.9 6.2 %collective-permute-done.33.r10 = bf16[104,2048]{1,0:T(8,128)(2,1)S(1)} collective-permute-done((bf16[104,2048]{1,0:T(8,128)(2,1)S(1)}, bf16[104,2048]{1,0:T(8,128)(2,1)S(1)}, u32[]{:S(2)}, u32[]{:S(2)}) %collective-permute-start.33) | collective-permute-done | bytes 426016 | tf_op jit(solution)/shard_map/ppermute | solution.py:278
  190.6 5.8 %expert.7 = (bf16[208,1408]{1,0:T(8,128)(2,1)S(1)}, bf16[208,704]{1,0:T(8,128)(2,1)S(1)}, bf16[208,2048]{1,0:T(8,128)(2,1)S(1)}, bf16[104,2048]{1,0:T(8,128)(2,1)S(1)}, bf16[104,2048]{1,0:T(8,128)(2,1)S(1)}) custom-call(s32[4]{0:T(128)S(1)} %pad_add_fusion.sc, bf16[2,2,2,12,128]{4,3,2,1,0:T(8,128)(2,1)S(1)} %collective-permute-done.36.meta.refs_3_, ...), custom_call_target="tpu_custom_call" | custom-call | flops 2617245696 | bytes 16000000 | tf_op jit(solution)/shard_map/expert/pallas_call | solution.py:334
  196.5 1.3 collective-permute-start.45
  199.7 1.6 collective-permute-done.58.refs_14_
  201.4 1.3 collective-permute-start.62
  204.8 5.7 %collective-permute-done.45.r10 = bf16[104,2048]{1,0:T(8,128)(2,1)S(1)} collective-permute-done((bf16[104,2048]{1,0:T(8,128)(2,1)S(1)}, bf16[104,2048]{1,0:T(8,128)(2,1)S(1)}, u32[]{:S(2)}, u32[]{:S(2)}) %collective-permute-start.45) | collective-permute-done | bytes 426016 | tf_op jit(solution)/shard_map/ppermute | solution.py:278
  210.5 2.3 collective-permute-done.66.refs_25_
  217.6 3.5 %collective-permute-done.62.refs_18_ = bf16[256,1024]{1,0:T(8,128)(2,1)S(1)} collective-permute-done((bf16[256,1024]{1,0:T(8,128)(2,1)S(1)}, bf16[256,1024]{1,0:T(8,128)(2,1)S(1)}, u32[]{:S(2)}, u32[]{:S(2)}) %collective-permute-start.62) | collective-permute-done | bytes 524320 | tf_op jit(solution)/shard_map/ppermute | solution.py:278
  221.2 1.1 copy-done.43
  223.3 6.3 %outer.1 = (f32[704,1024]{1,0:T(8,128)S(1)}, bf16[1,704,1024]{2,1,0:T(8,128)(2,1)S(1)}) custom-call(s32[4]{0:T(128)S(1)} %pad_add_fusion.sc, bf16[208,704]{1,0:T(8,128)(2,1)S(1)} %copy-done.41, bf16[208,704]{1,0:T(8,128)(2,1)S(1)} %copy-done.43, bf16[208,704]{1,0:T(8,128)(2,1)S(1)} %copy-done.45, bf16[208,704]{1,0:T(8,128)(2,1)S(1)} %get-tuple-element.63.refs_3_, ...), custom_call_target="tpu_custom_call" | custom-call | flops 2399141888 | bytes 10000000 | tf_op jit(solution)/shard_map/outer/pallas_call | solution.py:374
  229.6 2.0 collective-permute-start.68
  231.7 1.8 combine.5
  233.5 1.8 combine.6
  235.4 1.8 combine.7
  237.2 3.2 %collective-permute-start.23 = (bf16[128,2048]{1,0:T(8,128)(2,1)S(1)}, bf16[128,2048]{1,0:T(8,128)(2,1)S(1)}, u32[]{:S(2)}, u32[]{:S(2)}) collective-permute-start(bf16[128,2048]{1,0:T(8,128)(2,1)S(1)} %combine.5), channel_id=1, source_target_pairs={{0,12},{1,13},{2,14},{3,15},{4,0},{5,1},{6,2},{7,3},{8,4},{9,5},{1... | collective-permute-start | bytes 1572872 | tf_op jit(solution)/shard_map/ppermute | solution.py:275
  240.4 1.5 collective-permute-start.35
  241.9 1.7 collective-permute-start.47
  243.6 1.8 combine.4
  248.4 13.6 %inner.1 = (bf16[704,1024]{1,0:T(8,128)(2,1)}, bf16[704,1024]{1,0:T(8,128)(2,1)}) custom-call(s32[4]{0:T(128)S(1)} %pad_add_fusion.sc, bf16[2,2,2,12,128]{4,3,2,1,0:T(8,128)(2,1)S(1)} %pad_maximum_fusion.1.meta.refs_0_, bf16[2,2,2,12,128]{4,3,2,1,0:T(8,128)(2,1)S(1)} %collective-permute-done.12.meta.refs_1_, ...), custom_call_target="tpu_custom_call" | custom-call | flops 4798283776 | bytes 20000000 | tf_op jit(solution)/shard_map/inner/pallas_call | solution.py:405
  262.0 13.5 %collective-permute-done.35 = bf16[128,2048]{1,0:T(8,128)(2,1)S(1)} collective-permute-done((bf16[128,2048]{1,0:T(8,128)(2,1)S(1)}, bf16[128,2048]{1,0:T(8,128)(2,1)S(1)}, u32[]{:S(2)}, u32[]{:S(2)}) %collective-permute-start.35) | collective-permute-done | bytes 524320 | tf_op jit(solution)/shard_map/ppermute | solution.py:275
  275.5 11.1 %collective-permute-done.47 = bf16[128,2048]{1,0:T(8,128)(2,1)S(1)} collective-permute-done((bf16[128,2048]{1,0:T(8,128)(2,1)S(1)}, bf16[128,2048]{1,0:T(8,128)(2,1)S(1)}, u32[]{:S(2)}, u32[]{:S(2)}) %collective-permute-start.47) | collective-permute-done | bytes 524320 | tf_op jit(solution)/shard_map/ppermute | solution.py:275
  286.7 1.1 add_convert_fusion.1
  287.8 1.6 fusion
  (187 shorter events, 30.8 us)
Async XLA Ops:
  0.6 40.4 %collective-permute-start.6 = (bf16[6,704,128]{2,1,0:T(8,128)(2,1)}, bf16[6,704,128]{2,1,0:T(8,128)(2,1)S(1)}, u32[]{:S(2)}, u32[]{:S(2)}) collective-permute-start(bf16[6,704,128]{2,1,0:T(8,128)(2,1)} %bitcast.48), channel_id=1, source_target_pairs={{0,1},{1,0},{2,3},{3,2},{4,5},{5,4},{6,7},{7,6},{8,9},{9,8},{10,11... | collective-permute-start | bytes 3244040 | tf_op jit(solution)/shard_map/ppermute | solution.py:281
  0.7 41.9 %collective-permute-start.7 = (bf16[6,704,128]{2,1,0:T(8,128)(2,1)}, bf16[6,704,128]{2,1,0:T(8,128)(2,1)}, u32[]{:S(2)}, u32[]{:S(2)}) collective-permute-start(bf16[6,704,128]{2,1,0:T(8,128)(2,1)} %bitcast.50), channel_id=1, source_target_pairs={{0,1},{1,0},{2,3},{3,2},{4,5},{5,4},{6,7},{7,6},{8,9},{9,8},{10,11... | collective-permute-start | bytes 3244040 | tf_op jit(solution)/shard_map/ppermute | solution.py:281
  9.9 30.1 %collective-permute-start.4 = (bf16[128,2048]{1,0:T(8,128)(2,1)}, bf16[128,2048]{1,0:T(8,128)(2,1)S(1)}, u32[]{:S(2)}, u32[]{:S(2)}) collective-permute-start(bf16[128,2048]{1,0:T(8,128)(2,1)} %d00.1), channel_id=1, source_target_pairs={{0,2},{1,3},{2,0},{3,1},{4,6},{5,7},{6,4},{7,5},{8,10},{9,11},{10,... | collective-permute-start | bytes 1572872 | tf_op jit(solution)/shard_map/ppermute | solution.py:278
  10.4 30.1 %collective-permute-start.13 = (bf16[128,2048]{1,0:T(8,128)(2,1)}, bf16[128,2048]{1,0:T(8,128)(2,1)S(1)}, u32[]{:S(2)}, u32[]{:S(2)}) collective-permute-start(bf16[128,2048]{1,0:T(8,128)(2,1)} %d00.1), channel_id=1, source_target_pairs={{0,4},{1,5},{2,6},{3,7},{4,8},{5,9},{6,10},{7,11},{8,12},{9,13},{1... | collective-permute-start | bytes 1572872 | tf_op jit(solution)/shard_map/ppermute | solution.py:275
  12.1 12.7 %collective-permute-start.36 = (bf16[2,2,2,12,128]{4,3,2,1,0:T(8,128)(2,1)S(1)}, bf16[2,2,2,12,128]{4,3,2,1,0:T(8,128)(2,1)S(1)}, u32[]{:S(2)}, u32[]{:S(2)}) collective-permute-start(bf16[2,2,2,12,128]{4,3,2,1,0:T(8,128)(2,1)S(1)} %pad_maximum_fusion.1.meta.refs_0_), channel_id=1, source_target_pairs={{0,12},{1,13},{2,14},{3,15},{4,0},{5,1},{6,2},{7,3},{8,4},{9,5},{1... | collective-permute-start | bytes 73736 | tf_op jit(solution)/shard_map/ppermute | solution.py:275
  24.8 4.9 %collective-permute-start.24 = (bf16[2,2,2,12,128]{4,3,2,1,0:T(8,128)(2,1)S(1)}, bf16[2,2,2,12,128]{4,3,2,1,0:T(8,128)(2,1)S(1)}, u32[]{:S(2)}, u32[]{:S(2)}) collective-permute-start(bf16[2,2,2,12,128]{4,3,2,1,0:T(8,128)(2,1)S(1)} %pad_maximum_fusion.1.meta.refs_0_), channel_id=1, source_target_pairs={{0,8},{1,9},{2,10},{3,11},{4,12},{5,13},{6,14},{7,15},{8,0},{9,1},... | collective-permute-start | bytes 73736 | tf_op jit(solution)/shard_map/ppermute | solution.py:275
  33.6 6.4 %collective-permute-start.48 = (bf16[128,1024]{1,0:T(8,128)(2,1)S(1)}, bf16[128,1024]{1,0:T(8,128)(2,1)S(1)}, u32[]{:S(2)}, u32[]{:S(2)}) collective-permute-start(bf16[128,1024]{1,0:T(8,128)(2,1)S(1)} %get-tuple-element.71), channel_id=1, source_target_pairs={{0,16},{16,0},{1,17},{17,1},{2,18},{18,2},{3,19},{19,3},{4,20},{20... | collective-permute-start | bytes 786440 | tf_op jit(solution)/shard_map/ppermute | solution.py:284
  39.9 13.7 %collective-permute-start.3 = (bf16[128,2048]{1,0:T(8,128)(2,1)}, bf16[128,2048]{1,0:T(8,128)(2,1)S(1)}, u32[]{:S(2)}, u32[]{:S(2)}) collective-permute-start(bf16[128,2048]{1,0:T(8,128)(2,1)} %d00.1), channel_id=1, source_target_pairs={{0,1},{1,0},{2,3},{3,2},{4,5},{5,4},{6,7},{7,6},{8,9},{9,8},{10,11... | collective-permute-start | bytes 1572872 | tf_op jit(solution)/shard_map/ppermute | solution.py:281
  40.0 14.3 %collective-permute-start.5 = (bf16[128,2048]{1,0:T(8,128)(2,1)S(1)}, bf16[128,2048]{1,0:T(8,128)(2,1)S(1)}, u32[]{:S(2)}, u32[]{:S(2)}) collective-permute-start(bf16[128,2048]{1,0:T(8,128)(2,1)S(1)} %collective-permute-done.4.d10), channel_id=1, source_target_pairs={{0,1},{1,0},{2,3},{3,2},{4,5},{5,4},{6,7},{7,6},{8,9},{9,8},{10,11... | collective-permute-start | bytes 1572872 | tf_op jit(solution)/shard_map/ppermute | solution.py:281
  40.5 15.6 %collective-permute-start.25 = (bf16[128,2048]{1,0:T(8,128)(2,1)S(1)}, bf16[128,2048]{1,0:T(8,128)(2,1)S(1)}, u32[]{:S(2)}, u32[]{:S(2)}) collective-permute-start(bf16[128,2048]{1,0:T(8,128)(2,1)S(1)} %collective-permute-done.13.d00), channel_id=1, source_target_pairs={{0,4},{1,5},{2,6},{3,7},{4,8},{5,9},{6,10},{7,11},{8,12},{9,13},{1... | collective-permute-start | bytes 1572872 | tf_op jit(solution)/shard_map/ppermute | solution.py:275
  41.0 16.5 %collective-permute-start.15 = (bf16[128,2048]{1,0:T(8,128)(2,1)S(1)}, bf16[128,2048]{1,0:T(8,128)(2,1)S(1)}, u32[]{:S(2)}, u32[]{:S(2)}) collective-permute-start(bf16[128,2048]{1,0:T(8,128)(2,1)S(1)} %collective-permute-done.13.d00), channel_id=1, source_target_pairs={{0,2},{1,3},{2,0},{3,1},{4,6},{5,7},{6,4},{7,5},{8,10},{9,11},{10,... | collective-permute-start | bytes 1572872 | tf_op jit(solution)/shard_map/ppermute | solution.py:278
  42.6 17.1 %collective-permute-start.14 = (bf16[128,2048]{1,0:T(8,128)(2,1)S(1)}, bf16[128,2048]{1,0:T(8,128)(2,1)S(1)}, u32[]{:S(2)}, u32[]{:S(2)}) collective-permute-start(bf16[128,2048]{1,0:T(8,128)(2,1)S(1)} %collective-permute-done.13.d00), channel_id=1, source_target_pairs={{0,1},{1,0},{2,3},{3,2},{4,5},{5,4},{6,7},{7,6},{8,9},{9,8},{10,11... | collective-permute-start | bytes 1572872 | tf_op jit(solution)/shard_map/ppermute | solution.py:281
  53.7 9.8 %collective-permute-start.8 = (bf16[104,1408]{1,0:T(8,128)(2,1)S(1)}, bf16[104,1408]{1,0:T(8,128)(2,1)S(1)}, u32[]{:S(2)}, u32[]{:S(2)}) collective-permute-start(bf16[104,1408]{1,0:T(8,128)(2,1)S(1)} %get-tuple-element.38), channel_id=1, source_target_pairs={{0,2},{1,3},{2,0},{3,1},{4,6},{5,7},{6,4},{7,5},{8,10},{9,11},{10,... | collective-permute-start | bytes 878600 | tf_op jit(solution)/shard_map/ppermute | solution.py:278
  54.3 21.5 %collective-permute-start.17 = (bf16[104,1408]{1,0:T(8,128)(2,1)S(1)}, bf16[104,1408]{1,0:T(8,128)(2,1)S(1)}, u32[]{:S(2)}, u32[]{:S(2)}) collective-permute-start(bf16[104,1408]{1,0:T(8,128)(2,1)S(1)} %get-tuple-element.41), channel_id=1, source_target_pairs={{0,4},{1,5},{2,6},{3,7},{4,8},{5,9},{6,10},{7,11},{8,12},{9,13},{1... | collective-permute-start | bytes 878600 | tf_op jit(solution)/shard_map/ppermute | solution.py:275
  56.1 22.4 %collective-permute-start.18 = (bf16[104,1408]{1,0:T(8,128)(2,1)S(1)}, bf16[104,1408]{1,0:T(8,128)(2,1)S(1)}, u32[]{:S(2)}, u32[]{:S(2)}) collective-permute-start(bf16[104,1408]{1,0:T(8,128)(2,1)S(1)} %get-tuple-element.42), channel_id=1, source_target_pairs={{0,2},{1,3},{2,0},{3,1},{4,6},{5,7},{6,4},{7,5},{8,10},{9,11},{10,... | collective-permute-start | bytes 878600 | tf_op jit(solution)/shard_map/ppermute | solution.py:278
  57.6 24.7 %collective-permute-start.29 = (bf16[104,1408]{1,0:T(8,128)(2,1)S(1)}, bf16[104,1408]{1,0:T(8,128)(2,1)S(1)}, u32[]{:S(2)}, u32[]{:S(2)}) collective-permute-start(bf16[104,1408]{1,0:T(8,128)(2,1)S(1)} %get-tuple-element.45), channel_id=1, source_target_pairs={{0,8},{1,9},{2,10},{3,11},{4,12},{5,13},{6,14},{7,15},{8,0},{9,1},... | collective-permute-start | bytes 878600 | tf_op jit(solution)/shard_map/ppermute | solution.py:275
  59.7 24.1 %collective-permute-start.30 = (bf16[104,1408]{1,0:T(8,128)(2,1)S(1)}, bf16[104,1408]{1,0:T(8,128)(2,1)S(1)}, u32[]{:S(2)}, u32[]{:S(2)}) collective-permute-start(bf16[104,1408]{1,0:T(8,128)(2,1)S(1)} %get-tuple-element.46), channel_id=1, source_target_pairs={{0,2},{1,3},{2,0},{3,1},{4,6},{5,7},{6,4},{7,5},{8,10},{9,11},{10,... | collective-permute-start | bytes 878600 | tf_op jit(solution)/shard_map/ppermute | solution.py:278
  63.5 32.0 %collective-permute-start.41 = (bf16[104,1408]{1,0:T(8,128)(2,1)S(1)}, bf16[104,1408]{1,0:T(8,128)(2,1)S(1)}, u32[]{:S(2)}, u32[]{:S(2)}) collective-permute-start(bf16[104,1408]{1,0:T(8,128)(2,1)S(1)} %get-tuple-element.49), channel_id=1, source_target_pairs={{0,12},{1,13},{2,14},{3,15},{4,0},{5,1},{6,2},{7,3},{8,4},{9,5},{1... | collective-permute-start | bytes 878600 | tf_op jit(solution)/shard_map/ppermute | solution.py:275
  75.7 19.9 %collective-permute-start.37 = (bf16[128,2048]{1,0:T(8,128)(2,1)S(1)}, bf16[128,2048]{1,0:T(8,128)(2,1)S(1)}, u32[]{:S(2)}, u32[]{:S(2)}) collective-permute-start(bf16[128,2048]{1,0:T(8,128)(2,1)S(1)} %collective-permute-done.25.d00), channel_id=1, source_target_pairs={{0,4},{1,5},{2,6},{3,7},{4,8},{5,9},{6,10},{7,11},{8,12},{9,13},{1... | collective-permute-start | bytes 1572872 | tf_op jit(solution)/shard_map/ppermute | solution.py:275
  78.4 18.5 %collective-permute-start.27 = (bf16[128,2048]{1,0:T(8,128)(2,1)S(1)}, bf16[128,2048]{1,0:T(8,128)(2,1)S(1)}, u32[]{:S(2)}, u32[]{:S(2)}) collective-permute-start(bf16[128,2048]{1,0:T(8,128)(2,1)S(1)} %collective-permute-done.25.d00), channel_id=1, source_target_pairs={{0,2},{1,3},{2,0},{3,1},{4,6},{5,7},{6,4},{7,5},{8,10},{9,11},{10,... | collective-permute-start | bytes 1572872 | tf_op jit(solution)/shard_map/ppermute | solution.py:278
  82.2 13.3 %collective-permute-start.42 = (bf16[104,1408]{1,0:T(8,128)(2,1)S(1)}, bf16[104,1408]{1,0:T(8,128)(2,1)S(1)}, u32[]{:S(2)}, u32[]{:S(2)}) collective-permute-start(bf16[104,1408]{1,0:T(8,128)(2,1)S(1)} %get-tuple-element.50), channel_id=1, source_target_pairs={{0,2},{1,3},{2,0},{3,1},{4,6},{5,7},{6,4},{7,5},{8,10},{9,11},{10,... | collective-permute-start | bytes 878600 | tf_op jit(solution)/shard_map/ppermute | solution.py:278
  83.7 13.5 %collective-permute-start.26 = (bf16[128,2048]{1,0:T(8,128)(2,1)S(1)}, bf16[128,2048]{1,0:T(8,128)(2,1)S(1)}, u32[]{:S(2)}, u32[]{:S(2)}) collective-permute-start(bf16[128,2048]{1,0:T(8,128)(2,1)S(1)} %collective-permute-done.25.d00), channel_id=1, source_target_pairs={{0,1},{1,0},{2,3},{3,2},{4,5},{5,4},{6,7},{7,6},{8,9},{9,8},{10,11... | collective-permute-start | bytes 1572872 | tf_op jit(solution)/shard_map/ppermute | solution.py:281
  95.6 14.8 %collective-permute-start.52 = (bf16[256,1024]{1,0:T(8,128)(2,1)S(1)}, bf16[256,1024]{1,0:T(8,128)(2,1)S(1)}, u32[]{:S(2)}, u32[]{:S(2)}) collective-permute-start(bf16[256,1024]{1,0:T(8,128)(2,1)S(1)} %pad_maximum_fusion.refs_4_), channel_id=1, source_target_pairs={{0,4},{1,5},{2,6},{3,7},{4,8},{5,9},{6,10},{7,11},{8,12},{9,13},{1... | collective-permute-start | bytes 1572872 | tf_op jit(solution)/shard_map/ppermute | solution.py:275
  95.6 16.0 %collective-permute-start.50 = (bf16[256,1024]{1,0:T(8,128)(2,1)S(1)}, bf16[256,1024]{1,0:T(8,128)(2,1)S(1)}, u32[]{:S(2)}, u32[]{:S(2)}) collective-permute-start(bf16[256,1024]{1,0:T(8,128)(2,1)S(1)} %pad_maximum_fusion.refs_4_), channel_id=1, source_target_pairs={{0,2},{1,3},{2,0},{3,1},{4,6},{5,7},{6,4},{7,5},{8,10},{9,11},{10,... | collective-permute-start | bytes 1572872 | tf_op jit(solution)/shard_map/ppermute | solution.py:278
  97.0 15.0 %collective-permute-start.49 = (bf16[256,1024]{1,0:T(8,128)(2,1)S(1)}, bf16[256,1024]{1,0:T(8,128)(2,1)S(1)}, u32[]{:S(2)}, u32[]{:S(2)}) collective-permute-start(bf16[256,1024]{1,0:T(8,128)(2,1)S(1)} %pad_maximum_fusion.refs_4_), channel_id=1, source_target_pairs={{0,1},{1,0},{2,3},{3,2},{4,5},{5,4},{6,7},{7,6},{8,9},{9,8},{10,11... | collective-permute-start | bytes 1572872 | tf_op jit(solution)/shard_map/ppermute | solution.py:281
  97.2 19.4 %collective-permute-start.19 = (bf16[104,1408]{1,0:T(8,128)(2,1)S(1)}, bf16[104,1408]{1,0:T(8,128)(2,1)S(1)}, u32[]{:S(2)}, u32[]{:S(2)}) collective-permute-start(bf16[104,1408]{1,0:T(8,128)(2,1)S(1)} %collective-permute-done.18), channel_id=1, source_target_pairs={{0,4},{1,5},{2,6},{3,7},{4,8},{5,9},{6,10},{7,11},{8,12},{9,13},{1... | collective-permute-start | bytes 878600 | tf_op jit(solution)/shard_map/ppermute | solution.py:275
  98.1 34.7 %collective-permute-start.31 = (bf16[104,1408]{1,0:T(8,128)(2,1)S(1)}, bf16[104,1408]{1,0:T(8,128)(2,1)S(1)}, u32[]{:S(2)}, u32[]{:S(2)}) collective-permute-start(bf16[104,1408]{1,0:T(8,128)(2,1)S(1)} %collective-permute-done.30), channel_id=1, source_target_pairs={{0,8},{1,9},{2,10},{3,11},{4,12},{5,13},{6,14},{7,15},{8,0},{9,1},... | collective-permute-start | bytes 878600 | tf_op jit(solution)/shard_map/ppermute | solution.py:275
  110.3 31.1 %collective-permute-start.10 = (bf16[104,2048]{1,0:T(8,128)(2,1)S(1)}, bf16[104,2048]{1,0:T(8,128)(2,1)S(1)}, u32[]{:S(2)}, u32[]{:S(2)}) collective-permute-start(bf16[104,2048]{1,0:T(8,128)(2,1)S(1)} %get-tuple-element.40), channel_id=1, source_target_pairs={{0,2},{1,3},{2,0},{3,1},{4,6},{5,7},{6,4},{7,5},{8,10},{9,11},{10,... | collective-permute-start | bytes 1277960 | tf_op jit(solution)/shard_map/ppermute | solution.py:278
  111.6 29.1 %collective-permute-start.43 = (bf16[104,1408]{1,0:T(8,128)(2,1)S(1)}, bf16[104,1408]{1,0:T(8,128)(2,1)S(1)}, u32[]{:S(2)}, u32[]{:S(2)}) collective-permute-start(bf16[104,1408]{1,0:T(8,128)(2,1)S(1)} %collective-permute-done.42), channel_id=1, source_target_pairs={{0,12},{1,13},{2,14},{3,15},{4,0},{5,1},{6,2},{7,3},{8,4},{9,5},{1... | collective-permute-start | bytes 878600 | tf_op jit(solution)/shard_map/ppermute | solution.py:275
  111.9 29.5 %collective-permute-start.9 = (bf16[104,2048]{1,0:T(8,128)(2,1)S(1)}, bf16[104,2048]{1,0:T(8,128)(2,1)S(1)}, u32[]{:S(2)}, u32[]{:S(2)}) collective-permute-start(bf16[104,2048]{1,0:T(8,128)(2,1)S(1)} %get-tuple-element.39.r00), channel_id=1, source_target_pairs={{0,1},{1,0},{2,3},{3,2},{4,5},{5,4},{6,7},{7,6},{8,9},{9,8},{10,11... | collective-permute-start | bytes 1277960 | tf_op jit(solution)/shard_map/ppermute | solution.py:281
  116.6 25.4 %collective-permute-start.64 = (bf16[208,1408]{1,0:T(8,128)(2,1)S(1)}, bf16[208,1408]{1,0:T(8,128)(2,1)S(1)}, u32[]{:S(2)}, u32[]{:S(2)}) collective-permute-start(bf16[208,1408]{1,0:T(8,128)(2,1)S(1)} %get-tuple-element.54.refs_20_), channel_id=1, source_target_pairs={{0,16},{16,0},{1,17},{17,1},{2,18},{18,2},{3,19},{19,3},{4,20},{20... | collective-permute-start | bytes 1757192 | tf_op jit(solution)/shard_map/ppermute | solution.py:284
  132.9 24.2 %collective-permute-start.39 = (bf16[128,2048]{1,0:T(8,128)(2,1)S(1)}, bf16[128,2048]{1,0:T(8,128)(2,1)S(1)}, u32[]{:S(2)}, u32[]{:S(2)}) collective-permute-start(bf16[128,2048]{1,0:T(8,128)(2,1)S(1)} %collective-permute-done.37.d00), channel_id=1, source_target_pairs={{0,2},{1,3},{2,0},{3,1},{4,6},{5,7},{6,4},{7,5},{8,10},{9,11},{10,... | collective-permute-start | bytes 1572872 | tf_op jit(solution)/shard_map/ppermute | solution.py:278
  140.7 15.0 %collective-permute-start.21 = (bf16[104,2048]{1,0:T(8,128)(2,1)S(1)}, bf16[104,2048]{1,0:T(8,128)(2,1)S(1)}, u32[]{:S(2)}, u32[]{:S(2)}) collective-permute-start(bf16[104,2048]{1,0:T(8,128)(2,1)S(1)} %get-tuple-element.44), channel_id=1, source_target_pairs={{0,2},{1,3},{2,0},{3,1},{4,6},{5,7},{6,4},{7,5},{8,10},{9,11},{10,... | collective-permute-start | bytes 1277960 | tf_op jit(solution)/shard_map/ppermute | solution.py:278
  141.4 14.3 %collective-permute-start.20 = (bf16[104,2048]{1,0:T(8,128)(2,1)S(1)}, bf16[104,2048]{1,0:T(8,128)(2,1)S(1)}, u32[]{:S(2)}, u32[]{:S(2)}) collective-permute-start(bf16[104,2048]{1,0:T(8,128)(2,1)S(1)} %get-tuple-element.43.r00), channel_id=1, source_target_pairs={{0,1},{1,0},{2,3},{3,2},{4,5},{5,4},{6,7},{7,6},{8,9},{9,8},{10,11... | collective-permute-start | bytes 1277960 | tf_op jit(solution)/shard_map/ppermute | solution.py:281
  141.5 15.6 %collective-permute-start.38 = (bf16[128,2048]{1,0:T(8,128)(2,1)S(1)}, bf16[128,2048]{1,0:T(8,128)(2,1)S(1)}, u32[]{:S(2)}, u32[]{:S(2)}) collective-permute-start(bf16[128,2048]{1,0:T(8,128)(2,1)S(1)} %collective-permute-done.37.d00), channel_id=1, source_target_pairs={{0,1},{1,0},{2,3},{3,2},{4,5},{5,4},{6,7},{7,6},{8,9},{9,8},{10,11... | collective-permute-start | bytes 1572872 | tf_op jit(solution)/shard_map/ppermute | solution.py:281
  142.0 15.6 %collective-permute-start.28 = (bf16[128,2048]{1,0:T(8,128)(2,1)S(1)}, bf16[128,2048]{1,0:T(8,128)(2,1)S(1)}, u32[]{:S(2)}, u32[]{:S(2)}) collective-permute-start(bf16[128,2048]{1,0:T(8,128)(2,1)S(1)} %collective-permute-done.27.d10), channel_id=1, source_target_pairs={{0,1},{1,0},{2,3},{3,2},{4,5},{5,4},{6,7},{7,6},{8,9},{9,8},{10,11... | collective-permute-start | bytes 1572872 | tf_op jit(solution)/shard_map/ppermute | solution.py:281
  155.7 12.9 %collective-permute-start.56 = (bf16[256,1024]{1,0:T(8,128)(2,1)S(1)}, bf16[256,1024]{1,0:T(8,128)(2,1)S(1)}, u32[]{:S(2)}, u32[]{:S(2)}) collective-permute-start(bf16[256,1024]{1,0:T(8,128)(2,1)S(1)} %collective-permute-done.52.refs_8_), channel_id=1, source_target_pairs={{0,4},{1,5},{2,6},{3,7},{4,8},{5,9},{6,10},{7,11},{8,12},{9,13},{1... | collective-permute-start | bytes 1572872 | tf_op jit(solution)/shard_map/ppermute | solution.py:275
  155.7 12.9 %collective-permute-start.54 = (bf16[256,1024]{1,0:T(8,128)(2,1)S(1)}, bf16[256,1024]{1,0:T(8,128)(2,1)S(1)}, u32[]{:S(2)}, u32[]{:S(2)}) collective-permute-start(bf16[256,1024]{1,0:T(8,128)(2,1)S(1)} %collective-permute-done.52.refs_8_), channel_id=1, source_target_pairs={{0,2},{1,3},{2,0},{3,1},{4,6},{5,7},{6,4},{7,5},{8,10},{9,11},{10,... | collective-permute-start | bytes 1572872 | tf_op jit(solution)/shard_map/ppermute | solution.py:278
  157.0 12.1 %collective-permute-start.53 = (bf16[256,1024]{1,0:T(8,128)(2,1)S(1)}, bf16[256,1024]{1,0:T(8,128)(2,1)S(1)}, u32[]{:S(2)}, u32[]{:S(2)}) collective-permute-start(bf16[256,1024]{1,0:T(8,128)(2,1)S(1)} %collective-permute-done.52.refs_8_), channel_id=1, source_target_pairs={{0,1},{1,0},{2,3},{3,2},{4,5},{5,4},{6,7},{7,6},{8,9},{9,8},{10,11... | collective-permute-start | bytes 1572872 | tf_op jit(solution)/shard_map/ppermute | solution.py:281
  157.0 19.7 %collective-permute-start.51 = (bf16[256,1024]{1,0:T(8,128)(2,1)S(1)}, bf16[256,1024]{1,0:T(8,128)(2,1)S(1)}, u32[]{:S(2)}, u32[]{:S(2)}) collective-permute-start(bf16[256,1024]{1,0:T(8,128)(2,1)S(1)} %collective-permute-done.50.refs_6_), channel_id=1, source_target_pairs={{0,1},{1,0},{2,3},{3,2},{4,5},{5,4},{6,7},{7,6},{8,9},{9,8},{10,11... | collective-permute-start | bytes 1572872 | tf_op jit(solution)/shard_map/ppermute | solution.py:281
  157.5 24.7 %collective-permute-start.65 = (bf16[208,1408]{1,0:T(8,128)(2,1)S(1)}, bf16[208,1408]{1,0:T(8,128)(2,1)S(1)}, u32[]{:S(2)}, u32[]{:S(2)}) collective-permute-start(bf16[208,1408]{1,0:T(8,128)(2,1)S(1)} %get-tuple-element.55.refs_22_), channel_id=1, source_target_pairs={{0,16},{16,0},{1,17},{17,1},{2,18},{18,2},{3,19},{19,3},{4,20},{20... | collective-permute-start | bytes 1757192 | tf_op jit(solution)/shard_map/ppermute | solution.py:284
  168.6 10.2 %collective-permute-start.11 = (bf16[104,2048]{1,0:T(8,128)(2,1)S(1)}, bf16[104,2048]{1,0:T(8,128)(2,1)S(1)}, u32[]{:S(2)}, u32[]{:S(2)}) collective-permute-start(bf16[104,2048]{1,0:T(8,128)(2,1)S(1)} %collective-permute-done.10.r10), channel_id=1, source_target_pairs={{0,1},{1,0},{2,3},{3,2},{4,5},{5,4},{6,7},{7,6},{8,9},{9,8},{10,11... | collective-permute-start | bytes 1277960 | tf_op jit(solution)/shard_map/ppermute | solution.py:281
  168.6 14.5 %collective-permute-start.22 = (bf16[104,2048]{1,0:T(8,128)(2,1)S(1)}, bf16[104,2048]{1,0:T(8,128)(2,1)S(1)}, u32[]{:S(2)}, u32[]{:S(2)}) collective-permute-start(bf16[104,2048]{1,0:T(8,128)(2,1)S(1)} %collective-permute-done.21.r10), channel_id=1, source_target_pairs={{0,1},{1,0},{2,3},{3,2},{4,5},{5,4},{6,7},{7,6},{8,9},{9,8},{10,11... | collective-permute-start | bytes 1277960 | tf_op jit(solution)/shard_map/ppermute | solution.py:281
  169.9 20.2 %collective-permute-start.40 = (bf16[128,2048]{1,0:T(8,128)(2,1)S(1)}, bf16[128,2048]{1,0:T(8,128)(2,1)S(1)}, u32[]{:S(2)}, u32[]{:S(2)}) collective-permute-start(bf16[128,2048]{1,0:T(8,128)(2,1)S(1)} %collective-permute-done.39.d10), channel_id=1, source_target_pairs={{0,1},{1,0},{2,3},{3,2},{4,5},{5,4},{6,7},{7,6},{8,9},{9,8},{10,11... | collective-permute-start | bytes 1572872 | tf_op jit(solution)/shard_map/ppermute | solution.py:281
  177.5 12.6 %collective-permute-start.33 = (bf16[104,2048]{1,0:T(8,128)(2,1)S(1)}, bf16[104,2048]{1,0:T(8,128)(2,1)S(1)}, u32[]{:S(2)}, u32[]{:S(2)}) collective-permute-start(bf16[104,2048]{1,0:T(8,128)(2,1)S(1)} %get-tuple-element.48), channel_id=1, source_target_pairs={{0,2},{1,3},{2,0},{3,1},{4,6},{5,7},{6,4},{7,5},{8,10},{9,11},{10,... | collective-permute-start | bytes 1277960 | tf_op jit(solution)/shard_map/ppermute | solution.py:278
  178.8 19.1 %collective-permute-start.60 = (bf16[256,1024]{1,0:T(8,128)(2,1)S(1)}, bf16[256,1024]{1,0:T(8,128)(2,1)S(1)}, u32[]{:S(2)}, u32[]{:S(2)}) collective-permute-start(bf16[256,1024]{1,0:T(8,128)(2,1)S(1)} %collective-permute-done.56.refs_12_), channel_id=1, source_target_pairs={{0,4},{1,5},{2,6},{3,7},{4,8},{5,9},{6,10},{7,11},{8,12},{9,13},{1... | collective-permute-start | bytes 1572872 | tf_op jit(solution)/shard_map/ppermute | solution.py:275
  183.1 13.4 %collective-permute-start.32 = (bf16[104,2048]{1,0:T(8,128)(2,1)S(1)}, bf16[104,2048]{1,0:T(8,128)(2,1)S(1)}, u32[]{:S(2)}, u32[]{:S(2)}) collective-permute-start(bf16[104,2048]{1,0:T(8,128)(2,1)S(1)} %get-tuple-element.47.r00), channel_id=1, source_target_pairs={{0,1},{1,0},{2,3},{3,2},{4,5},{5,4},{6,7},{7,6},{8,9},{9,8},{10,11... | collective-permute-start | bytes 1277960 | tf_op jit(solution)/shard_map/ppermute | solution.py:281
  183.1 18.3 %collective-permute-start.58 = (bf16[256,1024]{1,0:T(8,128)(2,1)S(1)}, bf16[256,1024]{1,0:T(8,128)(2,1)S(1)}, u32[]{:S(2)}, u32[]{:S(2)}) collective-permute-start(bf16[256,1024]{1,0:T(8,128)(2,1)S(1)} %collective-permute-done.56.refs_12_), channel_id=1, source_target_pairs={{0,2},{1,3},{2,0},{3,1},{4,6},{5,7},{6,4},{7,5},{8,10},{9,11},{10,... | collective-permute-start | bytes 1572872 | tf_op jit(solution)/shard_map/ppermute | solution.py:278
  190.1 12.5 %collective-permute-start.57 = (bf16[256,1024]{1,0:T(8,128)(2,1)S(1)}, bf16[256,1024]{1,0:T(8,128)(2,1)S(1)}, u32[]{:S(2)}, u32[]{:S(2)}) collective-permute-start(bf16[256,1024]{1,0:T(8,128)(2,1)S(1)} %collective-permute-done.56.refs_12_), channel_id=1, source_target_pairs={{0,1},{1,0},{2,3},{3,2},{4,5},{5,4},{6,7},{7,6},{8,9},{9,8},{10,11... | collective-permute-start | bytes 1572872 | tf_op jit(solution)/shard_map/ppermute | solution.py:281
  190.2 13.3 %collective-permute-start.55 = (bf16[256,1024]{1,0:T(8,128)(2,1)S(1)}, bf16[256,1024]{1,0:T(8,128)(2,1)S(1)}, u32[]{:S(2)}, u32[]{:S(2)}) collective-permute-start(bf16[256,1024]{1,0:T(8,128)(2,1)S(1)} %collective-permute-done.54.refs_10_), channel_id=1, source_target_pairs={{0,1},{1,0},{2,3},{3,2},{4,5},{5,4},{6,7},{7,6},{8,9},{9,8},{10,11... | collective-permute-start | bytes 1572872 | tf_op jit(solution)/shard_map/ppermute | solution.py:281
  196.5 14.0 %collective-permute-start.45 = (bf16[104,2048]{1,0:T(8,128)(2,1)S(1)}, bf16[104,2048]{1,0:T(8,128)(2,1)S(1)}, u32[]{:S(2)}, u32[]{:S(2)}) collective-permute-start(bf16[104,2048]{1,0:T(8,128)(2,1)S(1)} %get-tuple-element.52), channel_id=1, source_target_pairs={{0,2},{1,3},{2,0},{3,1},{4,6},{5,7},{6,4},{7,5},{8,10},{9,11},{10,... | collective-permute-start | bytes 1277960 | tf_op jit(solution)/shard_map/ppermute | solution.py:278
  197.8 14.9 %collective-permute-start.66 = (bf16[208,1408]{1,0:T(8,128)(2,1)S(1)}, bf16[208,1408]{1,0:T(8,128)(2,1)S(1)}, u32[]{:S(2)}, u32[]{:S(2)}) collective-permute-start(bf16[208,1408]{1,0:T(8,128)(2,1)S(1)} %get-tuple-element.56.refs_24_), channel_id=1, source_target_pairs={{0,16},{16,0},{1,17},{17,1},{2,18},{18,2},{3,19},{19,3},{4,20},{20... | collective-permute-start | bytes 1757192 | tf_op jit(solution)/shard_map/ppermute | solution.py:284
  201.4 19.8 %collective-permute-start.62 = (bf16[256,1024]{1,0:T(8,128)(2,1)S(1)}, bf16[256,1024]{1,0:T(8,128)(2,1)S(1)}, u32[]{:S(2)}, u32[]{:S(2)}) collective-permute-start(bf16[256,1024]{1,0:T(8,128)(2,1)S(1)} %collective-permute-done.60.refs_16_), channel_id=1, source_target_pairs={{0,2},{1,3},{2,0},{3,1},{4,6},{5,7},{6,4},{7,5},{8,10},{9,11},{10,... | collective-permute-start | bytes 1572872 | tf_op jit(solution)/shard_map/ppermute | solution.py:278
  203.5 12.0 %collective-permute-start.34 = (bf16[104,2048]{1,0:T(8,128)(2,1)S(1)}, bf16[104,2048]{1,0:T(8,128)(2,1)S(1)}, u32[]{:S(2)}, u32[]{:S(2)}) collective-permute-start(bf16[104,2048]{1,0:T(8,128)(2,1)S(1)} %collective-permute-done.33.r10), channel_id=1, source_target_pairs={{0,1},{1,0},{2,3},{3,2},{4,5},{5,4},{6,7},{7,6},{8,9},{9,8},{10,11... | collective-permute-start | bytes 1277960 | tf_op jit(solution)/shard_map/ppermute | solution.py:281
  204.3 12.1 %collective-permute-start.44 = (bf16[104,2048]{1,0:T(8,128)(2,1)S(1)}, bf16[104,2048]{1,0:T(8,128)(2,1)S(1)}, u32[]{:S(2)}, u32[]{:S(2)}) collective-permute-start(bf16[104,2048]{1,0:T(8,128)(2,1)S(1)} %get-tuple-element.51.r00), channel_id=1, source_target_pairs={{0,1},{1,0},{2,3},{3,2},{4,5},{5,4},{6,7},{7,6},{8,9},{9,8},{10,11... | collective-permute-start | bytes 1277960 | tf_op jit(solution)/shard_map/ppermute | solution.py:281
  210.5 19.1 %collective-permute-start.46 = (bf16[104,2048]{1,0:T(8,128)(2,1)S(1)}, bf16[104,2048]{1,0:T(8,128)(2,1)S(1)}, u32[]{:S(2)}, u32[]{:S(2)}) collective-permute-start(bf16[104,2048]{1,0:T(8,128)(2,1)S(1)} %collective-permute-done.45.r10), channel_id=1, source_target_pairs={{0,1},{1,0},{2,3},{3,2},{4,5},{5,4},{6,7},{7,6},{8,9},{9,8},{10,11... | collective-permute-start | bytes 1277960 | tf_op jit(solution)/shard_map/ppermute | solution.py:281
  213.6 28.3 %collective-permute-start.67 = (bf16[208,1408]{1,0:T(8,128)(2,1)S(1)}, bf16[208,1408]{1,0:T(8,128)(2,1)S(1)}, u32[]{:S(2)}, u32[]{:S(2)}) collective-permute-start(bf16[208,1408]{1,0:T(8,128)(2,1)S(1)} %get-tuple-element.57.refs_26_), channel_id=1, source_target_pairs={{0,16},{16,0},{1,17},{17,1},{2,18},{18,2},{3,19},{19,3},{4,20},{20... | collective-permute-start | bytes 1757192 | tf_op jit(solution)/shard_map/ppermute | solution.py:284
  215.5 21.7 %collective-permute-start.61 = (bf16[256,1024]{1,0:T(8,128)(2,1)S(1)}, bf16[256,1024]{1,0:T(8,128)(2,1)S(1)}, u32[]{:S(2)}, u32[]{:S(2)}) collective-permute-start(bf16[256,1024]{1,0:T(8,128)(2,1)S(1)} %collective-permute-done.60.refs_16_), channel_id=1, source_target_pairs={{0,1},{1,0},{2,3},{3,2},{4,5},{5,4},{6,7},{7,6},{8,9},{9,8},{10,11... | collective-permute-start | bytes 1572872 | tf_op jit(solution)/shard_map/ppermute | solution.py:281
  216.3 24.0 %collective-permute-start.59 = (bf16[256,1024]{1,0:T(8,128)(2,1)S(1)}, bf16[256,1024]{1,0:T(8,128)(2,1)S(1)}, u32[]{:S(2)}, u32[]{:S(2)}) collective-permute-start(bf16[256,1024]{1,0:T(8,128)(2,1)S(1)} %collective-permute-done.58.refs_14_), channel_id=1, source_target_pairs={{0,1},{1,0},{2,3},{3,2},{4,5},{5,4},{6,7},{7,6},{8,9},{9,8},{10,11... | collective-permute-start | bytes 1572872 | tf_op jit(solution)/shard_map/ppermute | solution.py:281
  221.2 24.2 %collective-permute-start.63 = (bf16[256,1024]{1,0:T(8,128)(2,1)S(1)}, bf16[256,1024]{1,0:T(8,128)(2,1)S(1)}, u32[]{:S(2)}, u32[]{:S(2)}) collective-permute-start(bf16[256,1024]{1,0:T(8,128)(2,1)S(1)} %collective-permute-done.62.refs_18_), channel_id=1, source_target_pairs={{0,1},{1,0},{2,3},{3,2},{4,5},{5,4},{6,7},{7,6},{8,9},{9,8},{10,11... | collective-permute-start | bytes 1572872 | tf_op jit(solution)/shard_map/ppermute | solution.py:281
  229.6 58.2 %collective-permute-start.68 = (bf16[704,1024]{1,0:T(8,128)(2,1)S(1)}, bf16[704,1024]{1,0:T(8,128)(2,1)S(1)}, u32[]{:S(2)}, u32[]{:S(2)}) collective-permute-start(bf16[704,1024]{1,0:T(8,128)(2,1)S(1)} %bitcast.47), channel_id=1, source_target_pairs={{0,16},{16,0},{1,17},{17,1},{2,18},{18,2},{3,19},{19,3},{4,20},{20... | collective-permute-start | bytes 4325384 | tf_op jit(solution)/shard_map/ppermute | solution.py:284
  237.2 24.8 %collective-permute-start.23 = (bf16[128,2048]{1,0:T(8,128)(2,1)S(1)}, bf16[128,2048]{1,0:T(8,128)(2,1)S(1)}, u32[]{:S(2)}, u32[]{:S(2)}) collective-permute-start(bf16[128,2048]{1,0:T(8,128)(2,1)S(1)} %combine.5), channel_id=1, source_target_pairs={{0,12},{1,13},{2,14},{3,15},{4,0},{5,1},{6,2},{7,3},{8,4},{9,5},{1... | collective-permute-start | bytes 1572872 | tf_op jit(solution)/shard_map/ppermute | solution.py:275
  240.4 35.2 %collective-permute-start.35 = (bf16[128,2048]{1,0:T(8,128)(2,1)S(1)}, bf16[128,2048]{1,0:T(8,128)(2,1)S(1)}, u32[]{:S(2)}, u32[]{:S(2)}) collective-permute-start(bf16[128,2048]{1,0:T(8,128)(2,1)S(1)} %combine.6), channel_id=1, source_target_pairs={{0,8},{1,9},{2,10},{3,11},{4,12},{5,13},{6,14},{7,15},{8,0},{9,1},... | collective-permute-start | bytes 1572872 | tf_op jit(solution)/shard_map/ppermute | solution.py:275
  241.9 44.8 %collective-permute-start.47 = (bf16[128,2048]{1,0:T(8,128)(2,1)S(1)}, bf16[128,2048]{1,0:T(8,128)(2,1)S(1)}, u32[]{:S(2)}, u32[]{:S(2)}) collective-permute-start(bf16[128,2048]{1,0:T(8,128)(2,1)S(1)} %combine.7), channel_id=1, source_target_pairs={{0,4},{1,5},{2,6},{3,7},{4,8},{5,9},{6,10},{7,11},{8,12},{9,13},{1... | collective-permute-start | bytes 1572872 | tf_op jit(solution)/shard_map/ppermute | solution.py:275
  (51 other events, 607.5 us)

commit v3 on v2

v3 whole, which is shorter than its diff:
```python
import functools

import jax
import jax.numpy as jnp
from jax import lax
from jax.experimental import pallas as pl
from jax.experimental.pallas import tpu as pltpu
from jax.sharding import PartitionSpec as P

BF16 = jnp.bfloat16
F32 = jnp.float32
MIB = 1024 * 1024
PACK, EXPERT, COMBINE, OUTER, INNER = 24, 40, 12, 24, 40
NT = (((1,), (1,)), ((), ()))
TN = (((0,), (0,)), ((), ()))


def params(mib):
    return pltpu.CompilerParams(vmem_limit_bytes=mib * MIB)


def cost(flops, moved):
    return pl.CostEstimate(flops=int(flops), bytes_accessed=int(moved), transcendentals=0)


def dot(a, b):
    return jnp.dot(a, b, preferred_element_type=F32)


def before_matrix(size):
    row = lax.broadcasted_iota(jnp.int32, (size, size), 0)
    col = lax.broadcasted_iota(jnp.int32, (size, size), 1)
    return jnp.where(row < col, 1.0, 0.0).astype(BF16)


def slot_rows(slot, count):
    row = lax.broadcasted_iota(jnp.int32, (count, slot.shape[1]), 0).astype(F32)
    return jnp.where(row == slot, 1.0, 0.0)


def moved(slot, by):
    return jnp.where(slot < 0, -1.0, slot + by)


def with_notes(rows, notes, slots, block):
    count, lanes = rows.shape[0], notes[0].shape[1]
    row = lax.rem(lax.broadcasted_iota(jnp.int32, (count, lanes), 0), block)
    spread = jnp.concatenate([jnp.broadcast_to(note, (block, lanes)) for note in notes], axis=0)
    return jnp.concatenate([jnp.where(row >= slots, spread, rows[:, :lanes]), rows[:, lanes:]], axis=1)


def pack_kernel(top, slots, block, sc, meta_ref, gate_pre, up_pre, keep, swap, cat, sem):
    ffw, tok = gate_pre.shape[1:]
    copies = []
    for part, src in enumerate((gate_pre, up_pre)):
        for k in range(top):
            copies.append(
                pltpu.make_async_copy(
                    src.at[k],
                    cat.at[pl.ds(part * ffw, ffw), pl.ds(k * tok, tok)],
                    sem.at[len(copies)],
                )
            )
    for copy in copies:
        copy.start()
    zn = keep.shape[0]
    experts = 4 * zn
    meta = meta_ref[...].astype(F32)
    order = lax.broadcasted_iota(jnp.int32, (experts, 1), 0)

    def turned(value, by):
        return lax.bitwise_xor(value, jnp.broadcast_to(by, value.shape))

    here = sc[0] * 4 + sc[1] * 2 + sc[2]
    across = jnp.where(order >= 2 * zn, 1, 0)
    expert = turned(lax.bitwise_and(order, 2 * zn - 1) * 2 + across, here).astype(F32)
    hits = [jnp.where(meta[k : k + 1] == expert, 1.0, 0.0) for k in range(top)]
    mask = sum(hits)
    slot = dot(mask.astype(BF16), before_matrix(tok))
    gates = sum(hits[k] * meta[top + k : top + k + 1] for k in range(top))
    notes = jnp.concatenate([jnp.where(mask > 0, slot, -1.0), gates], axis=1)
    place = slot + order.astype(F32) * block + 1.0
    target = jnp.concatenate(
        [jnp.sum(hits[k] * place, axis=0, keepdims=True) - 1.0 for k in range(top)], axis=1
    )
    for copy in copies:
        copy.wait()
    table = cat[...]
    lot = 4
    for first in range(0, experts, lot):
        pick = slot_rows(moved(target, -float(first * block)), lot * block).astype(BF16)
        packed = lax.dot_general(pick, table, NT, preferred_element_type=F32)
        packed = with_notes(packed, [notes[first + n : first + n + 1] for n in range(lot)], slots, block)
        for n in range(lot):
            at = (first + n) % (2 * zn)
            out = keep if first + n < 2 * zn else swap
            out[at // 2, at % 2] = packed[n * block : (n + 1) * block].astype(BF16)


def expert_kernel(
    slots, block, d00, d01, d10, d11, near, far, w_gate, w_up, w_down,
    grads_out, hidden_out, rows_out, keep_out, swap_out, hop_out, down_at, both_at, sem,
):
    ffw = w_down.shape[0]
    copies = [
        pltpu.make_async_copy(w_down, down_at.at[pl.ds(0, ffw)], sem.at[0]),
        pltpu.make_async_copy(w_down, down_at.at[pl.ds(ffw, ffw)], sem.at[1]),
        pltpu.make_async_copy(w_gate, both_at.at[pl.ds(0, ffw)], sem.at[2]),
        pltpu.make_async_copy(w_up, both_at.at[pl.ds(ffw, ffw)], sem.at[3]),
    ]
    for copy in copies:
        copy.start()
    tok = d00.shape[0]
    quad = 4 * block
    pre = jnp.concatenate([near[...].astype(F32), far[...].astype(F32)], axis=0)
    notes = [pre[n * block + slots : n * block + slots + 1, : 2 * tok] for n in range(4)]
    target = jnp.concatenate([moved(note[:, :tok], float(n * block)) for n, note in enumerate(notes)], axis=1)
    gates = jnp.concatenate([note[:, tok:] for note in notes], axis=1)
    pick = slot_rows(target, quad)
    weight = jnp.sum(pick * gates, axis=1, keepdims=True)
    table = jnp.concatenate([ref[...] for ref in (d00, d01, d10, d11)], axis=0)
    rows = dot(pick.astype(BF16), table).astype(BF16)
    rows_out[...] = rows
    copies[0].wait()
    copies[1].wait()
    back = lax.dot_general(rows, down_at[...], NT, preferred_element_type=F32)
    swapped = pltpu.roll(pre, ffw, axis=1)
    front = lax.broadcasted_iota(jnp.int32, pre.shape, 1) < ffw
    gate_pre = jnp.where(front, pre, swapped)
    up_pre = jnp.where(front, swapped, pre)
    sig = jax.nn.sigmoid(gate_pre)
    active = gate_pre * sig
    slope = jnp.where(front, up_pre * sig * (1.0 + gate_pre * (1.0 - sig)), active)
    grads = weight * back * slope
    hidden_out[...] = (weight * active * up_pre)[:, :ffw].astype(BF16)
    grads_out[...] = with_notes(grads, notes, slots, block).astype(BF16)
    copies[2].wait()
    copies[3].wait()
    route = with_notes(dot(grads.astype(BF16), both_at[...]), notes, slots, block).astype(BF16)
    keep_out[...] = route[:block]
    swap_out[...] = route[block : 2 * block]
    hop_out[...] = route[2 * block :]


def combine_kernel(slots, block, keep, swap, hop, hop_swap, out):
    tok = out.shape[0]
    total = jnp.zeros(out.shape, F32)
    for ref, start in ((keep, 0), (swap, 0), (hop, 0), (hop_swap, block)):
        rows = ref[...].astype(F32)
        slot = moved(rows[start + slots : start + slots + 1, :tok], float(start))
        pick = slot_rows(slot, rows.shape[0]).astype(BF16)
        total = total + lax.dot_general(pick, ref[...], TN, preferred_element_type=F32)
    out[...] = total.astype(BF16)


def inner_kernel(zn, ng, slots, block, *refs):
    n_x, n_g = 4 * zn, zn * ng
    xs, gs = refs[:n_x], refs[n_x : n_x + n_g]
    gate_out, up_out, table, grads, grads_t, rows, sem_x, sem_g = refs[n_x + n_g :]
    tok = xs[0].shape[0] // ng
    ffw, width = gate_out.shape
    quad = 4 * block
    units = n_g
    copies = []
    for u in range(units):
        j, r = u // ng, u % ng
        mine = [pltpu.make_async_copy(gs[u], grads.at[pl.ds(u * quad, quad)], sem_g.at[u])]
        for n in range(4):
            mine.append(
                pltpu.make_async_copy(
                    xs[4 * j + n].at[pl.ds(r * tok, tok)],
                    table.at[u, pl.ds(n * tok, tok)],
                    sem_x.at[4 * u + n],
                )
            )
        copies.append(mine)
        for copy in mine:
            copy.start()
    for u in range(units):
        for copy in copies[u]:
            copy.wait()
        targets = []
        for n in range(4):
            row = n * block + slots
            near = u * quad + row // 16 * 16
            note = grads[near : near + 16, :tok].astype(F32)[row % 16 : row % 16 + 1]
            targets.append(moved(note, float(n * block)))
        pick = slot_rows(jnp.concatenate(targets, axis=1), quad).astype(BF16)
        rows[u * quad : (u + 1) * quad, :] = dot(pick, table[u]).astype(BF16)
    total = units * quad
    step = 128
    for i in range(0, total, step):
        grads_t[:, i : i + step] = grads[i : i + step, :].T
    chunk = min(256, width)

    def product(n, carry):
        cols = pl.ds(pl.multiple_of(n * chunk, chunk), chunk)
        both = dot(grads_t[...], rows[:, cols])
        gate_out[:, cols] = both[:ffw].astype(BF16)
        up_out[:, cols] = both[ffw:].astype(BF16)
        return carry

    lax.fori_loop(0, width // chunk, product, 0)


def outer_kernel(zn, ng, sc, *refs):
    hs, ds = refs[:zn], refs[zn : 2 * zn]
    own, sent, hidden, rows, sem = refs[2 * zn :]
    quad = hs[0].shape[0]
    copies = []
    for j in range(zn):
        copies.append(pltpu.make_async_copy(hs[j], hidden.at[pl.ds(j * quad, quad)], sem.at[2 * j]))
        copies.append(pltpu.make_async_copy(ds[j], rows.at[pl.ds(j * quad, quad)], sem.at[2 * j + 1]))
    for copy in copies:
        copy.start()
    for copy in copies:
        copy.wait()
    g = sc[3]
    width = own.shape[1]
    chunk = min(256, width)
    hidden_t = hidden[...].T

    for r in range(ng):
        base = lax.rem(g + r, ng) * width

        def product(n, carry):
            cols = pl.ds(pl.multiple_of(base + n * chunk, chunk), chunk)
            value = dot(hidden_t, rows[:, cols])
            to = pl.ds(pl.multiple_of(n * chunk, chunk), chunk)
            if r == 0:
                own[:, to] = value
            else:
                sent[r - 1, :, to] = value.astype(BF16)
            return carry

        lax.fori_loop(0, width // chunk, product, 0)


def per_device(
    tokens, d_out, expert_ids, gate_values, saved_gate_pre, saved_up_pre, w_gate, w_up, w_down
):
    tok, width = tokens.shape
    top = expert_ids.shape[1]
    ffw = saved_gate_pre.shape[2]
    nb, ng = lax.axis_size("blk"), lax.axis_size("grp")
    zn = nb // 4
    experts = w_gate.shape[0] * nb
    slots = 13 * tok // (2 * experts)
    block = -(-(slots + 1) // 8) * 8
    quad = 4 * block
    part = width // ng
    me, g = lax.axis_index("blk"), lax.axis_index("grp")
    z, x, c = me // 4, (me // 2) % 2, me % 2
    sc = jnp.stack([z, x, c, g]).astype(jnp.int32)

    def over_z(value, n):
        return lax.ppermute(value, "blk", [(b, b ^ (4 * n)) for b in range(nb)])

    def along_z(value, pairs):
        return lax.ppermute(value, "blk", [(4 * a + n, 4 * b + n) for a, b in pairs for n in range(4)])

    def over_x(value):
        return lax.ppermute(value, "blk", [(b, b ^ 2) for b in range(nb)])

    def over_core(value):
        return lax.ppermute(value, "blk", [(b, b ^ 1) for b in range(nb)])

    def over_groups(value, n):
        return lax.ppermute(value, "grp", [(b, (b + n) % ng) for b in range(ng)])

    def after(value, *others):
        return lax.optimization_barrier((value,) + others)[0]

    inner_plane = (z == 1) | (z == 2)
    middle, outward = [(1, 2), (2, 1)], [(1, 0), (2, 3)]
    smem = pl.BlockSpec(memory_space=pltpu.SMEM)
    vmem = pl.BlockSpec(memory_space=pltpu.VMEM)
    anywhere = pl.BlockSpec(memory_space=pl.ANY)

    def shape(*dims, dtype=BF16):
        return jax.ShapeDtypeStruct(dims, dtype)

    meta = jnp.concatenate([expert_ids.T.astype(BF16), gate_values.T], axis=0)
    def together(*values):
        return lax.optimization_barrier(values)

    keep, swap = pl.pallas_call(
        functools.partial(pack_kernel, top, slots, block),
        out_shape=[shape(zn, 2, block, 2 * ffw)] * 2,
        in_specs=[smem, vmem, anywhere, anywhere],
        out_specs=[vmem] * 2,
        scratch_shapes=[
            pltpu.VMEM((2 * ffw, top * tok), BF16),
            pltpu.SemaphoreType.DMA((2 * top,)),
        ],
        compiler_params=params(PACK),
        cost_estimate=cost(4 * experts * block * top * tok * ffw, 4 * top * tok * ffw),
        name="pack",
    )(sc, meta, saved_gate_pre.transpose(1, 2, 0), saved_up_pre.transpose(1, 2, 0))
    other = over_core(swap)
    pairs = [jnp.concatenate([keep[j], other[j]], axis=1) for j in range(zn)]

    mixed = [lax.dynamic_slice(tokens, (0, g * part), (tok, part))]
    for r in range(1, ng):
        there = lax.dynamic_slice(tokens, (0, ((g + r) % ng) * part), (tok, part))
        mixed.append(over_groups(there, r))
    mixed = jnp.concatenate(mixed, axis=0)
    weights = (w_gate[0].T, w_up[0].T, w_down[0])

    def expert(table, near, far):
        return pl.pallas_call(
            functools.partial(expert_kernel, slots, block),
            out_shape=[
                shape(quad, 2 * ffw),
                shape(quad, ffw),
                shape(quad, width),
                shape(block, width),
                shape(block, width),
                shape(2 * block, width),
            ],
            in_specs=[vmem] * 6 + [anywhere] * 3,
            out_specs=[vmem] * 6,
            scratch_shapes=[
                pltpu.VMEM((2 * ffw, width), BF16),
                pltpu.VMEM((2 * ffw, width), BF16),
                pltpu.SemaphoreType.DMA((4,)),
            ],
            compiler_params=params(EXPERT),
            cost_estimate=cost(2 * quad * width * (ffw * 4 + 4 * tok), 16e6),
            name="expert",
        )(*table, near, far, *weights)

    def combine(keep, swap, hop):
        return pl.pallas_call(
            functools.partial(combine_kernel, slots, block),
            out_shape=shape(tok, width),
            in_specs=[vmem] * 4,
            out_specs=vmem,
            compiler_params=params(COMBINE),
            cost_estimate=cost(2 * tok * 6 * block * width, 3e6),
            name="combine",
        )(keep, over_core(swap), hop, over_core(hop))

    def to_groups(value):
        return [value] + [over_groups(value, r) for r in range(1, ng)]

    def four(value, hop):
        return [value, over_core(value), hop, over_core(hop)]

    if zn == 4:
        d1, da, h0 = over_z(d_out, 1), along_z(d_out, middle), over_x(d_out)
        d1, da, h0, mixed, *pairs = together(d1, da, h0, mixed, *pairs)

        q1, db, h1 = over_z(pairs[1], 1), along_z(d1, middle), over_x(d1)
        c0, c1 = four(d_out, h0), over_core(d1)
        done = [expert(c0, pairs[0][0], over_x(pairs[0][1]))]
        q1, db, h1, c1, p2, da, *done[0] = together(q1, db, h1, c1, pairs[2], da, *done[0])

        q2, dc, f1 = over_z(p2, 2), along_z(da, outward), over_x(q1[1])
        back, grads = [over_x(done[0][5])], [to_groups(done[0][0])]
        mixed_hop = over_x(after(mixed, f1))
        done.append(expert([d1, c1, h1, over_core(h1)], q1[0], f1))
        q2, dc, mixed_hop, back[0], db, p3, *rest = together(
            q2, dc, mixed_hop, back[0], db, pairs[3], *grads[0], *done[1]
        )
        grads[0], done[1] = rest[:ng], rest[ng:]

        q3, dd, f2 = over_z(p3, 3), along_z(db, outward), over_x(q2[1])
        d2 = jnp.where(inner_plane, db, dc)
        h2 = over_x(d2)
        back.append(over_x(after(done[1][5], f2)))
        grads.append(to_groups(done[1][0]))
        sums = [combine(done[0][3], done[0][4], back[0])]
        done.append(expert(four(d2, h2), q2[0], f2))
        q3, dd, back[1], mixed, *rest = together(q3, dd, back[1], mixed, *grads[1], *done[2])
        grads[1], done[2] = rest[:ng], rest[ng:]

        m1, ma, f3 = over_z(mixed, 1), along_z(mixed, middle), over_x(q3[1])
        d3 = jnp.where(inner_plane, da, dd)
        h3 = over_x(d3)
        back.append(over_x(after(done[2][5], f3)))
        grads.append(to_groups(done[2][0]))
        mb, mc = along_z(m1, middle), along_z(ma, outward)
        sums.append(combine(done[1][3], done[1][4], back[1]))
        done.append(expert(four(d3, h3), q3[0], f3))
        m1, ma, mb, mc, back[2], sums[1], *rest = together(
            m1, ma, mb, mc, back[2], sums[1], *grads[2], *done[3]
        )
        grads[2], done[3] = rest[:ng], rest[ng:]

        md, m1_hop = along_z(mb, outward), over_x(m1)
        back.append(over_x(done[3][5]))
        grads.append(to_groups(done[3][0]))
        sums.append(combine(done[2][3], done[2][4], back[2]))
        inputs = four(mixed, mixed_hop) + four(m1, m1_hop)
        m2 = jnp.where(inner_plane, mb, mc)
        md, back[3], m2, *rest = together(md, back[3], m2, *inputs, *grads[3])
        inputs, grads[3] = rest[:8], rest[8:]

        m3 = jnp.where(inner_plane, ma, md)
        inputs += four(m2, over_x(m2)) + four(m3, over_x(m3))
        sums.append(combine(done[3][3], done[3][4], back[3]))
    else:
        done, grads, sums, inputs = [], [], [], []
        for j in range(zn):
            d, q, m = (over_z(v, j) if j else v for v in (d_out, pairs[j], mixed))
            done.append(expert(four(d, over_x(d)), q[0], over_x(q[1])))
            grads.append(to_groups(done[j][0]))
            sums.append(combine(done[j][3], done[j][4], over_x(done[j][5])))
            inputs += four(m, over_x(m))
    d_tokens = sums[0].astype(F32)
    for j in range(1, zn):
        d_tokens = d_tokens + over_z(sums[j], j).astype(F32)
    grads = [value for plane in grads for value in plane]

    down_own, down_sent = pl.pallas_call(
        functools.partial(outer_kernel, zn, ng),
        out_shape=[shape(ffw, part, dtype=F32), shape(max(ng - 1, 1), ffw, part)],
        in_specs=[smem] + [anywhere] * (2 * zn),
        out_specs=[vmem, vmem],
        scratch_shapes=[
            pltpu.VMEM((zn * quad, ffw), BF16),
            pltpu.VMEM((zn * quad, width), BF16),
            pltpu.SemaphoreType.DMA((2 * zn,)),
        ],
        compiler_params=params(OUTER),
        cost_estimate=cost(2 * zn * quad * ffw * width, 10e6),
        name="outer",
    )(sc, *[d[1] for d in done], *[d[2] for d in done])
    d_down = down_own
    for r in range(1, ng):
        d_down = d_down + over_groups(down_sent[r - 1], r).astype(F32)

    units = zn * ng
    d_gate, d_up = pl.pallas_call(
        functools.partial(inner_kernel, zn, ng, slots, block),
        out_shape=[shape(ffw, part)] * 2,
        in_specs=[anywhere] * (len(inputs) + len(grads)),
        out_specs=[vmem, vmem],
        scratch_shapes=[
            pltpu.VMEM((units, 4 * tok, part), BF16),
            pltpu.VMEM((units * quad, 2 * ffw), BF16),
            pltpu.VMEM((2 * ffw, units * quad), BF16),
            pltpu.VMEM((units * quad, part), BF16),
            pltpu.SemaphoreType.DMA((4 * units,)),
            pltpu.SemaphoreType.DMA((units,)),
        ],
        compiler_params=params(INNER if units <= 16 else 58),
        cost_estimate=cost(4 * units * quad * ffw * part, 20e6),
        name="inner",
    )(*inputs, *grads)
    return (
        d_tokens.astype(BF16),
        d_gate.T[None],
        d_up.T[None],
        d_down.astype(BF16)[None],
    )


def solution(mesh):
    return jax.shard_map(
        per_device,
        mesh=mesh,
        in_specs=(
            P(("grp", "blk"), None),
            P(("grp", "blk"), None),
            P(("grp", "blk"), None),
            P(("grp", "blk"), None),
            P(("grp", "blk"), None, None),
            P(("grp", "blk"), None, None),
            P("blk", None, None),
            P("blk", None, None),
            P("blk", None, None),
        ),
        out_specs=(
            P(("grp", "blk"), None),
            P("blk", "grp", None),
            P("blk", "grp", None),
            P("blk", None, "grp"),
        ),
        check_vma=False,
    )
```

time: 292 us -> 263 us (0.901)
  waiting for transfers between devices: 146 us -> 122 us
  Pallas kernels: 58.9 us -> 52.9 us
  other arithmetic: 4.29 us -> 7.68 us
  starting transfers between devices: 59.9 us -> 56.7 us
    ppermute x18 -> x16, waiting for transfers between devices: 98.7 us -> 52.4 us  [the longest x8 38.8 us: over_z(): return lax.ppermute(value, 'blk', [(b, b ^ 4 * n) for b in range(nb)])]
    ppermute x17 -> x16, waiting for transfers between devices: 37.2 us -> 56.3 us  [over_x(): return lax.ppermute(value, 'blk', [(b, b ^ 2) for b in range(nb)])]
    pallas_call x10, Pallas kernels: 52.6 us -> 46.1 us  [the longest x4 24.7 us: expert(): pl.pallas_call(functools.partial(expert_kernel, slots, block), out_shape=...]
    ppermute x17 -> x16, starting transfers between devices: 18.9 us -> 16.7 us  [over_x(): return lax.ppermute(value, 'blk', [(b, b ^ 2) for b in range(nb)])]
    ppermute x7 -> x6, waiting for transfers between devices: 8.41 us -> 10.3 us  [over_groups(): return lax.ppermute(value, 'grp', [(b, (b + n) % ng) for b in range(ng)])]
    unnamed x92 -> x62, local copies, waits for them, and re-layouts: 17.8 us -> 16.5 us
    ppermute x7 -> x6, starting transfers between devices: 9.25 us -> 8.2 us  [over_groups(): return lax.ppermute(value, 'grp', [(b, (b + n) % ng) for b in range(ng)])]
    ppermute x18 -> x16, starting transfers between devices: 27.1 us -> 27.6 us  [the longest x8 22.7 us: along_z(): lax.ppermute(value, 'blk', [(4 * a + n, 4 * b + n) for a, b in pairs for...]
  transfers between devices with their start and end apart: 69 -> 63, of which waited for: 23 -> 18; matrix products, arithmetic and copies ran while one was open for 1% -> 3% of each run, Pallas kernels for 20% -> 14%
where the time goes in v3:
time: 263 us; the launch traced here: 261 us
  waiting for transfers between devices  122 us (46%)
  starting transfers between devices  56.7 us (22%)
  Pallas kernels  52.9 us (20%)
  local copies, waits for them, and re-layouts  20.4 us (8%)
  other arithmetic  7.68 us (3%)
    ppermute x16, waiting for transfers between devices, over_x(): return lax.ppermute(value, 'blk', [(b, b ^ 2) for b in range(nb)])  56.3 us
    ppermute x8, waiting for transfers between devices, over_z(): return lax.ppermute(value, 'blk', [(b, b ^ 4 * n) for b in range(nb)])  38.8 us
    pallas_call x4, Pallas kernels, expert(): pl.pallas_call(functools.partial(expert_kernel, slots, block), out_shape=...  24.7 us
    ppermute x8, starting transfers between devices, along_z(): lax.ppermute(value, 'blk', [(4 * a + n, 4 * b + n) for a, b in pairs for...  22.7 us
    ppermute x16, starting transfers between devices, over_x(): return lax.ppermute(value, 'blk', [(b, b ^ 2) for b in range(nb)])  16.7 us
    unnamed x62, local copies, waits for them, and re-layouts  16.5 us
    ppermute x8, waiting for transfers between devices, along_z(): lax.ppermute(value, 'blk', [(4 * a + n, 4 * b + n) for a, b in pairs for...  13.6 us
    pallas_call x1, Pallas kernels, per_device(): pl.pallas_call(functools.partial(inner_kernel, zn, ng, slots, block), out...  13.6 us
  transfers between devices with their start and end apart: 63, of which 18 were waited for; matrix products, arithmetic and copies ran while one was open for 3% of the time, Pallas kernels for 14%

profile of v3, /device:TPU:10, one launch (start us, length us, event | category | flops | bytes accessed | tf_op | source)
XLA Modules:
  0.0 261.1 jit_solution(11441003185739781782)
XLA Ops:
  2.1 1.2 copy-done.16
  3.4 1.2 copy-done.17
  4.6 3.9 %pack.1 = (bf16[4,2,56,1408]{3,2,1,0:T(8,128)(2,1)S(1)}, bf16[4,2,56,1408]{3,2,1,0:T(8,128)(2,1)S(1)}) custom-call(s32[4]{0:T(128)S(1)} %pad_add_fusion.sc, bf16[12,128]{1,0:T(8,128)(2,1)S(1)} %pad_maximum_fusion.5.meta_ref, bf16[6,704,128]{2,1,0:T(8,128)(2,1)S(1)} %bitcast.70, bf16[6,704,128]{2,1,0:T(8,128)(2,1)S(1)} %bitcast.71), custom_call_target="tpu_custom_call" | custom-call | flops 1937768448 | bytes 2162688 | tf_op jit(solution)/shard_map/pack/pallas_call | solution.py:287
  9.1 4.6 %collective-permute-start.1 = (bf16[128,2048]{1,0:T(8,128)(2,1)S(1)}, bf16[128,2048]{1,0:T(8,128)(2,1)}, u32[]{:S(2)}, u32[]{:S(2)}) collective-permute-start(bf16[128,2048]{1,0:T(8,128)(2,1)S(1)} %copy-done.7), channel_id=1, source_target_pairs={{4,8},{5,9},{6,10},{7,11},{8,4},{9,5},{10,6},{11,7},{20,24},{21,25... | collective-permute-start | bytes 1572872 | tf_op jit(solution)/shard_map/ppermute | solution.py:260
  14.3 1.1 constant_dynamic-slice_fusion.1
  15.4 1.6 collective-permute-start.3
  17.1 6.2 %collective-permute-done.3 = bf16[128,1024]{1,0:T(8,128)(2,1)S(1)} collective-permute-done((bf16[128,1024]{1,0:T(8,128)(2,1)S(1)}, bf16[128,1024]{1,0:T(8,128)(2,1)S(1)}, u32[]{:S(2)}, u32[]{:S(2)}) %collective-permute-start.3) | collective-permute-done | bytes 262176 | tf_op jit(solution)/shard_map/ppermute | solution.py:269
  24.1 1.5 slice_bitcast_fusion
  25.6 1.1 pad_maximum_fusion.2
  28.8 2.2 collective-permute-start.6
  31.0 1.0 collective-permute-start.7
  32.0 6.0 %collective-permute-done.11.far = bf16[112,1408]{1,0:T(8,128)(2,1)S(1)} collective-permute-done((bf16[112,1408]{1,0:T(8,128)(2,1)S(1)}, bf16[112,1408]{1,0:T(8,128)(2,1)S(1)}, u32[]{:S(2)}, u32[]{:S(2)}) %collective-permute-start.11) | collective-permute-done | bytes 315424 | tf_op jit(solution)/shard_map/ppermute | solution.py:263
  38.1 7.3 %expert.4 = (bf16[224,1408]{1,0:T(8,128)(2,1)}, bf16[224,704]{1,0:T(8,128)(2,1)S(1)}, bf16[224,2048]{1,0:T(8,128)(2,1)S(1)}, bf16[56,2048]{1,0:T(8,128)(2,1)S(1)...) custom-call(bf16[128,2048]{1,0:T(8,128)(2,1)S(1)} %copy-done.7, ...), custom_call_target="tpu_custom_call" | custom-call | flops 3053453312 | bytes 16000000 | tf_op jit(solution)/shard_map/expert/pallas_call | solution.py:311
  46.1 0.9 copy-done.18
  51.5 1.5 collective-permute-start.18
  53.0 4.5 %collective-permute-start.14 = (bf16[128,2048]{1,0:T(8,128)(2,1)}, bf16[128,2048]{1,0:T(8,128)(2,1)}, u32[]{:S(2)}, u32[]{:S(2)}) collective-permute-start(bf16[128,2048]{1,0:T(8,128)(2,1)} %collective-permute-done.1), channel_id=1, source_target_pairs={{4,0},{5,1},{6,2},{7,3},{8,12},{9,13},{10,14},{11,15},{20,16},{21,... | collective-permute-start | bytes 1572872 | tf_op jit(solution)/shard_map/ppermute | solution.py:260
  57.5 2.7 %collective-permute-done.15.far = bf16[112,1408]{1,0:T(8,128)(2,1)S(1)} collective-permute-done((bf16[112,1408]{1,0:T(8,128)(2,1)S(1)}, bf16[112,1408]{1,0:T(8,128)(2,1)S(1)}, u32[]{:S(2)}, u32[]{:S(2)}) %collective-permute-start.15) | collective-permute-done | bytes 315424 | tf_op jit(solution)/shard_map/ppermute | solution.py:263
  60.1 1.1 collective-permute-start.16
  62.9 1.8 copy-done.2
  64.7 1.8 copy-done.5
  66.6 1.0 copy-done.9
  67.6 1.0 copy-done.11
  68.6 1.0 copy-done.13
  69.7 6.5 %expert.5 = (bf16[224,1408]{1,0:T(8,128)(2,1)S(1)}, bf16[224,704]{1,0:T(8,128)(2,1)S(1)}, bf16[224,2048]{1,0:T(8,128)(2,1)S(1)}, bf16[56,2048]{1,0:T(8,128)(2,1)...) custom-call(bf16[128,2048]{1,0:T(8,128)(2,1)} %collective-permute-done.d00, ...), custom_call_target="tpu_custom_call" | custom-call | flops 3053453312 | bytes 16000000 | tf_op jit(solution)/shard_map/expert/pallas_call | solution.py:311
  76.2 7.1 %collective-permute-done.17.hop = bf16[112,2048]{1,0:T(8,128)(2,1)} collective-permute-done((bf16[112,2048]{1,0:T(8,128)(2,1)}, bf16[112,2048]{1,0:T(8,128)(2,1)}, u32[]{:S(2)}, u32[]{:S(2)}) %collective-permute-start.17) | collective-permute-done | bytes 458784 | tf_op jit(solution)/shard_map/ppermute | solution.py:263
  83.5 1.7 collective-permute-start.27
  85.2 1.1 slice_bitcast_fusion.6
  86.8 11.7 %collective-permute-done.27.d10 = bf16[128,2048]{1,0:T(8,128)(2,1)S(1)} collective-permute-done((bf16[128,2048]{1,0:T(8,128)(2,1)S(1)}, bf16[128,2048]{1,0:T(8,128)(2,1)S(1)}, u32[]{:S(2)}, u32[]{:S(2)}) %collective-permute-start.27) | collective-permute-done | bytes 524320 | tf_op jit(solution)/shard_map/ppermute | solution.py:263
  98.7 1.5 collective-permute-start.25
  100.2 2.6 %collective-permute-done.23.far = bf16[112,1408]{1,0:T(8,128)(2,1)S(1)} collective-permute-done((bf16[112,1408]{1,0:T(8,128)(2,1)S(1)}, bf16[112,1408]{1,0:T(8,128)(2,1)S(1)}, u32[]{:S(2)}, u32[]{:S(2)}) %collective-permute-start.23) | collective-permute-done | bytes 315424 | tf_op jit(solution)/shard_map/ppermute | solution.py:263
  102.9 2.1 collective-permute-start.22
  105.0 1.3 collective-permute-start.24
  106.4 5.4 %expert.6 = (bf16[224,1408]{1,0:T(8,128)(2,1)S(1)}, bf16[224,704]{1,0:T(8,128)(2,1)S(1)}, bf16[224,2048]{1,0:T(8,128)(2,1)S(1)}, bf16[56,2048]{1,0:T(8,128)(2,1)...) custom-call(bf16[128,2048]{1,0:T(8,128)(2,1)S(1)} %broadcast_select_fusion.3.d00, ...), custom_call_target="tpu_custom_call" | custom-call | flops 3053453312 | bytes 16000000 | tf_op jit(solution)/shard_map/expert/pallas_call | solution.py:311
  111.8 13.6 %collective-permute-done.22 = bf16[128,2048]{1,0:T(8,128)(2,1)S(1)} collective-permute-done((bf16[128,2048]{1,0:T(8,128)(2,1)S(1)}, bf16[128,2048]{1,0:T(8,128)(2,1)S(1)}, u32[]{:S(2)}, u32[]{:S(2)}) %collective-permute-start.22) | collective-permute-done | bytes 524320 | tf_op jit(solution)/shard_map/ppermute | solution.py:260
  125.4 3.2 %collective-permute-done.21 = bf16[2,112,1408]{2,1,0:T(8,128)(2,1)S(1)} collective-permute-done((bf16[2,112,1408]{2,1,0:T(8,128)(2,1)S(1)}, bf16[2,112,1408]{2,1,0:T(8,128)(2,1)S(1)}, u32[]{:S(2)}, u32[]{:S(2)}) %collective-permute-start.21) | collective-permute-done | bytes 630816 | tf_op jit(solution)/shard_map/ppermute | solution.py:257
  128.6 1.1 broadcast_select_fusion.2.d00
  129.7 1.7 collective-permute-start.39
  132.4 1.0 collective-permute-done.35.swap
  133.4 2.2 collective-permute-start.30
  135.6 14.7 %collective-permute-done.33.far = bf16[112,1408]{1,0:T(8,128)(2,1)S(1)} collective-permute-done((bf16[112,1408]{1,0:T(8,128)(2,1)S(1)}, bf16[112,1408]{1,0:T(8,128)(2,1)S(1)}, u32[]{:S(2)}, u32[]{:S(2)}) %collective-permute-start.33) | collective-permute-done | bytes 315424 | tf_op jit(solution)/shard_map/ppermute | solution.py:263
  150.8 1.5 collective-permute-start.37
  152.4 1.9 collective-permute-start.31
  154.3 2.1 collective-permute-start.32
  156.4 1.6 collective-permute-start.34
  158.9 5.4 %expert.7 = (bf16[224,1408]{1,0:T(8,128)(2,1)S(1)}, bf16[224,704]{1,0:T(8,128)(2,1)S(1)}, bf16[224,2048]{1,0:T(8,128)(2,1)S(1)}, bf16[56,2048]{1,0:T(8,128)(2,1)...) custom-call(bf16[128,2048]{1,0:T(8,128)(2,1)S(1)} %broadcast_select_fusion.2.d00, ...), custom_call_target="tpu_custom_call" | custom-call | flops 3053453312 | bytes 16000000 | tf_op jit(solution)/shard_map/expert/pallas_call | solution.py:311
  165.1 1.9 collective-permute-done.37.refs_21_
  167.0 1.6 collective-permute-done.34.hop
  168.6 1.6 collective-permute-start.51
  171.1 3.1 %collective-permute-start.46 = (bf16[256,1024]{1,0:T(8,128)(2,1)S(1)}, bf16[256,1024]{1,0:T(8,128)(2,1)S(1)}, u32[]{:S(2)}, u32[]{:S(2)}) collective-permute-start(bf16[256,1024]{1,0:T(8,128)(2,1)S(1)} %collective-permute-done.31), channel_id=1, source_target_pairs={{4,0},{5,1},{6,2},{7,3},{8,12},{9,13},{10,14},{11,15},{20,16},{21,... | collective-permute-start | bytes 1572872 | tf_op jit(solution)/shard_map/ppermute | solution.py:260
  174.4 9.1 %collective-permute-done.51.refs_6_ = bf16[256,1024]{1,0:T(8,128)(2,1)S(1)} collective-permute-done((bf16[256,1024]{1,0:T(8,128)(2,1)S(1)}, bf16[256,1024]{1,0:T(8,128)(2,1)S(1)}, u32[]{:S(2)}, u32[]{:S(2)}) %collective-permute-start.51) | collective-permute-done | bytes 524320 | tf_op jit(solution)/shard_map/ppermute | solution.py:263
  183.5 1.0 copy-done.23
  184.5 6.8 %outer.1 = (f32[704,1024]{1,0:T(8,128)S(1)}, bf16[1,704,1024]{2,1,0:T(8,128)(2,1)S(1)}) custom-call(s32[4]{0:T(128)S(1)} %pad_add_fusion.sc, bf16[224,704]{1,0:T(8,128)(2,1)S(1)} %copy-done.21, bf16[224,704]{1,0:T(8,128)(2,1)S(1)} %get-tuple-element.207.refs_1_, bf16[224,704]{1,0:T(8,128)(2,1)S(1)} %get-tuple-element.208.refs_2_, ...), custom_call_target="tpu_custom_call" | custom-call | flops 2583691264 | bytes 10000000 | tf_op jit(solution)/shard_map/outer/pallas_call | solution.py:416
  191.3 1.5 collective-permute-start.62
  193.9 2.0 collective-permute-done.42.swap
  197.4 2.1 collective-permute-start.44
  199.6 1.6 collective-permute-start.60
  202.4 17.0 %collective-permute-done.41 = bf16[128,2048]{1,0:T(8,128)(2,1)S(1)} collective-permute-done((bf16[128,2048]{1,0:T(8,128)(2,1)S(1)}, bf16[128,2048]{1,0:T(8,128)(2,1)S(1)}, u32[]{:S(2)}, u32[]{:S(2)}) %collective-permute-start.41) | collective-permute-done | bytes 524320 | tf_op jit(solution)/shard_map/ppermute | solution.py:257
  219.4 1.8 collective-permute-start.55
  221.3 1.8 combine.4
  223.1 2.2 collective-permute-done.62
  225.9 1.7 fusion
  227.6 18.6 %collective-permute-done.55 = bf16[128,2048]{1,0:T(8,128)(2,1)S(1)} collective-permute-done((bf16[128,2048]{1,0:T(8,128)(2,1)S(1)}, bf16[128,2048]{1,0:T(8,128)(2,1)S(1)}, u32[]{:S(2)}, u32[]{:S(2)}) %collective-permute-start.55) | collective-permute-done | bytes 524320 | tf_op jit(solution)/shard_map/ppermute | solution.py:257
  246.2 1.1 add_convert_fusion.1
  247.3 13.6 %inner.1 = (bf16[704,1024]{1,0:T(8,128)(2,1)}, bf16[704,1024]{1,0:T(8,128)(2,1)}) custom-call(bf16[256,1024]{1,0:T(8,128)(2,1)} %pad_maximum_fusion.4.refs_0_, bf16[256,1024]{1,0:T(8,128)(2,1)S(1)} %collective-permute-done.48.refs_1_, bf16[256,1024]{1,0:T(8,128)(2,1)} %collective-permute-done.16.refs_2_, ...), custom_call_target="tpu_custom_call" | custom-call | flops 5167382528 | bytes 20000000 | tf_op jit(solution)/shard_map/inner/pallas_call | solution.py:435
  (154 shorter events, 22.0 us)
Async XLA Ops:
  8.5 15.6 %collective-permute-start.4 = (bf16[4,2,56,1408]{3,2,1,0:T(8,128)(2,1)S(1)}, bf16[4,2,56,1408]{3,2,1,0:T(8,128)(2,1)}, u32[]{:S(2)}, u32[]{:S(2)}) collective-permute-start(bf16[4,2,56,1408]{3,2,1,0:T(8,128)(2,1)S(1)} %get-tuple-element.111), channel_id=1, source_target_pairs={{0,1},{1,0},{2,3},{3,2},{4,5},{5,4},{6,7},{7,6},{8,9},{9,8},{10,11... | collective-permute-start | bytes 3784712 | tf_op jit(solution)/shard_map/ppermute | solution.py:266
  8.6 18.3 %collective-permute-start = (bf16[128,2048]{1,0:T(8,128)(2,1)S(1)}, bf16[128,2048]{1,0:T(8,128)(2,1)}, u32[]{:S(2)}, u32[]{:S(2)}) collective-permute-start(bf16[128,2048]{1,0:T(8,128)(2,1)S(1)} %copy-done.7), channel_id=1, source_target_pairs={{0,4},{1,5},{2,6},{3,7},{4,0},{5,1},{6,2},{7,3},{8,12},{9,13},{10,... | collective-permute-start | bytes 1572872 | tf_op jit(solution)/shard_map/ppermute | solution.py:257
  9.1 17.8 %collective-permute-start.1 = (bf16[128,2048]{1,0:T(8,128)(2,1)S(1)}, bf16[128,2048]{1,0:T(8,128)(2,1)}, u32[]{:S(2)}, u32[]{:S(2)}) collective-permute-start(bf16[128,2048]{1,0:T(8,128)(2,1)S(1)} %copy-done.7), channel_id=1, source_target_pairs={{4,8},{5,9},{6,10},{7,11},{8,4},{9,5},{10,6},{11,7},{20,24},{21,25... | collective-permute-start | bytes 1572872 | tf_op jit(solution)/shard_map/ppermute | solution.py:260
  13.7 13.9 %collective-permute-start.2 = (bf16[128,2048]{1,0:T(8,128)(2,1)S(1)}, bf16[128,2048]{1,0:T(8,128)(2,1)}, u32[]{:S(2)}, u32[]{:S(2)}) collective-permute-start(bf16[128,2048]{1,0:T(8,128)(2,1)S(1)} %copy-done.7), channel_id=1, source_target_pairs={{0,2},{1,3},{2,0},{3,1},{4,6},{5,7},{6,4},{7,5},{8,10},{9,11},{10,... | collective-permute-start | bytes 1572872 | tf_op jit(solution)/shard_map/ppermute | solution.py:263
  15.4 7.9 %collective-permute-start.3 = (bf16[128,1024]{1,0:T(8,128)(2,1)S(1)}, bf16[128,1024]{1,0:T(8,128)(2,1)S(1)}, u32[]{:S(2)}, u32[]{:S(2)}) collective-permute-start(bf16[128,1024]{1,0:T(8,128)(2,1)S(1)} %get-tuple-element.233), channel_id=1, source_target_pairs={{0,16},{16,0},{1,17},{17,1},{2,18},{18,2},{3,19},{19,3},{4,20},{20... | collective-permute-start | bytes 786440 | tf_op jit(solution)/shard_map/ppermute | solution.py:269
  23.3 7.7 %collective-permute-start.9 = (bf16[128,2048]{1,0:T(8,128)(2,1)S(1)}, bf16[128,2048]{1,0:T(8,128)(2,1)S(1)}, u32[]{:S(2)}, u32[]{:S(2)}) collective-permute-start(bf16[128,2048]{1,0:T(8,128)(2,1)S(1)} %copy-done.7), channel_id=1, source_target_pairs={{0,1},{1,0},{2,3},{3,2},{4,5},{5,4},{6,7},{7,6},{8,9},{9,8},{10,11... | collective-permute-start | bytes 1572872 | tf_op jit(solution)/shard_map/ppermute | solution.py:266
  27.6 10.4 %collective-permute-start.11 = (bf16[112,1408]{1,0:T(8,128)(2,1)S(1)}, bf16[112,1408]{1,0:T(8,128)(2,1)S(1)}, u32[]{:S(2)}, u32[]{:S(2)}) collective-permute-start(bf16[112,1408]{1,0:T(8,128)(2,1)S(1)} %get-tuple-element.230), channel_id=1, source_target_pairs={{0,2},{1,3},{2,0},{3,1},{4,6},{5,7},{6,4},{7,5},{8,10},{9,11},{10,... | collective-permute-start | bytes 946184 | tf_op jit(solution)/shard_map/ppermute | solution.py:263
  28.5 9.5 %collective-permute-start.10 = (bf16[128,2048]{1,0:T(8,128)(2,1)}, bf16[128,2048]{1,0:T(8,128)(2,1)S(1)}, u32[]{:S(2)}, u32[]{:S(2)}) collective-permute-start(bf16[128,2048]{1,0:T(8,128)(2,1)} %collective-permute-done.2.d10), channel_id=1, source_target_pairs={{0,1},{1,0},{2,3},{3,2},{4,5},{5,4},{6,7},{7,6},{8,9},{9,8},{10,11... | collective-permute-start | bytes 1572872 | tf_op jit(solution)/shard_map/ppermute | solution.py:266
  28.8 20.6 %collective-permute-start.5 = (bf16[2,112,1408]{2,1,0:T(8,128)(2,1)S(1)}, bf16[2,112,1408]{2,1,0:T(8,128)(2,1)S(1)}, u32[]{:S(2)}, u32[]{:S(2)}) collective-permute-start(bf16[2,112,1408]{2,1,0:T(8,128)(2,1)S(1)} %get-tuple-element.112), channel_id=1, source_target_pairs={{0,4},{1,5},{2,6},{3,7},{4,0},{5,1},{6,2},{7,3},{8,12},{9,13},{10,... | collective-permute-start | bytes 1892360 | tf_op jit(solution)/shard_map/ppermute | solution.py:257
  28.8 19.7 %collective-permute-start.6 = (bf16[128,2048]{1,0:T(8,128)(2,1)}, bf16[128,2048]{1,0:T(8,128)(2,1)S(1)}, u32[]{:S(2)}, u32[]{:S(2)}) collective-permute-start(bf16[128,2048]{1,0:T(8,128)(2,1)} %collective-permute-done.d00), channel_id=1, source_target_pairs={{4,8},{5,9},{6,10},{7,11},{8,4},{9,5},{10,6},{11,7},{20,24},{21,25... | collective-permute-start | bytes 1572872 | tf_op jit(solution)/shard_map/ppermute | solution.py:260
  31.0 17.5 %collective-permute-start.7 = (bf16[128,2048]{1,0:T(8,128)(2,1)}, bf16[128,2048]{1,0:T(8,128)(2,1)S(1)}, u32[]{:S(2)}, u32[]{:S(2)}) collective-permute-start(bf16[128,2048]{1,0:T(8,128)(2,1)} %collective-permute-done.d00), channel_id=1, source_target_pairs={{0,2},{1,3},{2,0},{3,1},{4,6},{5,7},{6,4},{7,5},{8,10},{9,11},{10,... | collective-permute-start | bytes 1572872 | tf_op jit(solution)/shard_map/ppermute | solution.py:263
  38.0 10.4 %collective-permute-start.8 = (bf16[128,2048]{1,0:T(8,128)(2,1)}, bf16[128,2048]{1,0:T(8,128)(2,1)S(1)}, u32[]{:S(2)}, u32[]{:S(2)}) collective-permute-start(bf16[128,2048]{1,0:T(8,128)(2,1)} %collective-permute-done.d00), channel_id=1, source_target_pairs={{0,1},{1,0},{2,3},{3,2},{4,5},{5,4},{6,7},{7,6},{8,9},{9,8},{10,11... | collective-permute-start | bytes 1572872 | tf_op jit(solution)/shard_map/ppermute | solution.py:266
  49.3 11.9 %collective-permute-start.19 = (bf16[128,2048]{1,0:T(8,128)(2,1)S(1)}, bf16[128,2048]{1,0:T(8,128)(2,1)S(1)}, u32[]{:S(2)}, u32[]{:S(2)}) collective-permute-start(bf16[128,2048]{1,0:T(8,128)(2,1)S(1)} %collective-permute-done.7.d10), channel_id=1, source_target_pairs={{0,1},{1,0},{2,3},{3,2},{4,5},{5,4},{6,7},{7,6},{8,9},{9,8},{10,11... | collective-permute-start | bytes 1572872 | tf_op jit(solution)/shard_map/ppermute | solution.py:266
  50.7 9.4 %collective-permute-start.15 = (bf16[112,1408]{1,0:T(8,128)(2,1)S(1)}, bf16[112,1408]{1,0:T(8,128)(2,1)S(1)}, u32[]{:S(2)}, u32[]{:S(2)}) collective-permute-start(bf16[112,1408]{1,0:T(8,128)(2,1)S(1)} %get-tuple-element.229), channel_id=1, source_target_pairs={{0,2},{1,3},{2,0},{3,1},{4,6},{5,7},{6,4},{7,5},{8,10},{9,11},{10,... | collective-permute-start | bytes 946184 | tf_op jit(solution)/shard_map/ppermute | solution.py:263
  51.5 31.9 %collective-permute-start.13 = (bf16[2,112,1408]{2,1,0:T(8,128)(2,1)}, bf16[2,112,1408]{2,1,0:T(8,128)(2,1)}, u32[]{:S(2)}, u32[]{:S(2)}) collective-permute-start(bf16[2,112,1408]{2,1,0:T(8,128)(2,1)} %get-tuple-element.126), channel_id=1, source_target_pairs={{0,8},{1,9},{2,10},{3,11},{4,12},{5,13},{6,14},{7,15},{8,0},{9,1},... | collective-permute-start | bytes 1892360 | tf_op jit(solution)/shard_map/ppermute | solution.py:257
  51.5 31.9 %collective-permute-start.18 = (bf16[224,1408]{1,0:T(8,128)(2,1)}, bf16[224,1408]{1,0:T(8,128)(2,1)}, u32[]{:S(2)}, u32[]{:S(2)}) collective-permute-start(bf16[224,1408]{1,0:T(8,128)(2,1)} %get-tuple-element.196.refs_16_), channel_id=1, source_target_pairs={{0,16},{16,0},{1,17},{17,1},{2,18},{18,2},{3,19},{19,3},{4,20},{20... | collective-permute-start | bytes 1892360 | tf_op jit(solution)/shard_map/ppermute | solution.py:269
  53.0 30.4 %collective-permute-start.14 = (bf16[128,2048]{1,0:T(8,128)(2,1)}, bf16[128,2048]{1,0:T(8,128)(2,1)}, u32[]{:S(2)}, u32[]{:S(2)}) collective-permute-start(bf16[128,2048]{1,0:T(8,128)(2,1)} %collective-permute-done.1), channel_id=1, source_target_pairs={{4,0},{5,1},{6,2},{7,3},{8,12},{9,13},{10,14},{11,15},{20,16},{21,... | collective-permute-start | bytes 1572872 | tf_op jit(solution)/shard_map/ppermute | solution.py:260
  60.1 23.3 %collective-permute-start.16 = (bf16[256,1024]{1,0:T(8,128)(2,1)}, bf16[256,1024]{1,0:T(8,128)(2,1)}, u32[]{:S(2)}, u32[]{:S(2)}) collective-permute-start(bf16[256,1024]{1,0:T(8,128)(2,1)} %pad_maximum_fusion.4.refs_0_), channel_id=1, source_target_pairs={{0,2},{1,3},{2,0},{3,1},{4,6},{5,7},{6,4},{7,5},{8,10},{9,11},{10,... | collective-permute-start | bytes 1572872 | tf_op jit(solution)/shard_map/ppermute | solution.py:263
  62.0 21.3 %collective-permute-start.17 = (bf16[112,2048]{1,0:T(8,128)(2,1)}, bf16[112,2048]{1,0:T(8,128)(2,1)}, u32[]{:S(2)}, u32[]{:S(2)}) collective-permute-start(bf16[112,2048]{1,0:T(8,128)(2,1)} %get-tuple-element.131), channel_id=1, source_target_pairs={{0,2},{1,3},{2,0},{3,1},{4,6},{5,7},{6,4},{7,5},{8,10},{9,11},{10,... | collective-permute-start | bytes 1376264 | tf_op jit(solution)/shard_map/ppermute | solution.py:263
  83.5 14.9 %collective-permute-start.27 = (bf16[128,2048]{1,0:T(8,128)(2,1)S(1)}, bf16[128,2048]{1,0:T(8,128)(2,1)S(1)}, u32[]{:S(2)}, u32[]{:S(2)}) collective-permute-start(bf16[128,2048]{1,0:T(8,128)(2,1)S(1)} %broadcast_select_fusion.3.d00), channel_id=1, source_target_pairs={{0,2},{1,3},{2,0},{3,1},{4,6},{5,7},{6,4},{7,5},{8,10},{9,11},{10,... | collective-permute-start | bytes 1572872 | tf_op jit(solution)/shard_map/ppermute | solution.py:263
  85.2 19.8 %collective-permute-start.26 = (bf16[128,2048]{1,0:T(8,128)(2,1)S(1)}, bf16[128,2048]{1,0:T(8,128)(2,1)S(1)}, u32[]{:S(2)}, u32[]{:S(2)}) collective-permute-start(bf16[128,2048]{1,0:T(8,128)(2,1)S(1)} %broadcast_select_fusion.3.d00), channel_id=1, source_target_pairs={{0,1},{1,0},{2,3},{3,2},{4,5},{5,4},{6,7},{7,6},{8,9},{9,8},{10,11... | collective-permute-start | bytes 1572872 | tf_op jit(solution)/shard_map/ppermute | solution.py:266
  86.3 16.6 %collective-permute-start.23 = (bf16[112,1408]{1,0:T(8,128)(2,1)S(1)}, bf16[112,1408]{1,0:T(8,128)(2,1)S(1)}, u32[]{:S(2)}, u32[]{:S(2)}) collective-permute-start(bf16[112,1408]{1,0:T(8,128)(2,1)S(1)} %get-tuple-element.227), channel_id=1, source_target_pairs={{0,2},{1,3},{2,0},{3,1},{4,6},{5,7},{6,4},{7,5},{8,10},{9,11},{10,... | collective-permute-start | bytes 946184 | tf_op jit(solution)/shard_map/ppermute | solution.py:263
  98.4 7.9 %collective-permute-start.28 = (bf16[128,2048]{1,0:T(8,128)(2,1)S(1)}, bf16[128,2048]{1,0:T(8,128)(2,1)S(1)}, u32[]{:S(2)}, u32[]{:S(2)}) collective-permute-start(bf16[128,2048]{1,0:T(8,128)(2,1)S(1)} %collective-permute-done.27.d10), channel_id=1, source_target_pairs={{0,1},{1,0},{2,3},{3,2},{4,5},{5,4},{6,7},{7,6},{8,9},{9,8},{10,11... | collective-permute-start | bytes 1572872 | tf_op jit(solution)/shard_map/ppermute | solution.py:266
  98.4 30.1 %collective-permute-start.21 = (bf16[2,112,1408]{2,1,0:T(8,128)(2,1)S(1)}, bf16[2,112,1408]{2,1,0:T(8,128)(2,1)S(1)}, u32[]{:S(2)}, u32[]{:S(2)}) collective-permute-start(bf16[2,112,1408]{2,1,0:T(8,128)(2,1)S(1)} %copy-done.28), channel_id=1, source_target_pairs={{0,12},{1,13},{2,14},{3,15},{4,8},{5,9},{6,10},{7,11},{8,4},{9,5},... | collective-permute-start | bytes 1892360 | tf_op jit(solution)/shard_map/ppermute | solution.py:257
  98.7 29.9 %collective-permute-start.25 = (bf16[224,1408]{1,0:T(8,128)(2,1)S(1)}, bf16[224,1408]{1,0:T(8,128)(2,1)S(1)}, u32[]{:S(2)}, u32[]{:S(2)}) collective-permute-start(bf16[224,1408]{1,0:T(8,128)(2,1)S(1)} %get-tuple-element.198.refs_18_), channel_id=1, source_target_pairs={{0,16},{16,0},{1,17},{17,1},{2,18},{18,2},{3,19},{19,3},{4,20},{20... | collective-permute-start | bytes 1892360 | tf_op jit(solution)/shard_map/ppermute | solution.py:269
  102.9 22.5 %collective-permute-start.22 = (bf16[128,2048]{1,0:T(8,128)(2,1)S(1)}, bf16[128,2048]{1,0:T(8,128)(2,1)S(1)}, u32[]{:S(2)}, u32[]{:S(2)}) collective-permute-start(bf16[128,2048]{1,0:T(8,128)(2,1)S(1)} %copy-done.30), channel_id=1, source_target_pairs={{4,0},{5,1},{6,2},{7,3},{8,12},{9,13},{10,14},{11,15},{20,16},{21,... | collective-permute-start | bytes 1572872 | tf_op jit(solution)/shard_map/ppermute | solution.py:260
  105.0 23.5 %collective-permute-start.24 = (bf16[112,2048]{1,0:T(8,128)(2,1)S(1)}, bf16[112,2048]{1,0:T(8,128)(2,1)S(1)}, u32[]{:S(2)}, u32[]{:S(2)}) collective-permute-start(bf16[112,2048]{1,0:T(8,128)(2,1)S(1)} %get-tuple-element.148), channel_id=1, source_target_pairs={{0,2},{1,3},{2,0},{3,1},{4,6},{5,7},{6,4},{7,5},{8,10},{9,11},{10,... | collective-permute-start | bytes 1376264 | tf_op jit(solution)/shard_map/ppermute | solution.py:263
  106.4 52.5 %copy-start.6 = (bf16[1,704,2048]{2,1,0:T(8,128)(2,1)S(1)}, bf16[1,704,2048]{2,1,0:T(8,128)(2,1)}, u32[]{:S(2)}) copy-start(bf16[1,704,2048]{2,1,0:T(8,128)(2,1)} %param.17) | copy-start | bytes 8650756
  129.7 20.6 %collective-permute-start.39 = (bf16[128,2048]{1,0:T(8,128)(2,1)S(1)}, bf16[128,2048]{1,0:T(8,128)(2,1)S(1)}, u32[]{:S(2)}, u32[]{:S(2)}) collective-permute-start(bf16[128,2048]{1,0:T(8,128)(2,1)S(1)} %broadcast_select_fusion.2.d00), channel_id=1, source_target_pairs={{0,2},{1,3},{2,0},{3,1},{4,6},{5,7},{6,4},{7,5},{8,10},{9,11},{10,... | collective-permute-start | bytes 1572872 | tf_op jit(solution)/shard_map/ppermute | solution.py:263
  131.4 18.9 %collective-permute-start.33 = (bf16[112,1408]{1,0:T(8,128)(2,1)S(1)}, bf16[112,1408]{1,0:T(8,128)(2,1)S(1)}, u32[]{:S(2)}, u32[]{:S(2)}) collective-permute-start(bf16[112,1408]{1,0:T(8,128)(2,1)S(1)} %get-tuple-element.225), channel_id=1, source_target_pairs={{0,2},{1,3},{2,0},{3,1},{4,6},{5,7},{6,4},{7,5},{8,10},{9,11},{10,... | collective-permute-start | bytes 946184 | tf_op jit(solution)/shard_map/ppermute | solution.py:263
  131.9 1.5 collective-permute-start.35
  131.9 18.9 %collective-permute-start.36 = (bf16[112,2048]{1,0:T(8,128)(2,1)S(1)}, bf16[112,2048]{1,0:T(8,128)(2,1)S(1)}, u32[]{:S(2)}, u32[]{:S(2)}) collective-permute-start(bf16[112,2048]{1,0:T(8,128)(2,1)S(1)} %collective-permute-done.24.hop), channel_id=1, source_target_pairs={{0,1},{1,0},{2,3},{3,2},{4,5},{5,4},{6,7},{7,6},{8,9},{9,8},{10,11... | collective-permute-start | bytes 1376264 | tf_op jit(solution)/shard_map/ppermute | solution.py:266
  132.4 20.0 %collective-permute-start.29 = (bf16[256,1024]{1,0:T(8,128)(2,1)}, bf16[256,1024]{1,0:T(8,128)(2,1)S(1)}, u32[]{:S(2)}, u32[]{:S(2)}) collective-permute-start(bf16[256,1024]{1,0:T(8,128)(2,1)} %pad_maximum_fusion.4.refs_0_), channel_id=1, source_target_pairs={{0,4},{1,5},{2,6},{3,7},{4,0},{5,1},{6,2},{7,3},{8,12},{9,13},{10,... | collective-permute-start | bytes 1572872 | tf_op jit(solution)/shard_map/ppermute | solution.py:257
  133.4 20.9 %collective-permute-start.30 = (bf16[256,1024]{1,0:T(8,128)(2,1)}, bf16[256,1024]{1,0:T(8,128)(2,1)S(1)}, u32[]{:S(2)}, u32[]{:S(2)}) collective-permute-start(bf16[256,1024]{1,0:T(8,128)(2,1)} %pad_maximum_fusion.4.refs_0_), channel_id=1, source_target_pairs={{4,8},{5,9},{6,10},{7,11},{8,4},{9,5},{10,6},{11,7},{20,24},{21,25... | collective-permute-start | bytes 1572872 | tf_op jit(solution)/shard_map/ppermute | solution.py:260
  150.3 6.1 %collective-permute-start.38 = (bf16[128,2048]{1,0:T(8,128)(2,1)S(1)}, bf16[128,2048]{1,0:T(8,128)(2,1)S(1)}, u32[]{:S(2)}, u32[]{:S(2)}) collective-permute-start(bf16[128,2048]{1,0:T(8,128)(2,1)S(1)} %broadcast_select_fusion.2.d00), channel_id=1, source_target_pairs={{0,1},{1,0},{2,3},{3,2},{4,5},{5,4},{6,7},{7,6},{8,9},{9,8},{10,11... | collective-permute-start | bytes 1572872 | tf_op jit(solution)/shard_map/ppermute | solution.py:266
  150.3 8.4 %collective-permute-start.40 = (bf16[128,2048]{1,0:T(8,128)(2,1)S(1)}, bf16[128,2048]{1,0:T(8,128)(2,1)S(1)}, u32[]{:S(2)}, u32[]{:S(2)}) collective-permute-start(bf16[128,2048]{1,0:T(8,128)(2,1)S(1)} %collective-permute-done.39.d10), channel_id=1, source_target_pairs={{0,1},{1,0},{2,3},{3,2},{4,5},{5,4},{6,7},{7,6},{8,9},{9,8},{10,11... | collective-permute-start | bytes 1572872 | tf_op jit(solution)/shard_map/ppermute | solution.py:266
  150.8 16.2 %collective-permute-start.37 = (bf16[224,1408]{1,0:T(8,128)(2,1)S(1)}, bf16[224,1408]{1,0:T(8,128)(2,1)S(1)}, u32[]{:S(2)}, u32[]{:S(2)}) collective-permute-start(bf16[224,1408]{1,0:T(8,128)(2,1)S(1)} %get-tuple-element.200.refs_20_), channel_id=1, source_target_pairs={{0,16},{16,0},{1,17},{17,1},{2,18},{18,2},{3,19},{19,3},{4,20},{20... | collective-permute-start | bytes 1892360 | tf_op jit(solution)/shard_map/ppermute | solution.py:269
  152.4 16.2 %collective-permute-start.31 = (bf16[256,1024]{1,0:T(8,128)(2,1)S(1)}, bf16[256,1024]{1,0:T(8,128)(2,1)S(1)}, u32[]{:S(2)}, u32[]{:S(2)}) collective-permute-start(bf16[256,1024]{1,0:T(8,128)(2,1)S(1)} %collective-permute-done.29.refs_4_), channel_id=1, source_target_pairs={{4,8},{5,9},{6,10},{7,11},{8,4},{9,5},{10,6},{11,7},{20,24},{21,25... | collective-permute-start | bytes 1572872 | tf_op jit(solution)/shard_map/ppermute | solution.py:260
  154.3 14.3 %collective-permute-start.32 = (bf16[256,1024]{1,0:T(8,128)(2,1)S(1)}, bf16[256,1024]{1,0:T(8,128)(2,1)}, u32[]{:S(2)}, u32[]{:S(2)}) collective-permute-start(bf16[256,1024]{1,0:T(8,128)(2,1)S(1)} %collective-permute-done.30), channel_id=1, source_target_pairs={{4,0},{5,1},{6,2},{7,3},{8,12},{9,13},{10,14},{11,15},{20,16},{21,... | collective-permute-start | bytes 1572872 | tf_op jit(solution)/shard_map/ppermute | solution.py:260
  156.4 12.2 %collective-permute-start.34 = (bf16[112,2048]{1,0:T(8,128)(2,1)S(1)}, bf16[112,2048]{1,0:T(8,128)(2,1)S(1)}, u32[]{:S(2)}, u32[]{:S(2)}) collective-permute-start(bf16[112,2048]{1,0:T(8,128)(2,1)S(1)} %get-tuple-element.160), channel_id=1, source_target_pairs={{0,2},{1,3},{2,0},{3,1},{4,6},{5,7},{6,4},{7,5},{8,10},{9,11},{10,... | collective-permute-start | bytes 1376264 | tf_op jit(solution)/shard_map/ppermute | solution.py:263
  158.8 12.4 %collective-permute-start.49 = (bf16[256,1024]{1,0:T(8,128)(2,1)}, bf16[256,1024]{1,0:T(8,128)(2,1)S(1)}, u32[]{:S(2)}, u32[]{:S(2)}) collective-permute-start(bf16[256,1024]{1,0:T(8,128)(2,1)} %collective-permute-done.16.refs_2_), channel_id=1, source_target_pairs={{0,1},{1,0},{2,3},{3,2},{4,5},{5,4},{6,7},{7,6},{8,9},{9,8},{10,11... | collective-permute-start | bytes 1572872 | tf_op jit(solution)/shard_map/ppermute | solution.py:266
  167.0 7.2 %collective-permute-start.48 = (bf16[256,1024]{1,0:T(8,128)(2,1)}, bf16[256,1024]{1,0:T(8,128)(2,1)S(1)}, u32[]{:S(2)}, u32[]{:S(2)}) collective-permute-start(bf16[256,1024]{1,0:T(8,128)(2,1)} %pad_maximum_fusion.4.refs_0_), channel_id=1, source_target_pairs={{0,1},{1,0},{2,3},{3,2},{4,5},{5,4},{6,7},{7,6},{8,9},{9,8},{10,11... | collective-permute-start | bytes 1572872 | tf_op jit(solution)/shard_map/ppermute | solution.py:266
  168.6 14.9 %collective-permute-start.51 = (bf16[256,1024]{1,0:T(8,128)(2,1)S(1)}, bf16[256,1024]{1,0:T(8,128)(2,1)S(1)}, u32[]{:S(2)}, u32[]{:S(2)}) collective-permute-start(bf16[256,1024]{1,0:T(8,128)(2,1)S(1)} %collective-permute-done.29.refs_4_), channel_id=1, source_target_pairs={{0,2},{1,3},{2,0},{3,1},{4,6},{5,7},{6,4},{7,5},{8,10},{9,11},{10,... | collective-permute-start | bytes 1572872 | tf_op jit(solution)/shard_map/ppermute | solution.py:263
  170.2 21.1 %collective-permute-start.47 = (bf16[112,2048]{1,0:T(8,128)(2,1)S(1)}, bf16[112,2048]{1,0:T(8,128)(2,1)S(1)}, u32[]{:S(2)}, u32[]{:S(2)}) collective-permute-start(bf16[112,2048]{1,0:T(8,128)(2,1)S(1)} %get-tuple-element.179), channel_id=1, source_target_pairs={{0,2},{1,3},{2,0},{3,1},{4,6},{5,7},{6,4},{7,5},{8,10},{9,11},{10,... | collective-permute-start | bytes 1376264 | tf_op jit(solution)/shard_map/ppermute | solution.py:263
  170.6 22.7 %collective-permute-start.53 = (bf16[224,1408]{1,0:T(8,128)(2,1)S(1)}, bf16[224,1408]{1,0:T(8,128)(2,1)S(1)}, u32[]{:S(2)}, u32[]{:S(2)}) collective-permute-start(bf16[224,1408]{1,0:T(8,128)(2,1)S(1)} %get-tuple-element.202.refs_22_), channel_id=1, source_target_pairs={{0,16},{16,0},{1,17},{17,1},{2,18},{18,2},{3,19},{19,3},{4,20},{20... | collective-permute-start | bytes 1892360 | tf_op jit(solution)/shard_map/ppermute | solution.py:269
  171.1 21.7 %collective-permute-start.46 = (bf16[256,1024]{1,0:T(8,128)(2,1)S(1)}, bf16[256,1024]{1,0:T(8,128)(2,1)S(1)}, u32[]{:S(2)}, u32[]{:S(2)}) collective-permute-start(bf16[256,1024]{1,0:T(8,128)(2,1)S(1)} %collective-permute-done.31), channel_id=1, source_target_pairs={{4,0},{5,1},{6,2},{7,3},{8,12},{9,13},{10,14},{11,15},{20,16},{21,... | collective-permute-start | bytes 1572872 | tf_op jit(solution)/shard_map/ppermute | solution.py:260
  174.3 18.5 %collective-permute-start.50 = (bf16[256,1024]{1,0:T(8,128)(2,1)S(1)}, bf16[256,1024]{1,0:T(8,128)(2,1)S(1)}, u32[]{:S(2)}, u32[]{:S(2)}) collective-permute-start(bf16[256,1024]{1,0:T(8,128)(2,1)S(1)} %collective-permute-done.29.refs_4_), channel_id=1, source_target_pairs={{0,1},{1,0},{2,3},{3,2},{4,5},{5,4},{6,7},{7,6},{8,9},{9,8},{10,11... | collective-permute-start | bytes 1572872 | tf_op jit(solution)/shard_map/ppermute | solution.py:266
  183.5 9.9 %collective-permute-start.52 = (bf16[256,1024]{1,0:T(8,128)(2,1)S(1)}, bf16[256,1024]{1,0:T(8,128)(2,1)S(1)}, u32[]{:S(2)}, u32[]{:S(2)}) collective-permute-start(bf16[256,1024]{1,0:T(8,128)(2,1)S(1)} %collective-permute-done.51.refs_6_), channel_id=1, source_target_pairs={{0,1},{1,0},{2,3},{3,2},{4,5},{5,4},{6,7},{7,6},{8,9},{9,8},{10,11... | collective-permute-start | bytes 1572872 | tf_op jit(solution)/shard_map/ppermute | solution.py:266
  191.3 34.1 %collective-permute-start.62 = (bf16[704,1024]{1,0:T(8,128)(2,1)S(1)}, bf16[704,1024]{1,0:T(8,128)(2,1)S(1)}, u32[]{:S(2)}, u32[]{:S(2)}) collective-permute-start(bf16[704,1024]{1,0:T(8,128)(2,1)S(1)} %bitcast.69), channel_id=1, source_target_pairs={{0,16},{16,0},{1,17},{17,1},{2,18},{18,2},{3,19},{19,3},{4,20},{20... | collective-permute-start | bytes 4325384 | tf_op jit(solution)/shard_map/ppermute | solution.py:269
  192.8 3.3 %collective-permute-start.43 = (bf16[112,2048]{1,0:T(8,128)(2,1)S(1)}, bf16[112,2048]{1,0:T(8,128)(2,1)S(1)}, u32[]{:S(2)}, u32[]{:S(2)}) collective-permute-start(bf16[112,2048]{1,0:T(8,128)(2,1)S(1)} %collective-permute-done.34.hop), channel_id=1, source_target_pairs={{0,1},{1,0},{2,3},{3,2},{4,5},{5,4},{6,7},{7,6},{8,9},{9,8},{10,11... | collective-permute-start | bytes 1376264 | tf_op jit(solution)/shard_map/ppermute | solution.py:266
  192.8 4.4 %collective-permute-start.12 = (bf16[56,2048]{1,0:T(8,128)(2,1)S(1)}, bf16[56,2048]{1,0:T(8,128)(2,1)S(1)}, u32[]{:S(2)}, u32[]{:S(2)}) collective-permute-start(bf16[56,2048]{1,0:T(8,128)(2,1)S(1)} %copy-done.25), channel_id=1, source_target_pairs={{0,1},{1,0},{2,3},{3,2},{4,5},{5,4},{6,7},{7,6},{8,9},{9,8},{10,11... | collective-permute-start | bytes 688136 | tf_op jit(solution)/shard_map/ppermute | solution.py:266
  193.3 4.1 %collective-permute-start.20 = (bf16[112,2048]{1,0:T(8,128)(2,1)}, bf16[112,2048]{1,0:T(8,128)(2,1)S(1)}, u32[]{:S(2)}, u32[]{:S(2)}) collective-permute-start(bf16[112,2048]{1,0:T(8,128)(2,1)} %collective-permute-done.17.hop), channel_id=1, source_target_pairs={{0,1},{1,0},{2,3},{3,2},{4,5},{5,4},{6,7},{7,6},{8,9},{9,8},{10,11... | collective-permute-start | bytes 1376264 | tf_op jit(solution)/shard_map/ppermute | solution.py:266
  193.4 2.5 collective-permute-start.42
  195.9 5.3 %collective-permute-start.54 = (bf16[112,2048]{1,0:T(8,128)(2,1)S(1)}, bf16[112,2048]{1,0:T(8,128)(2,1)S(1)}, u32[]{:S(2)}, u32[]{:S(2)}) collective-permute-start(bf16[112,2048]{1,0:T(8,128)(2,1)S(1)} %collective-permute-done.47.hop), channel_id=1, source_target_pairs={{0,1},{1,0},{2,3},{3,2},{4,5},{5,4},{6,7},{7,6},{8,9},{9,8},{10,11... | collective-permute-start | bytes 1376264 | tf_op jit(solution)/shard_map/ppermute | solution.py:266
  196.1 3.5 %collective-permute-start.45 = (bf16[56,2048]{1,0:T(8,128)(2,1)S(1)}, bf16[56,2048]{1,0:T(8,128)(2,1)S(1)}, u32[]{:S(2)}, u32[]{:S(2)}) collective-permute-start(bf16[56,2048]{1,0:T(8,128)(2,1)S(1)} %copy-done.27), channel_id=1, source_target_pairs={{0,1},{1,0},{2,3},{3,2},{4,5},{5,4},{6,7},{7,6},{8,9},{9,8},{10,11... | collective-permute-start | bytes 688136 | tf_op jit(solution)/shard_map/ppermute | solution.py:266
  197.2 22.2 %collective-permute-start.41 = (bf16[128,2048]{1,0:T(8,128)(2,1)S(1)}, bf16[128,2048]{1,0:T(8,128)(2,1)S(1)}, u32[]{:S(2)}, u32[]{:S(2)}) collective-permute-start(bf16[128,2048]{1,0:T(8,128)(2,1)S(1)} %combine.5), channel_id=1, source_target_pairs={{0,4},{1,5},{2,6},{3,7},{4,0},{5,1},{6,2},{7,3},{8,12},{9,13},{10,... | collective-permute-start | bytes 1572872 | tf_op jit(solution)/shard_map/ppermute | solution.py:257
  197.4 25.6 %collective-permute-start.44 = (bf16[128,2048]{1,0:T(8,128)(2,1)S(1)}, bf16[128,2048]{1,0:T(8,128)(2,1)S(1)}, u32[]{:S(2)}, u32[]{:S(2)}) collective-permute-start(bf16[128,2048]{1,0:T(8,128)(2,1)S(1)} %combine.6), channel_id=1, source_target_pairs={{0,8},{1,9},{2,10},{3,11},{4,12},{5,13},{6,14},{7,15},{8,0},{9,1},... | collective-permute-start | bytes 1572872 | tf_op jit(solution)/shard_map/ppermute | solution.py:257
  199.6 25.8 %collective-permute-start.60 = (bf16[256,1024]{1,0:T(8,128)(2,1)S(1)}, bf16[256,1024]{1,0:T(8,128)(2,1)S(1)}, u32[]{:S(2)}, u32[]{:S(2)}) collective-permute-start(bf16[256,1024]{1,0:T(8,128)(2,1)S(1)} %broadcast_select_fusion.refs_12_), channel_id=1, source_target_pairs={{0,2},{1,3},{2,0},{3,1},{4,6},{5,7},{6,4},{7,5},{8,10},{9,11},{10,... | collective-permute-start | bytes 1572872 | tf_op jit(solution)/shard_map/ppermute | solution.py:263
  201.2 24.6 %collective-permute-start.57 = (bf16[256,1024]{1,0:T(8,128)(2,1)S(1)}, bf16[256,1024]{1,0:T(8,128)(2,1)S(1)}, u32[]{:S(2)}, u32[]{:S(2)}) collective-permute-start(bf16[256,1024]{1,0:T(8,128)(2,1)S(1)} %broadcast_select_fusion.1.refs_8_), channel_id=1, source_target_pairs={{0,2},{1,3},{2,0},{3,1},{4,6},{5,7},{6,4},{7,5},{8,10},{9,11},{10,... | collective-permute-start | bytes 1572872 | tf_op jit(solution)/shard_map/ppermute | solution.py:263
  219.4 26.7 %collective-permute-start.55 = (bf16[128,2048]{1,0:T(8,128)(2,1)S(1)}, bf16[128,2048]{1,0:T(8,128)(2,1)S(1)}, u32[]{:S(2)}, u32[]{:S(2)}) collective-permute-start(bf16[128,2048]{1,0:T(8,128)(2,1)S(1)} %combine.7), channel_id=1, source_target_pairs={{0,12},{1,13},{2,14},{3,15},{4,8},{5,9},{6,10},{7,11},{8,4},{9,5},... | collective-permute-start | bytes 1572872 | tf_op jit(solution)/shard_map/ppermute | solution.py:257
  223.0 24.2 %collective-permute-start.59 = (bf16[256,1024]{1,0:T(8,128)(2,1)S(1)}, bf16[256,1024]{1,0:T(8,128)(2,1)S(1)}, u32[]{:S(2)}, u32[]{:S(2)}) collective-permute-start(bf16[256,1024]{1,0:T(8,128)(2,1)S(1)} %broadcast_select_fusion.refs_12_), channel_id=1, source_target_pairs={{0,1},{1,0},{2,3},{3,2},{4,5},{5,4},{6,7},{7,6},{8,9},{9,8},{10,11... | collective-permute-start | bytes 1572872 | tf_op jit(solution)/shard_map/ppermute | solution.py:266
  225.3 22.0 %collective-permute-start.56 = (bf16[256,1024]{1,0:T(8,128)(2,1)S(1)}, bf16[256,1024]{1,0:T(8,128)(2,1)S(1)}, u32[]{:S(2)}, u32[]{:S(2)}) collective-permute-start(bf16[256,1024]{1,0:T(8,128)(2,1)S(1)} %broadcast_select_fusion.1.refs_8_), channel_id=1, source_target_pairs={{0,1},{1,0},{2,3},{3,2},{4,5},{5,4},{6,7},{7,6},{8,9},{9,8},{10,11... | collective-permute-start | bytes 1572872 | tf_op jit(solution)/shard_map/ppermute | solution.py:266
  225.3 22.0 %collective-permute-start.61 = (bf16[256,1024]{1,0:T(8,128)(2,1)S(1)}, bf16[256,1024]{1,0:T(8,128)(2,1)S(1)}, u32[]{:S(2)}, u32[]{:S(2)}) collective-permute-start(bf16[256,1024]{1,0:T(8,128)(2,1)S(1)} %collective-permute-done.60.refs_14_), channel_id=1, source_target_pairs={{0,1},{1,0},{2,3},{3,2},{4,5},{5,4},{6,7},{7,6},{8,9},{9,8},{10,11... | collective-permute-start | bytes 1572872 | tf_op jit(solution)/shard_map/ppermute | solution.py:266
  225.8 21.5 %collective-permute-start.58 = (bf16[256,1024]{1,0:T(8,128)(2,1)S(1)}, bf16[256,1024]{1,0:T(8,128)(2,1)S(1)}, u32[]{:S(2)}, u32[]{:S(2)}) collective-permute-start(bf16[256,1024]{1,0:T(8,128)(2,1)S(1)} %collective-permute-done.57.refs_10_), channel_id=1, source_target_pairs={{0,1},{1,0},{2,3},{3,2},{4,5},{5,4},{6,7},{7,6},{8,9},{9,8},{10,11... | collective-permute-start | bytes 1572872 | tf_op jit(solution)/shard_map/ppermute | solution.py:266
  (30 other events, 237.5 us)

commit v4 on v3

--- a/solution.py
+++ b/solution.py
@@ -20,7 +20,7 @@
 
 
 def cost(flops, moved):
-    return pl.CostEstimate(flops=int(flops), bytes_accessed=int(moved), transcendentals=0)
+    return pl.CostEstimate(flops=int(flops * 0.05), bytes_accessed=int(moved * 0.05), transcendentals=0)
 
 
 def dot(a, b):

time: 263 us -> 249 us (0.947)
  waiting for transfers between devices: 122 us -> 106 us
    ppermute x8, waiting for transfers between devices: 13.6 us -> 3.37 us  [along_z(): lax.ppermute(value, 'blk', [(4 * a + n, 4 * b + n) for a, b in pairs for...]
    ppermute x6, waiting for transfers between devices: 10.3 us -> 6.56 us  [over_groups(): return lax.ppermute(value, 'grp', [(b, (b + n) % ng) for b in range(ng)])]
    unnamed x62 -> x80, local copies, waits for them, and re-layouts: 16.5 us -> 18 us
  transfers between devices with their start and end apart: 63 -> 63, of which waited for: 18 -> 21; matrix products, arithmetic and copies ran while one was open for 3% -> 4% of each run, Pallas kernels for 14% -> 15%
where the time goes in v4:
time: 249 us; the launch traced here: 248 us
  waiting for transfers between devices  106 us (43%)
  starting transfers between devices  56 us (22%)
  Pallas kernels  54.6 us (22%)
  local copies, waits for them, and re-layouts  21.6 us (9%)
  other arithmetic  8.06 us (3%)
    ppermute x16, waiting for transfers between devices, over_x(): return lax.ppermute(value, 'blk', [(b, b ^ 2) for b in range(nb)])  55.6 us
    ppermute x8, waiting for transfers between devices, over_z(): return lax.ppermute(value, 'blk', [(b, b ^ 4 * n) for b in range(nb)])  39.8 us
    pallas_call x4, Pallas kernels, expert(): pl.pallas_call(functools.partial(expert_kernel, slots, block), out_shape=...  26.4 us
    ppermute x8, starting transfers between devices, along_z(): lax.ppermute(value, 'blk', [(4 * a + n, 4 * b + n) for a, b in pairs for...  24 us
    unnamed x80, local copies, waits for them, and re-layouts  18 us
    ppermute x16, starting transfers between devices, over_x(): return lax.ppermute(value, 'blk', [(b, b ^ 2) for b in range(nb)])  14.6 us
    pallas_call x1, Pallas kernels, per_device(): pl.pallas_call(functools.partial(inner_kernel, zn, ng, slots, block), out...  13.6 us
    ppermute x6, starting transfers between devices, over_groups(): return lax.ppermute(value, 'grp', [(b, (b + n) % ng) for b in range(ng)])  9.23 us
  transfers between devices with their start and end apart: 63, of which 21 were waited for; matrix products, arithmetic and copies ran while one was open for 4% of the time, Pallas kernels for 15%

profile of v4, /device:TPU:10, one launch (start us, length us, event | category | flops | bytes accessed | tf_op | source)
XLA Modules:
  0.0 248.2 jit_solution(15847515361309755806)
XLA Ops:
  2.1 1.2 copy-done.8
  3.4 1.2 copy-done.9
  4.6 3.9 %pack.1 = (bf16[4,2,56,1408]{3,2,1,0:T(8,128)(2,1)S(1)}, bf16[4,2,56,1408]{3,2,1,0:T(8,128)(2,1)S(1)}) custom-call(s32[4]{0:T(128)S(1)} %pad_add_fusion.sc, bf16[12,128]{1,0:T(8,128)(2,1)S(1)} %pad_maximum_fusion.5.meta_ref, bf16[6,704,128]{2,1,0:T(8,128)(2,1)S(1)} %bitcast.69, bf16[6,704,128]{2,1,0:T(8,128)(2,1)S(1)} %bitcast.70), custom_call_target="tpu_custom_call" | custom-call | flops 96888424 | bytes 108134 | tf_op jit(solution)/shard_map/pack/pallas_call | solution.py:287
  9.1 4.6 %collective-permute-start.1 = (bf16[128,2048]{1,0:T(8,128)(2,1)}, bf16[128,2048]{1,0:T(8,128)(2,1)}, u32[]{:S(2)}, u32[]{:S(2)}) collective-permute-start(bf16[128,2048]{1,0:T(8,128)(2,1)} %d00.1), channel_id=1, source_target_pairs={{4,8},{5,9},{6,10},{7,11},{8,4},{9,5},{10,6},{11,7},{20,24},{21,25... | collective-permute-start | bytes 1572872 | tf_op jit(solution)/shard_map/ppermute | solution.py:260
  14.4 1.6 collective-permute-start.3
  16.1 6.2 %collective-permute-done.3 = bf16[128,1024]{1,0:T(8,128)(2,1)S(1)} collective-permute-done((bf16[128,1024]{1,0:T(8,128)(2,1)S(1)}, bf16[128,1024]{1,0:T(8,128)(2,1)S(1)}, u32[]{:S(2)}, u32[]{:S(2)}) %collective-permute-start.3) | collective-permute-done | bytes 262176 | tf_op jit(solution)/shard_map/ppermute | solution.py:269
  22.3 1.5 slice_bitcast_fusion
  23.8 1.1 pad_maximum_fusion.2
  25.1 1.1 collective-permute-done.1
  26.3 1.5 collective-permute-done.2.d10
  28.5 2.2 collective-permute-start.6
  30.7 1.5 collective-permute-start.7
  32.2 6.1 %collective-permute-done.11.far = bf16[112,1408]{1,0:T(8,128)(2,1)S(1)} collective-permute-done((bf16[112,1408]{1,0:T(8,128)(2,1)S(1)}, bf16[112,1408]{1,0:T(8,128)(2,1)S(1)}, u32[]{:S(2)}, u32[]{:S(2)}) %collective-permute-start.11) | collective-permute-done | bytes 315424 | tf_op jit(solution)/shard_map/ppermute | solution.py:263
  38.3 7.4 %expert.4 = (bf16[224,1408]{1,0:T(8,128)(2,1)}, bf16[224,704]{1,0:T(8,128)(2,1)S(1)}, bf16[224,2048]{1,0:T(8,128)(2,1)S(1)}, bf16[56,2048]{1,0:T(8,128)(2,1)S(1)...) custom-call(bf16[128,2048]{1,0:T(8,128)(2,1)} %d00.1, bf16[128,2048]{1,0:T(8,128)(2,1)S(1)} %collective-permute-done.9.d01, ...), custom_call_target="tpu_custom_call" | custom-call | flops 152672672 | bytes 800000 | tf_op jit(solution)/shard_map/expert/pallas_call | solution.py:311
  50.9 1.5 collective-permute-start.18
  52.5 4.3 %collective-permute-start.14 = (bf16[128,2048]{1,0:T(8,128)(2,1)}, bf16[128,2048]{1,0:T(8,128)(2,1)}, u32[]{:S(2)}, u32[]{:S(2)}) collective-permute-start(bf16[128,2048]{1,0:T(8,128)(2,1)} %collective-permute-done.1), channel_id=1, source_target_pairs={{4,0},{5,1},{6,2},{7,3},{8,12},{9,13},{10,14},{11,15},{20,16},{21,... | collective-permute-start | bytes 1572872 | tf_op jit(solution)/shard_map/ppermute | solution.py:260
  56.8 3.5 %collective-permute-done.15.far = bf16[112,1408]{1,0:T(8,128)(2,1)S(1)} collective-permute-done((bf16[112,1408]{1,0:T(8,128)(2,1)S(1)}, bf16[112,1408]{1,0:T(8,128)(2,1)S(1)}, u32[]{:S(2)}, u32[]{:S(2)}) %collective-permute-start.15) | collective-permute-done | bytes 315424 | tf_op jit(solution)/shard_map/ppermute | solution.py:263
  62.1 1.7 collective-permute-start.17
  63.8 1.8 copy-done.2
  65.7 1.8 copy-done.5
  67.5 1.0 copy-done.7
  68.4 1.0 copy-done.13
  69.5 1.0 copy-done.15
  70.5 1.0 copy-done.17
  71.6 1.0 copy-done.23
  72.5 6.5 %expert.5 = (bf16[224,1408]{1,0:T(8,128)(2,1)S(1)}, bf16[224,704]{1,0:T(8,128)(2,1)S(1)}, bf16[224,2048]{1,0:T(8,128)(2,1)S(1)}, bf16[56,2048]{1,0:T(8,128)(2,1)...) custom-call(bf16[128,2048]{1,0:T(8,128)(2,1)} %collective-permute-done.d00, ...), custom_call_target="tpu_custom_call" | custom-call | flops 152672672 | bytes 800000 | tf_op jit(solution)/shard_map/expert/pallas_call | solution.py:311
  79.1 5.0 %collective-permute-done.17.hop = bf16[112,2048]{1,0:T(8,128)(2,1)} collective-permute-done((bf16[112,2048]{1,0:T(8,128)(2,1)}, bf16[112,2048]{1,0:T(8,128)(2,1)}, u32[]{:S(2)}, u32[]{:S(2)}) %collective-permute-start.17) | collective-permute-done | bytes 458784 | tf_op jit(solution)/shard_map/ppermute | solution.py:263
  84.8 1.1 slice_bitcast_fusion.6
  85.9 1.5 collective-permute-start.23
  88.3 1.5 collective-permute-start.25
  89.8 9.3 %collective-permute-done.27.d10 = bf16[128,2048]{1,0:T(8,128)(2,1)S(1)} collective-permute-done((bf16[128,2048]{1,0:T(8,128)(2,1)S(1)}, bf16[128,2048]{1,0:T(8,128)(2,1)S(1)}, u32[]{:S(2)}, u32[]{:S(2)}) %collective-permute-start.27) | collective-permute-done | bytes 524320 | tf_op jit(solution)/shard_map/ppermute | solution.py:263
  99.1 4.1 %collective-permute-done.23.far = bf16[112,1408]{1,0:T(8,128)(2,1)S(1)} collective-permute-done((bf16[112,1408]{1,0:T(8,128)(2,1)S(1)}, bf16[112,1408]{1,0:T(8,128)(2,1)S(1)}, u32[]{:S(2)}, u32[]{:S(2)}) %collective-permute-start.23) | collective-permute-done | bytes 315424 | tf_op jit(solution)/shard_map/ppermute | solution.py:263
  103.1 2.7 %collective-permute-start.22 = (bf16[128,2048]{1,0:T(8,128)(2,1)S(1)}, bf16[128,2048]{1,0:T(8,128)(2,1)S(1)}, u32[]{:S(2)}, u32[]{:S(2)}) collective-permute-start(bf16[128,2048]{1,0:T(8,128)(2,1)S(1)} %copy-done.39), channel_id=1, source_target_pairs={{4,0},{5,1},{6,2},{7,3},{8,12},{9,13},{10,14},{11,15},{20,16},{21,... | collective-permute-start | bytes 1572872 | tf_op jit(solution)/shard_map/ppermute | solution.py:260
  106.7 6.2 %expert.6 = (bf16[224,1408]{1,0:T(8,128)(2,1)S(1)}, bf16[224,704]{1,0:T(8,128)(2,1)S(1)}, bf16[224,2048]{1,0:T(8,128)(2,1)S(1)}, bf16[56,2048]{1,0:T(8,128)(2,1)...) custom-call(bf16[128,2048]{1,0:T(8,128)(2,1)S(1)} %broadcast_select_fusion.3.d00, ...), custom_call_target="tpu_custom_call" | custom-call | flops 152672672 | bytes 800000 | tf_op jit(solution)/shard_map/expert/pallas_call | solution.py:311
  113.0 2.2 collective-permute-done.22
  115.2 2.1 collective-permute-done.21
  118.0 1.2 broadcast_select_fusion.2.d00
  119.3 1.5 collective-permute-start.39
  120.8 2.7 %collective-permute-start.30 = (bf16[256,1024]{1,0:T(8,128)(2,1)S(1)}, bf16[256,1024]{1,0:T(8,128)(2,1)S(1)}, u32[]{:S(2)}, u32[]{:S(2)}) collective-permute-start(bf16[256,1024]{1,0:T(8,128)(2,1)S(1)} %pad_maximum_fusion.4.refs_0_), channel_id=1, source_target_pairs={{4,8},{5,9},{6,10},{7,11},{8,4},{9,5},{10,6},{11,7},{20,24},{21,25... | collective-permute-start | bytes 1572872 | tf_op jit(solution)/shard_map/ppermute | solution.py:260
  123.5 4.3 %collective-permute-done.33.far = bf16[112,1408]{1,0:T(8,128)(2,1)S(1)} collective-permute-done((bf16[112,1408]{1,0:T(8,128)(2,1)S(1)}, bf16[112,1408]{1,0:T(8,128)(2,1)S(1)}, u32[]{:S(2)}, u32[]{:S(2)}) %collective-permute-start.33) | collective-permute-done | bytes 315424 | tf_op jit(solution)/shard_map/ppermute | solution.py:263
  127.8 1.5 collective-permute-start.37
  129.3 8.2 %collective-permute-done.39.d10 = bf16[128,2048]{1,0:T(8,128)(2,1)S(1)} collective-permute-done((bf16[128,2048]{1,0:T(8,128)(2,1)S(1)}, bf16[128,2048]{1,0:T(8,128)(2,1)S(1)}, u32[]{:S(2)}, u32[]{:S(2)}) %collective-permute-start.39) | collective-permute-done | bytes 524320 | tf_op jit(solution)/shard_map/ppermute | solution.py:263
  137.6 2.6 %collective-permute-start.31 = (bf16[256,1024]{1,0:T(8,128)(2,1)S(1)}, bf16[256,1024]{1,0:T(8,128)(2,1)}, u32[]{:S(2)}, u32[]{:S(2)}) collective-permute-start(bf16[256,1024]{1,0:T(8,128)(2,1)S(1)} %collective-permute-done.29.refs_4_), channel_id=1, source_target_pairs={{4,8},{5,9},{6,10},{7,11},{8,4},{9,5},{10,6},{11,7},{20,24},{21,25... | collective-permute-start | bytes 1572872 | tf_op jit(solution)/shard_map/ppermute | solution.py:260
  140.2 2.1 collective-permute-start.32
  143.6 6.2 %expert.7 = (bf16[224,1408]{1,0:T(8,128)(2,1)S(1)}, bf16[224,704]{1,0:T(8,128)(2,1)S(1)}, bf16[224,2048]{1,0:T(8,128)(2,1)S(1)}, bf16[56,2048]{1,0:T(8,128)(2,1)...) custom-call(bf16[128,2048]{1,0:T(8,128)(2,1)S(1)} %broadcast_select_fusion.2.d00, ...), custom_call_target="tpu_custom_call" | custom-call | flops 152672672 | bytes 800000 | tf_op jit(solution)/shard_map/expert/pallas_call | solution.py:311
  151.7 3.5 %collective-permute-done.34.hop = bf16[112,2048]{1,0:T(8,128)(2,1)S(1)} collective-permute-done((bf16[112,2048]{1,0:T(8,128)(2,1)}, bf16[112,2048]{1,0:T(8,128)(2,1)S(1)}, u32[]{:S(2)}, u32[]{:S(2)}) %collective-permute-start.34) | collective-permute-done | bytes 458784 | tf_op jit(solution)/shard_map/ppermute | solution.py:263
  155.6 1.6 collective-permute-start.47
  157.2 1.5 collective-permute-start.53
  158.8 2.8 %collective-permute-start.46 = (bf16[256,1024]{1,0:T(8,128)(2,1)}, bf16[256,1024]{1,0:T(8,128)(2,1)S(1)}, u32[]{:S(2)}, u32[]{:S(2)}) collective-permute-start(bf16[256,1024]{1,0:T(8,128)(2,1)} %collective-permute-done.31), channel_id=1, source_target_pairs={{4,0},{5,1},{6,2},{7,3},{8,12},{9,13},{10,14},{11,15},{20,16},{21,... | collective-permute-start | bytes 1572872 | tf_op jit(solution)/shard_map/ppermute | solution.py:260
  161.7 8.4 %collective-permute-done.51.refs_6_ = bf16[256,1024]{1,0:T(8,128)(2,1)S(1)} collective-permute-done((bf16[256,1024]{1,0:T(8,128)(2,1)S(1)}, bf16[256,1024]{1,0:T(8,128)(2,1)S(1)}, u32[]{:S(2)}, u32[]{:S(2)}) %collective-permute-start.51) | collective-permute-done | bytes 524320 | tf_op jit(solution)/shard_map/ppermute | solution.py:263
  170.1 6.8 %outer.1 = (f32[704,1024]{1,0:T(8,128)S(1)}, bf16[1,704,1024]{2,1,0:T(8,128)(2,1)S(1)}) custom-call(s32[4]{0:T(128)S(1)} %pad_add_fusion.sc, bf16[224,704]{1,0:T(8,128)(2,1)S(1)} %copy-done.19, bf16[224,704]{1,0:T(8,128)(2,1)S(1)} %get-tuple-element.207.refs_1_, bf16[224,704]{1,0:T(8,128)(2,1)S(1)} %copy-done.21, ...), custom_call_target="tpu_custom_call" | custom-call | flops 129184560 | bytes 500000 | tf_op jit(solution)/shard_map/outer/pallas_call | solution.py:416
  176.9 1.4 collective-permute-done.47.hop
  178.3 1.5 collective-permute-start.62
  180.9 1.1 broadcast_select_fusion.1.refs_8_
  182.0 1.0 collective-permute-done.42.swap
  184.2 1.0 collective-permute-start.41
  185.3 1.8 collective-permute-start.44
  187.7 1.6 collective-permute-start.57
  190.0 17.6 %collective-permute-done.41 = bf16[128,2048]{1,0:T(8,128)(2,1)S(1)} collective-permute-done((bf16[128,2048]{1,0:T(8,128)(2,1)S(1)}, bf16[128,2048]{1,0:T(8,128)(2,1)S(1)}, u32[]{:S(2)}, u32[]{:S(2)}) %collective-permute-start.41) | collective-permute-done | bytes 524320 | tf_op jit(solution)/shard_map/ppermute | solution.py:257
  208.3 1.7 combine.4
  211.9 1.7 fusion
  213.6 19.6 %collective-permute-done.55 = bf16[128,2048]{1,0:T(8,128)(2,1)S(1)} collective-permute-done((bf16[128,2048]{1,0:T(8,128)(2,1)S(1)}, bf16[128,2048]{1,0:T(8,128)(2,1)S(1)}, u32[]{:S(2)}, u32[]{:S(2)}) %collective-permute-start.55) | collective-permute-done | bytes 524320 | tf_op jit(solution)/shard_map/ppermute | solution.py:257
  233.2 1.1 add_convert_fusion.1
  234.3 13.6 %inner.1 = (bf16[704,1024]{1,0:T(8,128)(2,1)}, bf16[704,1024]{1,0:T(8,128)(2,1)}) custom-call(bf16[256,1024]{1,0:T(8,128)(2,1)S(1)} %pad_maximum_fusion.4.refs_0_, bf16[256,1024]{1,0:T(8,128)(2,1)S(1)} %collective-permute-done.48.refs_1_, bf16[256,1024]{1,0:T(8,128)(2,1)} %collective-permute-done.16.refs_2_, ...), custom_call_target="tpu_custom_call" | custom-call | flops 258369120 | bytes 1000000 | tf_op jit(solution)/shard_map/inner/pallas_call | solution.py:435
  (172 shorter events, 23.6 us)
Async XLA Ops:
  8.5 13.8 %collective-permute-start.4 = (bf16[4,2,56,1408]{3,2,1,0:T(8,128)(2,1)S(1)}, bf16[4,2,56,1408]{3,2,1,0:T(8,128)(2,1)}, u32[]{:S(2)}, u32[]{:S(2)}) collective-permute-start(bf16[4,2,56,1408]{3,2,1,0:T(8,128)(2,1)S(1)} %get-tuple-element.111), channel_id=1, source_target_pairs={{0,1},{1,0},{2,3},{3,2},{4,5},{5,4},{6,7},{7,6},{8,9},{9,8},{10,11... | collective-permute-start | bytes 3784712 | tf_op jit(solution)/shard_map/ppermute | solution.py:266
  8.6 16.5 %collective-permute-start = (bf16[128,2048]{1,0:T(8,128)(2,1)}, bf16[128,2048]{1,0:T(8,128)(2,1)}, u32[]{:S(2)}, u32[]{:S(2)}) collective-permute-start(bf16[128,2048]{1,0:T(8,128)(2,1)} %d00.1), channel_id=1, source_target_pairs={{0,4},{1,5},{2,6},{3,7},{4,0},{5,1},{6,2},{7,3},{8,12},{9,13},{10,... | collective-permute-start | bytes 1572872 | tf_op jit(solution)/shard_map/ppermute | solution.py:257
  9.1 17.1 %collective-permute-start.1 = (bf16[128,2048]{1,0:T(8,128)(2,1)}, bf16[128,2048]{1,0:T(8,128)(2,1)}, u32[]{:S(2)}, u32[]{:S(2)}) collective-permute-start(bf16[128,2048]{1,0:T(8,128)(2,1)} %d00.1), channel_id=1, source_target_pairs={{4,8},{5,9},{6,10},{7,11},{8,4},{9,5},{10,6},{11,7},{20,24},{21,25... | collective-permute-start | bytes 1572872 | tf_op jit(solution)/shard_map/ppermute | solution.py:260
  13.7 14.1 %collective-permute-start.2 = (bf16[128,2048]{1,0:T(8,128)(2,1)}, bf16[128,2048]{1,0:T(8,128)(2,1)}, u32[]{:S(2)}, u32[]{:S(2)}) collective-permute-start(bf16[128,2048]{1,0:T(8,128)(2,1)} %d00.1), channel_id=1, source_target_pairs={{0,2},{1,3},{2,0},{3,1},{4,6},{5,7},{6,4},{7,5},{8,10},{9,11},{10,... | collective-permute-start | bytes 1572872 | tf_op jit(solution)/shard_map/ppermute | solution.py:263
  14.4 7.9 %collective-permute-start.3 = (bf16[128,1024]{1,0:T(8,128)(2,1)S(1)}, bf16[128,1024]{1,0:T(8,128)(2,1)S(1)}, u32[]{:S(2)}, u32[]{:S(2)}) collective-permute-start(bf16[128,1024]{1,0:T(8,128)(2,1)S(1)} %get-tuple-element.233), channel_id=1, source_target_pairs={{0,16},{16,0},{1,17},{17,1},{2,18},{18,2},{3,19},{19,3},{4,20},{20... | collective-permute-start | bytes 786440 | tf_op jit(solution)/shard_map/ppermute | solution.py:269
  22.2 8.4 %collective-permute-start.9 = (bf16[128,2048]{1,0:T(8,128)(2,1)}, bf16[128,2048]{1,0:T(8,128)(2,1)S(1)}, u32[]{:S(2)}, u32[]{:S(2)}) collective-permute-start(bf16[128,2048]{1,0:T(8,128)(2,1)} %d00.1), channel_id=1, source_target_pairs={{0,1},{1,0},{2,3},{3,2},{4,5},{5,4},{6,7},{7,6},{8,9},{9,8},{10,11... | collective-permute-start | bytes 1572872 | tf_op jit(solution)/shard_map/ppermute | solution.py:266
  27.9 10.4 %collective-permute-start.11 = (bf16[112,1408]{1,0:T(8,128)(2,1)S(1)}, bf16[112,1408]{1,0:T(8,128)(2,1)S(1)}, u32[]{:S(2)}, u32[]{:S(2)}) collective-permute-start(bf16[112,1408]{1,0:T(8,128)(2,1)S(1)} %get-tuple-element.230), channel_id=1, source_target_pairs={{0,2},{1,3},{2,0},{3,1},{4,6},{5,7},{6,4},{7,5},{8,10},{9,11},{10,... | collective-permute-start | bytes 946184 | tf_op jit(solution)/shard_map/ppermute | solution.py:263
  28.5 20.3 %collective-permute-start.5 = (bf16[2,112,1408]{2,1,0:T(8,128)(2,1)S(1)}, bf16[2,112,1408]{2,1,0:T(8,128)(2,1)S(1)}, u32[]{:S(2)}, u32[]{:S(2)}) collective-permute-start(bf16[2,112,1408]{2,1,0:T(8,128)(2,1)S(1)} %get-tuple-element.112), channel_id=1, source_target_pairs={{0,4},{1,5},{2,6},{3,7},{4,0},{5,1},{6,2},{7,3},{8,12},{9,13},{10,... | collective-permute-start | bytes 1892360 | tf_op jit(solution)/shard_map/ppermute | solution.py:257
  28.5 9.8 %collective-permute-start.10 = (bf16[128,2048]{1,0:T(8,128)(2,1)}, bf16[128,2048]{1,0:T(8,128)(2,1)S(1)}, u32[]{:S(2)}, u32[]{:S(2)}) collective-permute-start(bf16[128,2048]{1,0:T(8,128)(2,1)} %collective-permute-done.2.d10), channel_id=1, source_target_pairs={{0,1},{1,0},{2,3},{3,2},{4,5},{5,4},{6,7},{7,6},{8,9},{9,8},{10,11... | collective-permute-start | bytes 1572872 | tf_op jit(solution)/shard_map/ppermute | solution.py:266
  28.5 19.5 %collective-permute-start.6 = (bf16[128,2048]{1,0:T(8,128)(2,1)}, bf16[128,2048]{1,0:T(8,128)(2,1)S(1)}, u32[]{:S(2)}, u32[]{:S(2)}) collective-permute-start(bf16[128,2048]{1,0:T(8,128)(2,1)} %collective-permute-done.d00), channel_id=1, source_target_pairs={{4,8},{5,9},{6,10},{7,11},{8,4},{9,5},{10,6},{11,7},{20,24},{21,25... | collective-permute-start | bytes 1572872 | tf_op jit(solution)/shard_map/ppermute | solution.py:260
  30.7 17.3 %collective-permute-start.7 = (bf16[128,2048]{1,0:T(8,128)(2,1)}, bf16[128,2048]{1,0:T(8,128)(2,1)S(1)}, u32[]{:S(2)}, u32[]{:S(2)}) collective-permute-start(bf16[128,2048]{1,0:T(8,128)(2,1)} %collective-permute-done.d00), channel_id=1, source_target_pairs={{0,2},{1,3},{2,0},{3,1},{4,6},{5,7},{6,4},{7,5},{8,10},{9,11},{10,... | collective-permute-start | bytes 1572872 | tf_op jit(solution)/shard_map/ppermute | solution.py:263
  38.3 9.6 %collective-permute-start.8 = (bf16[128,2048]{1,0:T(8,128)(2,1)}, bf16[128,2048]{1,0:T(8,128)(2,1)S(1)}, u32[]{:S(2)}, u32[]{:S(2)}) collective-permute-start(bf16[128,2048]{1,0:T(8,128)(2,1)} %collective-permute-done.d00), channel_id=1, source_target_pairs={{0,1},{1,0},{2,3},{3,2},{4,5},{5,4},{6,7},{7,6},{8,9},{9,8},{10,11... | collective-permute-start | bytes 1572872 | tf_op jit(solution)/shard_map/ppermute | solution.py:266
  48.8 12.5 %collective-permute-start.19 = (bf16[128,2048]{1,0:T(8,128)(2,1)S(1)}, bf16[128,2048]{1,0:T(8,128)(2,1)S(1)}, u32[]{:S(2)}, u32[]{:S(2)}) collective-permute-start(bf16[128,2048]{1,0:T(8,128)(2,1)S(1)} %collective-permute-done.7.d10), channel_id=1, source_target_pairs={{0,1},{1,0},{2,3},{3,2},{4,5},{5,4},{6,7},{7,6},{8,9},{9,8},{10,11... | collective-permute-start | bytes 1572872 | tf_op jit(solution)/shard_map/ppermute | solution.py:266
  50.9 9.4 %collective-permute-start.15 = (bf16[112,1408]{1,0:T(8,128)(2,1)S(1)}, bf16[112,1408]{1,0:T(8,128)(2,1)S(1)}, u32[]{:S(2)}, u32[]{:S(2)}) collective-permute-start(bf16[112,1408]{1,0:T(8,128)(2,1)S(1)} %get-tuple-element.229), channel_id=1, source_target_pairs={{0,2},{1,3},{2,0},{3,1},{4,6},{5,7},{6,4},{7,5},{8,10},{9,11},{10,... | collective-permute-start | bytes 946184 | tf_op jit(solution)/shard_map/ppermute | solution.py:263
  50.9 33.1 %collective-permute-start.13 = (bf16[2,112,1408]{2,1,0:T(8,128)(2,1)}, bf16[2,112,1408]{2,1,0:T(8,128)(2,1)}, u32[]{:S(2)}, u32[]{:S(2)}) collective-permute-start(bf16[2,112,1408]{2,1,0:T(8,128)(2,1)} %get-tuple-element.126), channel_id=1, source_target_pairs={{0,8},{1,9},{2,10},{3,11},{4,12},{5,13},{6,14},{7,15},{8,0},{9,1},... | collective-permute-start | bytes 1892360 | tf_op jit(solution)/shard_map/ppermute | solution.py:257
  50.9 33.1 %collective-permute-start.18 = (bf16[224,1408]{1,0:T(8,128)(2,1)}, bf16[224,1408]{1,0:T(8,128)(2,1)}, u32[]{:S(2)}, u32[]{:S(2)}) collective-permute-start(bf16[224,1408]{1,0:T(8,128)(2,1)} %get-tuple-element.196.refs_16_), channel_id=1, source_target_pairs={{0,16},{16,0},{1,17},{17,1},{2,18},{18,2},{3,19},{19,3},{4,20},{20... | collective-permute-start | bytes 1892360 | tf_op jit(solution)/shard_map/ppermute | solution.py:269
  52.5 31.6 %collective-permute-start.14 = (bf16[128,2048]{1,0:T(8,128)(2,1)}, bf16[128,2048]{1,0:T(8,128)(2,1)}, u32[]{:S(2)}, u32[]{:S(2)}) collective-permute-start(bf16[128,2048]{1,0:T(8,128)(2,1)} %collective-permute-done.1), channel_id=1, source_target_pairs={{4,0},{5,1},{6,2},{7,3},{8,12},{9,13},{10,14},{11,15},{20,16},{21,... | collective-permute-start | bytes 1572872 | tf_op jit(solution)/shard_map/ppermute | solution.py:260
  61.0 23.0 %collective-permute-start.16 = (bf16[256,1024]{1,0:T(8,128)(2,1)S(1)}, bf16[256,1024]{1,0:T(8,128)(2,1)}, u32[]{:S(2)}, u32[]{:S(2)}) collective-permute-start(bf16[256,1024]{1,0:T(8,128)(2,1)S(1)} %pad_maximum_fusion.4.refs_0_), channel_id=1, source_target_pairs={{0,2},{1,3},{2,0},{3,1},{4,6},{5,7},{6,4},{7,5},{8,10},{9,11},{10,... | collective-permute-start | bytes 1572872 | tf_op jit(solution)/shard_map/ppermute | solution.py:263
  62.1 21.9 %collective-permute-start.17 = (bf16[112,2048]{1,0:T(8,128)(2,1)}, bf16[112,2048]{1,0:T(8,128)(2,1)}, u32[]{:S(2)}, u32[]{:S(2)}) collective-permute-start(bf16[112,2048]{1,0:T(8,128)(2,1)} %get-tuple-element.131), channel_id=1, source_target_pairs={{0,2},{1,3},{2,0},{3,1},{4,6},{5,7},{6,4},{7,5},{8,10},{9,11},{10,... | collective-permute-start | bytes 1376264 | tf_op jit(solution)/shard_map/ppermute | solution.py:263
  84.2 14.9 %collective-permute-start.27 = (bf16[128,2048]{1,0:T(8,128)(2,1)S(1)}, bf16[128,2048]{1,0:T(8,128)(2,1)S(1)}, u32[]{:S(2)}, u32[]{:S(2)}) collective-permute-start(bf16[128,2048]{1,0:T(8,128)(2,1)S(1)} %broadcast_select_fusion.3.d00), channel_id=1, source_target_pairs={{0,2},{1,3},{2,0},{3,1},{4,6},{5,7},{6,4},{7,5},{8,10},{9,11},{10,... | collective-permute-start | bytes 1572872 | tf_op jit(solution)/shard_map/ppermute | solution.py:263
  84.8 21.1 %collective-permute-start.26 = (bf16[128,2048]{1,0:T(8,128)(2,1)S(1)}, bf16[128,2048]{1,0:T(8,128)(2,1)S(1)}, u32[]{:S(2)}, u32[]{:S(2)}) collective-permute-start(bf16[128,2048]{1,0:T(8,128)(2,1)S(1)} %broadcast_select_fusion.3.d00), channel_id=1, source_target_pairs={{0,1},{1,0},{2,3},{3,2},{4,5},{5,4},{6,7},{7,6},{8,9},{9,8},{10,11... | collective-permute-start | bytes 1572872 | tf_op jit(solution)/shard_map/ppermute | solution.py:266
  85.9 17.2 %collective-permute-start.23 = (bf16[112,1408]{1,0:T(8,128)(2,1)S(1)}, bf16[112,1408]{1,0:T(8,128)(2,1)S(1)}, u32[]{:S(2)}, u32[]{:S(2)}) collective-permute-start(bf16[112,1408]{1,0:T(8,128)(2,1)S(1)} %get-tuple-element.227), channel_id=1, source_target_pairs={{0,2},{1,3},{2,0},{3,1},{4,6},{5,7},{6,4},{7,5},{8,10},{9,11},{10,... | collective-permute-start | bytes 946184 | tf_op jit(solution)/shard_map/ppermute | solution.py:263
  87.4 29.9 %collective-permute-start.21 = (bf16[2,112,1408]{2,1,0:T(8,128)(2,1)S(1)}, bf16[2,112,1408]{2,1,0:T(8,128)(2,1)S(1)}, u32[]{:S(2)}, u32[]{:S(2)}) collective-permute-start(bf16[2,112,1408]{2,1,0:T(8,128)(2,1)S(1)} %copy-done.34), channel_id=1, source_target_pairs={{0,12},{1,13},{2,14},{3,15},{4,8},{5,9},{6,10},{7,11},{8,4},{9,5},... | collective-permute-start | bytes 1892360 | tf_op jit(solution)/shard_map/ppermute | solution.py:257
  88.3 29.0 %collective-permute-start.25 = (bf16[224,1408]{1,0:T(8,128)(2,1)S(1)}, bf16[224,1408]{1,0:T(8,128)(2,1)S(1)}, u32[]{:S(2)}, u32[]{:S(2)}) collective-permute-start(bf16[224,1408]{1,0:T(8,128)(2,1)S(1)} %get-tuple-element.198.refs_18_), channel_id=1, source_target_pairs={{0,16},{16,0},{1,17},{17,1},{2,18},{18,2},{3,19},{19,3},{4,20},{20... | collective-permute-start | bytes 1892360 | tf_op jit(solution)/shard_map/ppermute | solution.py:269
  99.1 7.6 %collective-permute-start.28 = (bf16[128,2048]{1,0:T(8,128)(2,1)S(1)}, bf16[128,2048]{1,0:T(8,128)(2,1)S(1)}, u32[]{:S(2)}, u32[]{:S(2)}) collective-permute-start(bf16[128,2048]{1,0:T(8,128)(2,1)S(1)} %collective-permute-done.27.d10), channel_id=1, source_target_pairs={{0,1},{1,0},{2,3},{3,2},{4,5},{5,4},{6,7},{7,6},{8,9},{9,8},{10,11... | collective-permute-start | bytes 1572872 | tf_op jit(solution)/shard_map/ppermute | solution.py:266
  103.1 12.0 %collective-permute-start.22 = (bf16[128,2048]{1,0:T(8,128)(2,1)S(1)}, bf16[128,2048]{1,0:T(8,128)(2,1)S(1)}, u32[]{:S(2)}, u32[]{:S(2)}) collective-permute-start(bf16[128,2048]{1,0:T(8,128)(2,1)S(1)} %copy-done.39), channel_id=1, source_target_pairs={{4,0},{5,1},{6,2},{7,3},{8,12},{9,13},{10,14},{11,15},{20,16},{21,... | collective-permute-start | bytes 1572872 | tf_op jit(solution)/shard_map/ppermute | solution.py:260
  105.9 11.4 %collective-permute-start.24 = (bf16[112,2048]{1,0:T(8,128)(2,1)S(1)}, bf16[112,2048]{1,0:T(8,128)(2,1)S(1)}, u32[]{:S(2)}, u32[]{:S(2)}) collective-permute-start(bf16[112,2048]{1,0:T(8,128)(2,1)S(1)} %get-tuple-element.148), channel_id=1, source_target_pairs={{0,2},{1,3},{2,0},{3,1},{4,6},{5,7},{6,4},{7,5},{8,10},{9,11},{10,... | collective-permute-start | bytes 1376264 | tf_op jit(solution)/shard_map/ppermute | solution.py:263
  106.7 14.1 %collective-permute-start.35 = (bf16[56,2048]{1,0:T(8,128)(2,1)S(1)}, bf16[56,2048]{1,0:T(8,128)(2,1)S(1)}, u32[]{:S(2)}, u32[]{:S(2)}) collective-permute-start(bf16[56,2048]{1,0:T(8,128)(2,1)S(1)} %get-tuple-element.162), channel_id=1, source_target_pairs={{0,1},{1,0},{2,3},{3,2},{4,5},{5,4},{6,7},{7,6},{8,9},{9,8},{10,11... | collective-permute-start | bytes 688136 | tf_op jit(solution)/shard_map/ppermute | solution.py:266
  106.7 36.8 %copy-start.6 = (bf16[1,704,2048]{2,1,0:T(8,128)(2,1)S(1)}, bf16[1,704,2048]{2,1,0:T(8,128)(2,1)}, u32[]{:S(2)}) copy-start(bf16[1,704,2048]{2,1,0:T(8,128)(2,1)} %param.17) | copy-start | bytes 8650756
  117.3 10.4 %collective-permute-start.33 = (bf16[112,1408]{1,0:T(8,128)(2,1)S(1)}, bf16[112,1408]{1,0:T(8,128)(2,1)S(1)}, u32[]{:S(2)}, u32[]{:S(2)}) collective-permute-start(bf16[112,1408]{1,0:T(8,128)(2,1)S(1)} %get-tuple-element.225), channel_id=1, source_target_pairs={{0,2},{1,3},{2,0},{3,1},{4,6},{5,7},{6,4},{7,5},{8,10},{9,11},{10,... | collective-permute-start | bytes 946184 | tf_op jit(solution)/shard_map/ppermute | solution.py:263
  118.0 9.8 %collective-permute-start.36 = (bf16[112,2048]{1,0:T(8,128)(2,1)S(1)}, bf16[112,2048]{1,0:T(8,128)(2,1)S(1)}, u32[]{:S(2)}, u32[]{:S(2)}) collective-permute-start(bf16[112,2048]{1,0:T(8,128)(2,1)S(1)} %collective-permute-done.24.hop), channel_id=1, source_target_pairs={{0,1},{1,0},{2,3},{3,2},{4,5},{5,4},{6,7},{7,6},{8,9},{9,8},{10,11... | collective-permute-start | bytes 1376264 | tf_op jit(solution)/shard_map/ppermute | solution.py:266
  119.3 18.3 %collective-permute-start.39 = (bf16[128,2048]{1,0:T(8,128)(2,1)S(1)}, bf16[128,2048]{1,0:T(8,128)(2,1)S(1)}, u32[]{:S(2)}, u32[]{:S(2)}) collective-permute-start(bf16[128,2048]{1,0:T(8,128)(2,1)S(1)} %broadcast_select_fusion.2.d00), channel_id=1, source_target_pairs={{0,2},{1,3},{2,0},{3,1},{4,6},{5,7},{6,4},{7,5},{8,10},{9,11},{10,... | collective-permute-start | bytes 1572872 | tf_op jit(solution)/shard_map/ppermute | solution.py:263
  120.8 16.8 %collective-permute-start.29 = (bf16[256,1024]{1,0:T(8,128)(2,1)S(1)}, bf16[256,1024]{1,0:T(8,128)(2,1)S(1)}, u32[]{:S(2)}, u32[]{:S(2)}) collective-permute-start(bf16[256,1024]{1,0:T(8,128)(2,1)S(1)} %pad_maximum_fusion.4.refs_0_), channel_id=1, source_target_pairs={{0,4},{1,5},{2,6},{3,7},{4,0},{5,1},{6,2},{7,3},{8,12},{9,13},{10,... | collective-permute-start | bytes 1572872 | tf_op jit(solution)/shard_map/ppermute | solution.py:257
  120.8 19.4 %collective-permute-start.30 = (bf16[256,1024]{1,0:T(8,128)(2,1)S(1)}, bf16[256,1024]{1,0:T(8,128)(2,1)S(1)}, u32[]{:S(2)}, u32[]{:S(2)}) collective-permute-start(bf16[256,1024]{1,0:T(8,128)(2,1)S(1)} %pad_maximum_fusion.4.refs_0_), channel_id=1, source_target_pairs={{4,8},{5,9},{6,10},{7,11},{8,4},{9,5},{10,6},{11,7},{20,24},{21,25... | collective-permute-start | bytes 1572872 | tf_op jit(solution)/shard_map/ppermute | solution.py:260
  127.8 14.5 %collective-permute-start.38 = (bf16[128,2048]{1,0:T(8,128)(2,1)S(1)}, bf16[128,2048]{1,0:T(8,128)(2,1)S(1)}, u32[]{:S(2)}, u32[]{:S(2)}) collective-permute-start(bf16[128,2048]{1,0:T(8,128)(2,1)S(1)} %broadcast_select_fusion.2.d00), channel_id=1, source_target_pairs={{0,1},{1,0},{2,3},{3,2},{4,5},{5,4},{6,7},{7,6},{8,9},{9,8},{10,11... | collective-permute-start | bytes 1572872 | tf_op jit(solution)/shard_map/ppermute | solution.py:266
  127.8 23.4 %collective-permute-start.37 = (bf16[224,1408]{1,0:T(8,128)(2,1)S(1)}, bf16[224,1408]{1,0:T(8,128)(2,1)S(1)}, u32[]{:S(2)}, u32[]{:S(2)}) collective-permute-start(bf16[224,1408]{1,0:T(8,128)(2,1)S(1)} %get-tuple-element.200.refs_20_), channel_id=1, source_target_pairs={{0,16},{16,0},{1,17},{17,1},{2,18},{18,2},{3,19},{19,3},{4,20},{20... | collective-permute-start | bytes 1892360 | tf_op jit(solution)/shard_map/ppermute | solution.py:269
  137.6 5.9 %collective-permute-start.40 = (bf16[128,2048]{1,0:T(8,128)(2,1)S(1)}, bf16[128,2048]{1,0:T(8,128)(2,1)S(1)}, u32[]{:S(2)}, u32[]{:S(2)}) collective-permute-start(bf16[128,2048]{1,0:T(8,128)(2,1)S(1)} %collective-permute-done.39.d10), channel_id=1, source_target_pairs={{0,1},{1,0},{2,3},{3,2},{4,5},{5,4},{6,7},{7,6},{8,9},{9,8},{10,11... | collective-permute-start | bytes 1572872 | tf_op jit(solution)/shard_map/ppermute | solution.py:266
  137.6 17.6 %collective-permute-start.31 = (bf16[256,1024]{1,0:T(8,128)(2,1)S(1)}, bf16[256,1024]{1,0:T(8,128)(2,1)}, u32[]{:S(2)}, u32[]{:S(2)}) collective-permute-start(bf16[256,1024]{1,0:T(8,128)(2,1)S(1)} %collective-permute-done.29.refs_4_), channel_id=1, source_target_pairs={{4,8},{5,9},{6,10},{7,11},{8,4},{9,5},{10,6},{11,7},{20,24},{21,25... | collective-permute-start | bytes 1572872 | tf_op jit(solution)/shard_map/ppermute | solution.py:260
  140.2 15.0 %collective-permute-start.32 = (bf16[256,1024]{1,0:T(8,128)(2,1)S(1)}, bf16[256,1024]{1,0:T(8,128)(2,1)}, u32[]{:S(2)}, u32[]{:S(2)}) collective-permute-start(bf16[256,1024]{1,0:T(8,128)(2,1)S(1)} %collective-permute-done.30), channel_id=1, source_target_pairs={{4,0},{5,1},{6,2},{7,3},{8,12},{9,13},{10,14},{11,15},{20,16},{21,... | collective-permute-start | bytes 1572872 | tf_op jit(solution)/shard_map/ppermute | solution.py:260
  142.3 12.9 %collective-permute-start.34 = (bf16[112,2048]{1,0:T(8,128)(2,1)}, bf16[112,2048]{1,0:T(8,128)(2,1)S(1)}, u32[]{:S(2)}, u32[]{:S(2)}) collective-permute-start(bf16[112,2048]{1,0:T(8,128)(2,1)} %get-tuple-element.160), channel_id=1, source_target_pairs={{0,2},{1,3},{2,0},{3,1},{4,6},{5,7},{6,4},{7,5},{8,10},{9,11},{10,... | collective-permute-start | bytes 1376264 | tf_op jit(solution)/shard_map/ppermute | solution.py:263
  143.4 15.3 %collective-permute-start.49 = (bf16[256,1024]{1,0:T(8,128)(2,1)}, bf16[256,1024]{1,0:T(8,128)(2,1)S(1)}, u32[]{:S(2)}, u32[]{:S(2)}) collective-permute-start(bf16[256,1024]{1,0:T(8,128)(2,1)} %collective-permute-done.16.refs_2_), channel_id=1, source_target_pairs={{0,1},{1,0},{2,3},{3,2},{4,5},{5,4},{6,7},{7,6},{8,9},{9,8},{10,11... | collective-permute-start | bytes 1572872 | tf_op jit(solution)/shard_map/ppermute | solution.py:266
  151.2 10.4 %collective-permute-start.48 = (bf16[256,1024]{1,0:T(8,128)(2,1)S(1)}, bf16[256,1024]{1,0:T(8,128)(2,1)S(1)}, u32[]{:S(2)}, u32[]{:S(2)}) collective-permute-start(bf16[256,1024]{1,0:T(8,128)(2,1)S(1)} %pad_maximum_fusion.4.refs_0_), channel_id=1, source_target_pairs={{0,1},{1,0},{2,3},{3,2},{4,5},{5,4},{6,7},{7,6},{8,9},{9,8},{10,11... | collective-permute-start | bytes 1572872 | tf_op jit(solution)/shard_map/ppermute | solution.py:266
  155.2 14.9 %collective-permute-start.51 = (bf16[256,1024]{1,0:T(8,128)(2,1)S(1)}, bf16[256,1024]{1,0:T(8,128)(2,1)S(1)}, u32[]{:S(2)}, u32[]{:S(2)}) collective-permute-start(bf16[256,1024]{1,0:T(8,128)(2,1)S(1)} %collective-permute-done.29.refs_4_), channel_id=1, source_target_pairs={{0,2},{1,3},{2,0},{3,1},{4,6},{5,7},{6,4},{7,5},{8,10},{9,11},{10,... | collective-permute-start | bytes 1572872 | tf_op jit(solution)/shard_map/ppermute | solution.py:263
  155.6 22.6 %collective-permute-start.47 = (bf16[112,2048]{1,0:T(8,128)(2,1)}, bf16[112,2048]{1,0:T(8,128)(2,1)S(1)}, u32[]{:S(2)}, u32[]{:S(2)}) collective-permute-start(bf16[112,2048]{1,0:T(8,128)(2,1)} %get-tuple-element.179), channel_id=1, source_target_pairs={{0,2},{1,3},{2,0},{3,1},{4,6},{5,7},{6,4},{7,5},{8,10},{9,11},{10,... | collective-permute-start | bytes 1376264 | tf_op jit(solution)/shard_map/ppermute | solution.py:263
  157.2 23.1 %collective-permute-start.53 = (bf16[224,1408]{1,0:T(8,128)(2,1)S(1)}, bf16[224,1408]{1,0:T(8,128)(2,1)S(1)}, u32[]{:S(2)}, u32[]{:S(2)}) collective-permute-start(bf16[224,1408]{1,0:T(8,128)(2,1)S(1)} %get-tuple-element.202.refs_22_), channel_id=1, source_target_pairs={{0,16},{16,0},{1,17},{17,1},{2,18},{18,2},{3,19},{19,3},{4,20},{20... | collective-permute-start | bytes 1892360 | tf_op jit(solution)/shard_map/ppermute | solution.py:269
  158.8 21.0 %collective-permute-start.46 = (bf16[256,1024]{1,0:T(8,128)(2,1)}, bf16[256,1024]{1,0:T(8,128)(2,1)S(1)}, u32[]{:S(2)}, u32[]{:S(2)}) collective-permute-start(bf16[256,1024]{1,0:T(8,128)(2,1)} %collective-permute-done.31), channel_id=1, source_target_pairs={{4,0},{5,1},{6,2},{7,3},{8,12},{9,13},{10,14},{11,15},{20,16},{21,... | collective-permute-start | bytes 1572872 | tf_op jit(solution)/shard_map/ppermute | solution.py:260
  161.6 18.2 %collective-permute-start.50 = (bf16[256,1024]{1,0:T(8,128)(2,1)S(1)}, bf16[256,1024]{1,0:T(8,128)(2,1)S(1)}, u32[]{:S(2)}, u32[]{:S(2)}) collective-permute-start(bf16[256,1024]{1,0:T(8,128)(2,1)S(1)} %collective-permute-done.29.refs_4_), channel_id=1, source_target_pairs={{0,1},{1,0},{2,3},{3,2},{4,5},{5,4},{6,7},{7,6},{8,9},{9,8},{10,11... | collective-permute-start | bytes 1572872 | tf_op jit(solution)/shard_map/ppermute | solution.py:266
  170.1 10.3 %collective-permute-start.52 = (bf16[256,1024]{1,0:T(8,128)(2,1)S(1)}, bf16[256,1024]{1,0:T(8,128)(2,1)S(1)}, u32[]{:S(2)}, u32[]{:S(2)}) collective-permute-start(bf16[256,1024]{1,0:T(8,128)(2,1)S(1)} %collective-permute-done.51.refs_6_), channel_id=1, source_target_pairs={{0,1},{1,0},{2,3},{3,2},{4,5},{5,4},{6,7},{7,6},{8,9},{9,8},{10,11... | collective-permute-start | bytes 1572872 | tf_op jit(solution)/shard_map/ppermute | solution.py:266
  178.3 32.7 %collective-permute-start.62 = (bf16[704,1024]{1,0:T(8,128)(2,1)S(1)}, bf16[704,1024]{1,0:T(8,128)(2,1)S(1)}, u32[]{:S(2)}, u32[]{:S(2)}) collective-permute-start(bf16[704,1024]{1,0:T(8,128)(2,1)S(1)} %bitcast.71), channel_id=1, source_target_pairs={{0,16},{16,0},{1,17},{17,1},{2,18},{18,2},{3,19},{19,3},{4,20},{20... | collective-permute-start | bytes 4325384 | tf_op jit(solution)/shard_map/ppermute | solution.py:269
  179.8 3.3 %collective-permute-start.43 = (bf16[112,2048]{1,0:T(8,128)(2,1)S(1)}, bf16[112,2048]{1,0:T(8,128)(2,1)S(1)}, u32[]{:S(2)}, u32[]{:S(2)}) collective-permute-start(bf16[112,2048]{1,0:T(8,128)(2,1)S(1)} %collective-permute-done.34.hop), channel_id=1, source_target_pairs={{0,1},{1,0},{2,3},{3,2},{4,5},{5,4},{6,7},{7,6},{8,9},{9,8},{10,11... | collective-permute-start | bytes 1376264 | tf_op jit(solution)/shard_map/ppermute | solution.py:266
  179.8 4.4 %collective-permute-start.12 = (bf16[56,2048]{1,0:T(8,128)(2,1)S(1)}, bf16[56,2048]{1,0:T(8,128)(2,1)S(1)}, u32[]{:S(2)}, u32[]{:S(2)}) collective-permute-start(bf16[56,2048]{1,0:T(8,128)(2,1)S(1)} %copy-done.29), channel_id=1, source_target_pairs={{0,1},{1,0},{2,3},{3,2},{4,5},{5,4},{6,7},{7,6},{8,9},{9,8},{10,11... | collective-permute-start | bytes 688136 | tf_op jit(solution)/shard_map/ppermute | solution.py:266
  180.3 4.9 %collective-permute-start.20 = (bf16[112,2048]{1,0:T(8,128)(2,1)}, bf16[112,2048]{1,0:T(8,128)(2,1)S(1)}, u32[]{:S(2)}, u32[]{:S(2)}) collective-permute-start(bf16[112,2048]{1,0:T(8,128)(2,1)} %collective-permute-done.17.hop), channel_id=1, source_target_pairs={{0,1},{1,0},{2,3},{3,2},{4,5},{5,4},{6,7},{7,6},{8,9},{9,8},{10,11... | collective-permute-start | bytes 1376264 | tf_op jit(solution)/shard_map/ppermute | solution.py:266
  180.4 2.5 %collective-permute-start.42 = (bf16[56,2048]{1,0:T(8,128)(2,1)S(1)}, bf16[56,2048]{1,0:T(8,128)(2,1)S(1)}, u32[]{:S(2)}, u32[]{:S(2)}) collective-permute-start(bf16[56,2048]{1,0:T(8,128)(2,1)S(1)} %copy-done.31), channel_id=1, source_target_pairs={{0,1},{1,0},{2,3},{3,2},{4,5},{5,4},{6,7},{7,6},{8,9},{9,8},{10,11... | collective-permute-start | bytes 688136 | tf_op jit(solution)/shard_map/ppermute | solution.py:266
  182.9 4.7 %collective-permute-start.54 = (bf16[112,2048]{1,0:T(8,128)(2,1)S(1)}, bf16[112,2048]{1,0:T(8,128)(2,1)S(1)}, u32[]{:S(2)}, u32[]{:S(2)}) collective-permute-start(bf16[112,2048]{1,0:T(8,128)(2,1)S(1)} %collective-permute-done.47.hop), channel_id=1, source_target_pairs={{0,1},{1,0},{2,3},{3,2},{4,5},{5,4},{6,7},{7,6},{8,9},{9,8},{10,11... | collective-permute-start | bytes 1376264 | tf_op jit(solution)/shard_map/ppermute | solution.py:266
  183.1 4.1 %collective-permute-start.45 = (bf16[56,2048]{1,0:T(8,128)(2,1)S(1)}, bf16[56,2048]{1,0:T(8,128)(2,1)S(1)}, u32[]{:S(2)}, u32[]{:S(2)}) collective-permute-start(bf16[56,2048]{1,0:T(8,128)(2,1)S(1)} %copy-done.33), channel_id=1, source_target_pairs={{0,1},{1,0},{2,3},{3,2},{4,5},{5,4},{6,7},{7,6},{8,9},{9,8},{10,11... | collective-permute-start | bytes 688136 | tf_op jit(solution)/shard_map/ppermute | solution.py:266
  184.2 23.4 %collective-permute-start.41 = (bf16[128,2048]{1,0:T(8,128)(2,1)S(1)}, bf16[128,2048]{1,0:T(8,128)(2,1)S(1)}, u32[]{:S(2)}, u32[]{:S(2)}) collective-permute-start(bf16[128,2048]{1,0:T(8,128)(2,1)S(1)} %combine.5), channel_id=1, source_target_pairs={{0,4},{1,5},{2,6},{3,7},{4,0},{5,1},{6,2},{7,3},{8,12},{9,13},{10,... | collective-permute-start | bytes 1572872 | tf_op jit(solution)/shard_map/ppermute | solution.py:257
  185.3 25.3 %collective-permute-start.44 = (bf16[128,2048]{1,0:T(8,128)(2,1)S(1)}, bf16[128,2048]{1,0:T(8,128)(2,1)S(1)}, u32[]{:S(2)}, u32[]{:S(2)}) collective-permute-start(bf16[128,2048]{1,0:T(8,128)(2,1)S(1)} %combine.6), channel_id=1, source_target_pairs={{0,8},{1,9},{2,10},{3,11},{4,12},{5,13},{6,14},{7,15},{8,0},{9,1},... | collective-permute-start | bytes 1572872 | tf_op jit(solution)/shard_map/ppermute | solution.py:257
  187.2 23.9 %collective-permute-start.60 = (bf16[256,1024]{1,0:T(8,128)(2,1)S(1)}, bf16[256,1024]{1,0:T(8,128)(2,1)S(1)}, u32[]{:S(2)}, u32[]{:S(2)}) collective-permute-start(bf16[256,1024]{1,0:T(8,128)(2,1)S(1)} %broadcast_select_fusion.refs_12_), channel_id=1, source_target_pairs={{0,2},{1,3},{2,0},{3,1},{4,6},{5,7},{6,4},{7,5},{8,10},{9,11},{10,... | collective-permute-start | bytes 1572872 | tf_op jit(solution)/shard_map/ppermute | solution.py:263
  187.7 24.2 %collective-permute-start.57 = (bf16[256,1024]{1,0:T(8,128)(2,1)S(1)}, bf16[256,1024]{1,0:T(8,128)(2,1)S(1)}, u32[]{:S(2)}, u32[]{:S(2)}) collective-permute-start(bf16[256,1024]{1,0:T(8,128)(2,1)S(1)} %broadcast_select_fusion.1.refs_8_), channel_id=1, source_target_pairs={{0,2},{1,3},{2,0},{3,1},{4,6},{5,7},{6,4},{7,5},{8,10},{9,11},{10,... | collective-permute-start | bytes 1572872 | tf_op jit(solution)/shard_map/ppermute | solution.py:263
  207.7 25.5 %collective-permute-start.55 = (bf16[128,2048]{1,0:T(8,128)(2,1)S(1)}, bf16[128,2048]{1,0:T(8,128)(2,1)S(1)}, u32[]{:S(2)}, u32[]{:S(2)}) collective-permute-start(bf16[128,2048]{1,0:T(8,128)(2,1)S(1)} %combine.7), channel_id=1, source_target_pairs={{0,12},{1,13},{2,14},{3,15},{4,8},{5,9},{6,10},{7,11},{8,4},{9,5},... | collective-permute-start | bytes 1572872 | tf_op jit(solution)/shard_map/ppermute | solution.py:257
  210.6 23.7 %collective-permute-start.59 = (bf16[256,1024]{1,0:T(8,128)(2,1)S(1)}, bf16[256,1024]{1,0:T(8,128)(2,1)S(1)}, u32[]{:S(2)}, u32[]{:S(2)}) collective-permute-start(bf16[256,1024]{1,0:T(8,128)(2,1)S(1)} %broadcast_select_fusion.refs_12_), channel_id=1, source_target_pairs={{0,1},{1,0},{2,3},{3,2},{4,5},{5,4},{6,7},{7,6},{8,9},{9,8},{10,11... | collective-permute-start | bytes 1572872 | tf_op jit(solution)/shard_map/ppermute | solution.py:266
  210.9 23.4 %collective-permute-start.56 = (bf16[256,1024]{1,0:T(8,128)(2,1)S(1)}, bf16[256,1024]{1,0:T(8,128)(2,1)S(1)}, u32[]{:S(2)}, u32[]{:S(2)}) collective-permute-start(bf16[256,1024]{1,0:T(8,128)(2,1)S(1)} %broadcast_select_fusion.1.refs_8_), channel_id=1, source_target_pairs={{0,1},{1,0},{2,3},{3,2},{4,5},{5,4},{6,7},{7,6},{8,9},{9,8},{10,11... | collective-permute-start | bytes 1572872 | tf_op jit(solution)/shard_map/ppermute | solution.py:266
  211.1 23.2 %collective-permute-start.61 = (bf16[256,1024]{1,0:T(8,128)(2,1)S(1)}, bf16[256,1024]{1,0:T(8,128)(2,1)S(1)}, u32[]{:S(2)}, u32[]{:S(2)}) collective-permute-start(bf16[256,1024]{1,0:T(8,128)(2,1)S(1)} %collective-permute-done.60.refs_14_), channel_id=1, source_target_pairs={{0,1},{1,0},{2,3},{3,2},{4,5},{5,4},{6,7},{7,6},{8,9},{9,8},{10,11... | collective-permute-start | bytes 1572872 | tf_op jit(solution)/shard_map/ppermute | solution.py:266
  211.9 22.4 %collective-permute-start.58 = (bf16[256,1024]{1,0:T(8,128)(2,1)S(1)}, bf16[256,1024]{1,0:T(8,128)(2,1)S(1)}, u32[]{:S(2)}, u32[]{:S(2)}) collective-permute-start(bf16[256,1024]{1,0:T(8,128)(2,1)S(1)} %collective-permute-done.57.refs_10_), channel_id=1, source_target_pairs={{0,1},{1,0},{2,3},{3,2},{4,5},{5,4},{6,7},{7,6},{8,9},{9,8},{10,11... | collective-permute-start | bytes 1572872 | tf_op jit(solution)/shard_map/ppermute | solution.py:266
  (39 other events, 323.6 us)

commit v5 on v4

--- a/solution.py
+++ b/solution.py
@@ -10,7 +10,7 @@
 BF16 = jnp.bfloat16
 F32 = jnp.float32
 MIB = 1024 * 1024
-PACK, EXPERT, COMBINE, OUTER, INNER = 24, 40, 12, 24, 40
+PACK, EXPERT, COMBINE, OUTER, INNER = 20, 30, 8, 20, 36
 NT = (((1,), (1,)), ((), ()))
 TN = (((0,), (0,)), ((), ()))
 

time: 249 us -> 248 us (level)
  waiting for transfers between devices: 106 us -> 109 us
    unnamed x80 -> x60, local copies, waits for them, and re-layouts: 18 us -> 16.6 us
  transfers between devices with their start and end apart: 63 -> 63, of which waited for: 21 -> 19; matrix products, arithmetic and copies ran while one was open for 4% -> 4% of each run, Pallas kernels for 15% -> 14%
where the time goes in v5:
time: 248 us; the launch traced here: 247 us
  waiting for transfers between devices  109 us (44%)
  starting transfers between devices  56.7 us (23%)
  Pallas kernels  53 us (21%)
  local copies, waits for them, and re-layouts  20.2 us (8%)
  other arithmetic  7.01 us (3%)
    ppermute x16, waiting for transfers between devices, over_x(): return lax.ppermute(value, 'blk', [(b, b ^ 2) for b in range(nb)])  56.5 us
    ppermute x8, waiting for transfers between devices, over_z(): return lax.ppermute(value, 'blk', [(b, b ^ 4 * n) for b in range(nb)])  40.1 us
    pallas_call x4, Pallas kernels, expert(): pl.pallas_call(functools.partial(expert_kernel, slots, block), out_shape=...  24.8 us
    ppermute x8, starting transfers between devices, along_z(): lax.ppermute(value, 'blk', [(4 * a + n, 4 * b + n) for a, b in pairs for...  24.3 us
    unnamed x60, local copies, waits for them, and re-layouts  16.6 us
    ppermute x16, starting transfers between devices, over_x(): return lax.ppermute(value, 'blk', [(b, b ^ 2) for b in range(nb)])  14.8 us
    pallas_call x1, Pallas kernels, per_device(): pl.pallas_call(functools.partial(inner_kernel, zn, ng, slots, block), out...  13.6 us
    ppermute x6, starting transfers between devices, over_groups(): return lax.ppermute(value, 'grp', [(b, (b + n) % ng) for b in range(ng)])  9.23 us
  transfers between devices with their start and end apart: 63, of which 19 were waited for; matrix products, arithmetic and copies ran while one was open for 4% of the time, Pallas kernels for 14%

profile of v5, /device:TPU:10, one launch (start us, length us, event | category | flops | bytes accessed | tf_op | source)
XLA Modules:
  0.0 247.3 jit_solution(2067173544181211329)
XLA Ops:
  2.1 1.2 copy-done.8
  3.4 1.2 copy-done.9
  4.6 3.9 %pack.1 = (bf16[4,2,56,1408]{3,2,1,0:T(8,128)(2,1)S(1)}, bf16[4,2,56,1408]{3,2,1,0:T(8,128)(2,1)S(1)}) custom-call(s32[4]{0:T(128)S(1)} %pad_add_fusion.sc, bf16[12,128]{1,0:T(8,128)(2,1)S(1)} %pad_maximum_fusion.5.meta_ref, bf16[6,704,128]{2,1,0:T(8,128)(2,1)S(1)} %bitcast.69, bf16[6,704,128]{2,1,0:T(8,128)(2,1)S(1)} %bitcast.70), custom_call_target="tpu_custom_call" | custom-call | flops 96888424 | bytes 108134 | tf_op jit(solution)/shard_map/pack/pallas_call | solution.py:287
  9.1 4.6 %collective-permute-start.1 = (bf16[128,2048]{1,0:T(8,128)(2,1)}, bf16[128,2048]{1,0:T(8,128)(2,1)}, u32[]{:S(2)}, u32[]{:S(2)}) collective-permute-start(bf16[128,2048]{1,0:T(8,128)(2,1)} %d00.1), channel_id=1, source_target_pairs={{4,8},{5,9},{6,10},{7,11},{8,4},{9,5},{10,6},{11,7},{20,24},{21,25... | collective-permute-start | bytes 1572872 | tf_op jit(solution)/shard_map/ppermute | solution.py:260
  14.4 1.6 collective-permute-start.3
  16.1 6.2 %collective-permute-done.3 = bf16[128,1024]{1,0:T(8,128)(2,1)S(1)} collective-permute-done((bf16[128,1024]{1,0:T(8,128)(2,1)S(1)}, bf16[128,1024]{1,0:T(8,128)(2,1)S(1)}, u32[]{:S(2)}, u32[]{:S(2)}) %collective-permute-start.3) | collective-permute-done | bytes 262176 | tf_op jit(solution)/shard_map/ppermute | solution.py:269
  22.3 1.5 slice_bitcast_fusion
  23.8 1.1 pad_maximum_fusion.2
  25.1 1.2 collective-permute-done.1
  26.3 1.5 collective-permute-done.2.d10
  28.5 2.2 collective-permute-start.6
  30.7 1.5 collective-permute-start.7
  32.2 6.1 %collective-permute-done.11.far = bf16[112,1408]{1,0:T(8,128)(2,1)S(1)} collective-permute-done((bf16[112,1408]{1,0:T(8,128)(2,1)S(1)}, bf16[112,1408]{1,0:T(8,128)(2,1)S(1)}, u32[]{:S(2)}, u32[]{:S(2)}) %collective-permute-start.11) | collective-permute-done | bytes 315424 | tf_op jit(solution)/shard_map/ppermute | solution.py:263
  38.3 7.4 %expert.4 = (bf16[224,1408]{1,0:T(8,128)(2,1)}, bf16[224,704]{1,0:T(8,128)(2,1)S(1)}, bf16[224,2048]{1,0:T(8,128)(2,1)S(1)}, bf16[56,2048]{1,0:T(8,128)(2,1)S(1)...) custom-call(bf16[128,2048]{1,0:T(8,128)(2,1)} %d00.1, bf16[128,2048]{1,0:T(8,128)(2,1)S(1)} %collective-permute-done.9.d01, ...), custom_call_target="tpu_custom_call" | custom-call | flops 152672672 | bytes 800000 | tf_op jit(solution)/shard_map/expert/pallas_call | solution.py:311
  50.9 1.5 collective-permute-start.18
  52.4 4.4 %collective-permute-start.14 = (bf16[128,2048]{1,0:T(8,128)(2,1)}, bf16[128,2048]{1,0:T(8,128)(2,1)}, u32[]{:S(2)}, u32[]{:S(2)}) collective-permute-start(bf16[128,2048]{1,0:T(8,128)(2,1)} %collective-permute-done.1), channel_id=1, source_target_pairs={{4,0},{5,1},{6,2},{7,3},{8,12},{9,13},{10,14},{11,15},{20,16},{21,... | collective-permute-start | bytes 1572872 | tf_op jit(solution)/shard_map/ppermute | solution.py:260
  56.8 3.4 %collective-permute-done.15.far = bf16[112,1408]{1,0:T(8,128)(2,1)S(1)} collective-permute-done((bf16[112,1408]{1,0:T(8,128)(2,1)S(1)}, bf16[112,1408]{1,0:T(8,128)(2,1)S(1)}, u32[]{:S(2)}, u32[]{:S(2)}) %collective-permute-start.15) | collective-permute-done | bytes 315424 | tf_op jit(solution)/shard_map/ppermute | solution.py:263
  62.1 1.7 collective-permute-start.17
  63.8 1.8 copy-done.2
  65.6 1.8 copy-done.5
  67.4 1.0 copy-done.7
  68.4 1.0 copy-done.13
  69.4 1.0 copy-done.15
  70.5 1.0 copy-done.17
  71.5 1.0 copy-done.21
  72.5 6.5 %expert.5 = (bf16[224,1408]{1,0:T(8,128)(2,1)S(1)}, bf16[224,704]{1,0:T(8,128)(2,1)S(1)}, bf16[224,2048]{1,0:T(8,128)(2,1)S(1)}, bf16[56,2048]{1,0:T(8,128)(2,1)...) custom-call(bf16[128,2048]{1,0:T(8,128)(2,1)} %collective-permute-done.d00, ...), custom_call_target="tpu_custom_call" | custom-call | flops 152672672 | bytes 800000 | tf_op jit(solution)/shard_map/expert/pallas_call | solution.py:311
  79.0 5.0 %collective-permute-done.17.hop = bf16[112,2048]{1,0:T(8,128)(2,1)} collective-permute-done((bf16[112,2048]{1,0:T(8,128)(2,1)}, bf16[112,2048]{1,0:T(8,128)(2,1)}, u32[]{:S(2)}, u32[]{:S(2)}) %collective-permute-start.17) | collective-permute-done | bytes 458784 | tf_op jit(solution)/shard_map/ppermute | solution.py:263
  84.8 1.1 slice_bitcast_fusion.6
  85.9 1.4 collective-permute-start.23
  88.2 1.5 collective-permute-start.25
  89.7 9.3 %collective-permute-done.27.d10 = bf16[128,2048]{1,0:T(8,128)(2,1)S(1)} collective-permute-done((bf16[128,2048]{1,0:T(8,128)(2,1)S(1)}, bf16[128,2048]{1,0:T(8,128)(2,1)S(1)}, u32[]{:S(2)}, u32[]{:S(2)}) %collective-permute-start.27) | collective-permute-done | bytes 524320 | tf_op jit(solution)/shard_map/ppermute | solution.py:263
  99.0 4.1 %collective-permute-done.23.far = bf16[112,1408]{1,0:T(8,128)(2,1)S(1)} collective-permute-done((bf16[112,1408]{1,0:T(8,128)(2,1)S(1)}, bf16[112,1408]{1,0:T(8,128)(2,1)S(1)}, u32[]{:S(2)}, u32[]{:S(2)}) %collective-permute-start.23) | collective-permute-done | bytes 315424 | tf_op jit(solution)/shard_map/ppermute | solution.py:263
  103.1 2.8 %collective-permute-start.22 = (bf16[128,2048]{1,0:T(8,128)(2,1)S(1)}, bf16[128,2048]{1,0:T(8,128)(2,1)S(1)}, u32[]{:S(2)}, u32[]{:S(2)}) collective-permute-start(bf16[128,2048]{1,0:T(8,128)(2,1)S(1)} %copy-done.29), channel_id=1, source_target_pairs={{4,0},{5,1},{6,2},{7,3},{8,12},{9,13},{10,14},{11,15},{20,16},{21,... | collective-permute-start | bytes 1572872 | tf_op jit(solution)/shard_map/ppermute | solution.py:260
  105.9 0.9 collective-permute-start.24
  106.8 5.4 %expert.6 = (bf16[224,1408]{1,0:T(8,128)(2,1)S(1)}, bf16[224,704]{1,0:T(8,128)(2,1)S(1)}, bf16[224,2048]{1,0:T(8,128)(2,1)S(1)}, bf16[56,2048]{1,0:T(8,128)(2,1)...) custom-call(bf16[128,2048]{1,0:T(8,128)(2,1)S(1)} %broadcast_select_fusion.3.d00, ...), custom_call_target="tpu_custom_call" | custom-call | flops 152672672 | bytes 800000 | tf_op jit(solution)/shard_map/expert/pallas_call | solution.py:311
  112.2 3.0 %collective-permute-done.22 = bf16[128,2048]{1,0:T(8,128)(2,1)S(1)} collective-permute-done((bf16[128,2048]{1,0:T(8,128)(2,1)S(1)}, bf16[128,2048]{1,0:T(8,128)(2,1)S(1)}, u32[]{:S(2)}, u32[]{:S(2)}) %collective-permute-start.22) | collective-permute-done | bytes 524320 | tf_op jit(solution)/shard_map/ppermute | solution.py:260
  115.2 2.0 collective-permute-done.21
  118.0 1.3 broadcast_select_fusion.2.d00
  119.3 1.4 collective-permute-start.39
  120.7 2.7 %collective-permute-start.30 = (bf16[256,1024]{1,0:T(8,128)(2,1)S(1)}, bf16[256,1024]{1,0:T(8,128)(2,1)S(1)}, u32[]{:S(2)}, u32[]{:S(2)}) collective-permute-start(bf16[256,1024]{1,0:T(8,128)(2,1)S(1)} %pad_maximum_fusion.4.refs_0_), channel_id=1, source_target_pairs={{4,8},{5,9},{6,10},{7,11},{8,4},{9,5},{10,6},{11,7},{20,24},{21,25... | collective-permute-start | bytes 1572872 | tf_op jit(solution)/shard_map/ppermute | solution.py:260
  123.4 4.3 %collective-permute-done.33.far = bf16[112,1408]{1,0:T(8,128)(2,1)S(1)} collective-permute-done((bf16[112,1408]{1,0:T(8,128)(2,1)S(1)}, bf16[112,1408]{1,0:T(8,128)(2,1)S(1)}, u32[]{:S(2)}, u32[]{:S(2)}) %collective-permute-start.33) | collective-permute-done | bytes 315424 | tf_op jit(solution)/shard_map/ppermute | solution.py:263
  127.7 1.5 collective-permute-start.37
  129.3 8.1 %collective-permute-done.39.d10 = bf16[128,2048]{1,0:T(8,128)(2,1)S(1)} collective-permute-done((bf16[128,2048]{1,0:T(8,128)(2,1)S(1)}, bf16[128,2048]{1,0:T(8,128)(2,1)S(1)}, u32[]{:S(2)}, u32[]{:S(2)}) %collective-permute-start.39) | collective-permute-done | bytes 524320 | tf_op jit(solution)/shard_map/ppermute | solution.py:263
  137.4 2.7 %collective-permute-start.31 = (bf16[256,1024]{1,0:T(8,128)(2,1)S(1)}, bf16[256,1024]{1,0:T(8,128)(2,1)S(1)}, u32[]{:S(2)}, u32[]{:S(2)}) collective-permute-start(bf16[256,1024]{1,0:T(8,128)(2,1)S(1)} %collective-permute-done.29.refs_4_), channel_id=1, source_target_pairs={{4,8},{5,9},{6,10},{7,11},{8,4},{9,5},{10,6},{11,7},{20,24},{21,25... | collective-permute-start | bytes 1572872 | tf_op jit(solution)/shard_map/ppermute | solution.py:260
  140.1 1.3 collective-permute-start.32
  142.9 5.4 %expert.7 = (bf16[224,1408]{1,0:T(8,128)(2,1)S(1)}, bf16[224,704]{1,0:T(8,128)(2,1)S(1)}, bf16[224,2048]{1,0:T(8,128)(2,1)S(1)}, bf16[56,2048]{1,0:T(8,128)(2,1)...) custom-call(bf16[128,2048]{1,0:T(8,128)(2,1)S(1)} %broadcast_select_fusion.2.d00, ...), custom_call_target="tpu_custom_call" | custom-call | flops 152672672 | bytes 800000 | tf_op jit(solution)/shard_map/expert/pallas_call | solution.py:311
  148.9 5.3 %collective-permute-done.34.hop = bf16[112,2048]{1,0:T(8,128)(2,1)S(1)} collective-permute-done((bf16[112,2048]{1,0:T(8,128)(2,1)S(1)}, bf16[112,2048]{1,0:T(8,128)(2,1)S(1)}, u32[]{:S(2)}, u32[]{:S(2)}) %collective-permute-start.34) | collective-permute-done | bytes 458784 | tf_op jit(solution)/shard_map/ppermute | solution.py:263
  154.7 1.5 collective-permute-start.47
  156.3 1.5 collective-permute-start.53
  157.8 3.6 %collective-permute-start.46 = (bf16[256,1024]{1,0:T(8,128)(2,1)S(1)}, bf16[256,1024]{1,0:T(8,128)(2,1)S(1)}, u32[]{:S(2)}, u32[]{:S(2)}) collective-permute-start(bf16[256,1024]{1,0:T(8,128)(2,1)S(1)} %collective-permute-done.31), channel_id=1, source_target_pairs={{4,0},{5,1},{6,2},{7,3},{8,12},{9,13},{10,14},{11,15},{20,16},{21,... | collective-permute-start | bytes 1572872 | tf_op jit(solution)/shard_map/ppermute | solution.py:260
  161.5 7.6 %collective-permute-done.51.refs_6_ = bf16[256,1024]{1,0:T(8,128)(2,1)S(1)} collective-permute-done((bf16[256,1024]{1,0:T(8,128)(2,1)S(1)}, bf16[256,1024]{1,0:T(8,128)(2,1)S(1)}, u32[]{:S(2)}, u32[]{:S(2)}) %collective-permute-start.51) | collective-permute-done | bytes 524320 | tf_op jit(solution)/shard_map/ppermute | solution.py:263
  169.1 6.8 %outer.1 = (f32[704,1024]{1,0:T(8,128)S(1)}, bf16[1,704,1024]{2,1,0:T(8,128)(2,1)S(1)}) custom-call(s32[4]{0:T(128)S(1)} %pad_add_fusion.sc, bf16[224,704]{1,0:T(8,128)(2,1)S(1)} %copy-done.19, bf16[224,704]{1,0:T(8,128)(2,1)S(1)} %get-tuple-element.207.refs_1_, bf16[224,704]{1,0:T(8,128)(2,1)S(1)} %get-tuple-element.208.refs_2_, ...), custom_call_target="tpu_custom_call" | custom-call | flops 129184560 | bytes 500000 | tf_op jit(solution)/shard_map/outer/pallas_call | solution.py:416
  175.9 1.4 collective-permute-done.47.hop
  177.3 1.5 collective-permute-start.62
  179.9 2.0 collective-permute-done.42.swap
  183.2 1.9 collective-permute-start.41
  185.1 0.9 collective-permute-start.44
  186.8 1.4 collective-permute-start.57
  188.9 18.4 %collective-permute-done.41 = bf16[128,2048]{1,0:T(8,128)(2,1)S(1)} collective-permute-done((bf16[128,2048]{1,0:T(8,128)(2,1)S(1)}, bf16[128,2048]{1,0:T(8,128)(2,1)S(1)}, u32[]{:S(2)}, u32[]{:S(2)}) %collective-permute-start.41) | collective-permute-done | bytes 524320 | tf_op jit(solution)/shard_map/ppermute | solution.py:257
  208.1 1.7 combine.4
  210.9 1.7 fusion
  212.6 19.7 %collective-permute-done.55 = bf16[128,2048]{1,0:T(8,128)(2,1)S(1)} collective-permute-done((bf16[128,2048]{1,0:T(8,128)(2,1)S(1)}, bf16[128,2048]{1,0:T(8,128)(2,1)S(1)}, u32[]{:S(2)}, u32[]{:S(2)}) %collective-permute-start.55) | collective-permute-done | bytes 524320 | tf_op jit(solution)/shard_map/ppermute | solution.py:257
  232.3 1.1 add_convert_fusion.1
  233.5 13.6 %inner.1 = (bf16[704,1024]{1,0:T(8,128)(2,1)}, bf16[704,1024]{1,0:T(8,128)(2,1)}) custom-call(bf16[256,1024]{1,0:T(8,128)(2,1)S(1)} %pad_maximum_fusion.4.refs_0_, bf16[256,1024]{1,0:T(8,128)(2,1)S(1)} %collective-permute-done.48.refs_1_, bf16[256,1024]{1,0:T(8,128)(2,1)} %collective-permute-done.16.refs_2_, ...), custom_call_target="tpu_custom_call" | custom-call | flops 258369120 | bytes 1000000 | tf_op jit(solution)/shard_map/inner/pallas_call | solution.py:435
  (152 shorter events, 21.4 us)
Async XLA Ops:
  8.5 13.8 %collective-permute-start.4 = (bf16[4,2,56,1408]{3,2,1,0:T(8,128)(2,1)S(1)}, bf16[4,2,56,1408]{3,2,1,0:T(8,128)(2,1)}, u32[]{:S(2)}, u32[]{:S(2)}) collective-permute-start(bf16[4,2,56,1408]{3,2,1,0:T(8,128)(2,1)S(1)} %get-tuple-element.111), channel_id=1, source_target_pairs={{0,1},{1,0},{2,3},{3,2},{4,5},{5,4},{6,7},{7,6},{8,9},{9,8},{10,11... | collective-permute-start | bytes 3784712 | tf_op jit(solution)/shard_map/ppermute | solution.py:266
  8.6 16.5 %collective-permute-start = (bf16[128,2048]{1,0:T(8,128)(2,1)}, bf16[128,2048]{1,0:T(8,128)(2,1)}, u32[]{:S(2)}, u32[]{:S(2)}) collective-permute-start(bf16[128,2048]{1,0:T(8,128)(2,1)} %d00.1), channel_id=1, source_target_pairs={{0,4},{1,5},{2,6},{3,7},{4,0},{5,1},{6,2},{7,3},{8,12},{9,13},{10,... | collective-permute-start | bytes 1572872 | tf_op jit(solution)/shard_map/ppermute | solution.py:257
  9.1 17.1 %collective-permute-start.1 = (bf16[128,2048]{1,0:T(8,128)(2,1)}, bf16[128,2048]{1,0:T(8,128)(2,1)}, u32[]{:S(2)}, u32[]{:S(2)}) collective-permute-start(bf16[128,2048]{1,0:T(8,128)(2,1)} %d00.1), channel_id=1, source_target_pairs={{4,8},{5,9},{6,10},{7,11},{8,4},{9,5},{10,6},{11,7},{20,24},{21,25... | collective-permute-start | bytes 1572872 | tf_op jit(solution)/shard_map/ppermute | solution.py:260
  13.7 14.1 %collective-permute-start.2 = (bf16[128,2048]{1,0:T(8,128)(2,1)}, bf16[128,2048]{1,0:T(8,128)(2,1)}, u32[]{:S(2)}, u32[]{:S(2)}) collective-permute-start(bf16[128,2048]{1,0:T(8,128)(2,1)} %d00.1), channel_id=1, source_target_pairs={{0,2},{1,3},{2,0},{3,1},{4,6},{5,7},{6,4},{7,5},{8,10},{9,11},{10,... | collective-permute-start | bytes 1572872 | tf_op jit(solution)/shard_map/ppermute | solution.py:263
  14.4 7.9 %collective-permute-start.3 = (bf16[128,1024]{1,0:T(8,128)(2,1)S(1)}, bf16[128,1024]{1,0:T(8,128)(2,1)S(1)}, u32[]{:S(2)}, u32[]{:S(2)}) collective-permute-start(bf16[128,1024]{1,0:T(8,128)(2,1)S(1)} %get-tuple-element.233), channel_id=1, source_target_pairs={{0,16},{16,0},{1,17},{17,1},{2,18},{18,2},{3,19},{19,3},{4,20},{20... | collective-permute-start | bytes 786440 | tf_op jit(solution)/shard_map/ppermute | solution.py:269
  22.2 8.4 %collective-permute-start.9 = (bf16[128,2048]{1,0:T(8,128)(2,1)}, bf16[128,2048]{1,0:T(8,128)(2,1)S(1)}, u32[]{:S(2)}, u32[]{:S(2)}) collective-permute-start(bf16[128,2048]{1,0:T(8,128)(2,1)} %d00.1), channel_id=1, source_target_pairs={{0,1},{1,0},{2,3},{3,2},{4,5},{5,4},{6,7},{7,6},{8,9},{9,8},{10,11... | collective-permute-start | bytes 1572872 | tf_op jit(solution)/shard_map/ppermute | solution.py:266
  27.9 10.4 %collective-permute-start.11 = (bf16[112,1408]{1,0:T(8,128)(2,1)S(1)}, bf16[112,1408]{1,0:T(8,128)(2,1)S(1)}, u32[]{:S(2)}, u32[]{:S(2)}) collective-permute-start(bf16[112,1408]{1,0:T(8,128)(2,1)S(1)} %get-tuple-element.230), channel_id=1, source_target_pairs={{0,2},{1,3},{2,0},{3,1},{4,6},{5,7},{6,4},{7,5},{8,10},{9,11},{10,... | collective-permute-start | bytes 946184 | tf_op jit(solution)/shard_map/ppermute | solution.py:263
  28.5 20.3 %collective-permute-start.5 = (bf16[2,112,1408]{2,1,0:T(8,128)(2,1)S(1)}, bf16[2,112,1408]{2,1,0:T(8,128)(2,1)S(1)}, u32[]{:S(2)}, u32[]{:S(2)}) collective-permute-start(bf16[2,112,1408]{2,1,0:T(8,128)(2,1)S(1)} %get-tuple-element.112), channel_id=1, source_target_pairs={{0,4},{1,5},{2,6},{3,7},{4,0},{5,1},{6,2},{7,3},{8,12},{9,13},{10,... | collective-permute-start | bytes 1892360 | tf_op jit(solution)/shard_map/ppermute | solution.py:257
  28.5 9.8 %collective-permute-start.10 = (bf16[128,2048]{1,0:T(8,128)(2,1)}, bf16[128,2048]{1,0:T(8,128)(2,1)S(1)}, u32[]{:S(2)}, u32[]{:S(2)}) collective-permute-start(bf16[128,2048]{1,0:T(8,128)(2,1)} %collective-permute-done.2.d10), channel_id=1, source_target_pairs={{0,1},{1,0},{2,3},{3,2},{4,5},{5,4},{6,7},{7,6},{8,9},{9,8},{10,11... | collective-permute-start | bytes 1572872 | tf_op jit(solution)/shard_map/ppermute | solution.py:266
  28.5 19.4 %collective-permute-start.6 = (bf16[128,2048]{1,0:T(8,128)(2,1)}, bf16[128,2048]{1,0:T(8,128)(2,1)S(1)}, u32[]{:S(2)}, u32[]{:S(2)}) collective-permute-start(bf16[128,2048]{1,0:T(8,128)(2,1)} %collective-permute-done.d00), channel_id=1, source_target_pairs={{4,8},{5,9},{6,10},{7,11},{8,4},{9,5},{10,6},{11,7},{20,24},{21,25... | collective-permute-start | bytes 1572872 | tf_op jit(solution)/shard_map/ppermute | solution.py:260
  30.7 17.2 %collective-permute-start.7 = (bf16[128,2048]{1,0:T(8,128)(2,1)}, bf16[128,2048]{1,0:T(8,128)(2,1)S(1)}, u32[]{:S(2)}, u32[]{:S(2)}) collective-permute-start(bf16[128,2048]{1,0:T(8,128)(2,1)} %collective-permute-done.d00), channel_id=1, source_target_pairs={{0,2},{1,3},{2,0},{3,1},{4,6},{5,7},{6,4},{7,5},{8,10},{9,11},{10,... | collective-permute-start | bytes 1572872 | tf_op jit(solution)/shard_map/ppermute | solution.py:263
  38.3 9.6 %collective-permute-start.8 = (bf16[128,2048]{1,0:T(8,128)(2,1)}, bf16[128,2048]{1,0:T(8,128)(2,1)S(1)}, u32[]{:S(2)}, u32[]{:S(2)}) collective-permute-start(bf16[128,2048]{1,0:T(8,128)(2,1)} %collective-permute-done.d00), channel_id=1, source_target_pairs={{0,1},{1,0},{2,3},{3,2},{4,5},{5,4},{6,7},{7,6},{8,9},{9,8},{10,11... | collective-permute-start | bytes 1572872 | tf_op jit(solution)/shard_map/ppermute | solution.py:266
  48.7 12.5 %collective-permute-start.19 = (bf16[128,2048]{1,0:T(8,128)(2,1)S(1)}, bf16[128,2048]{1,0:T(8,128)(2,1)S(1)}, u32[]{:S(2)}, u32[]{:S(2)}) collective-permute-start(bf16[128,2048]{1,0:T(8,128)(2,1)S(1)} %collective-permute-done.7.d10), channel_id=1, source_target_pairs={{0,1},{1,0},{2,3},{3,2},{4,5},{5,4},{6,7},{7,6},{8,9},{9,8},{10,11... | collective-permute-start | bytes 1572872 | tf_op jit(solution)/shard_map/ppermute | solution.py:266
  50.8 9.4 %collective-permute-start.15 = (bf16[112,1408]{1,0:T(8,128)(2,1)S(1)}, bf16[112,1408]{1,0:T(8,128)(2,1)S(1)}, u32[]{:S(2)}, u32[]{:S(2)}) collective-permute-start(bf16[112,1408]{1,0:T(8,128)(2,1)S(1)} %get-tuple-element.229), channel_id=1, source_target_pairs={{0,2},{1,3},{2,0},{3,1},{4,6},{5,7},{6,4},{7,5},{8,10},{9,11},{10,... | collective-permute-start | bytes 946184 | tf_op jit(solution)/shard_map/ppermute | solution.py:263
  50.9 33.1 %collective-permute-start.13 = (bf16[2,112,1408]{2,1,0:T(8,128)(2,1)}, bf16[2,112,1408]{2,1,0:T(8,128)(2,1)}, u32[]{:S(2)}, u32[]{:S(2)}) collective-permute-start(bf16[2,112,1408]{2,1,0:T(8,128)(2,1)} %get-tuple-element.126), channel_id=1, source_target_pairs={{0,8},{1,9},{2,10},{3,11},{4,12},{5,13},{6,14},{7,15},{8,0},{9,1},... | collective-permute-start | bytes 1892360 | tf_op jit(solution)/shard_map/ppermute | solution.py:257
  50.9 33.1 %collective-permute-start.18 = (bf16[224,1408]{1,0:T(8,128)(2,1)}, bf16[224,1408]{1,0:T(8,128)(2,1)}, u32[]{:S(2)}, u32[]{:S(2)}) collective-permute-start(bf16[224,1408]{1,0:T(8,128)(2,1)} %get-tuple-element.196.refs_16_), channel_id=1, source_target_pairs={{0,16},{16,0},{1,17},{17,1},{2,18},{18,2},{3,19},{19,3},{4,20},{20... | collective-permute-start | bytes 1892360 | tf_op jit(solution)/shard_map/ppermute | solution.py:269
  52.4 31.6 %collective-permute-start.14 = (bf16[128,2048]{1,0:T(8,128)(2,1)}, bf16[128,2048]{1,0:T(8,128)(2,1)}, u32[]{:S(2)}, u32[]{:S(2)}) collective-permute-start(bf16[128,2048]{1,0:T(8,128)(2,1)} %collective-permute-done.1), channel_id=1, source_target_pairs={{4,0},{5,1},{6,2},{7,3},{8,12},{9,13},{10,14},{11,15},{20,16},{21,... | collective-permute-start | bytes 1572872 | tf_op jit(solution)/shard_map/ppermute | solution.py:260
  60.9 23.0 %collective-permute-start.16 = (bf16[256,1024]{1,0:T(8,128)(2,1)S(1)}, bf16[256,1024]{1,0:T(8,128)(2,1)}, u32[]{:S(2)}, u32[]{:S(2)}) collective-permute-start(bf16[256,1024]{1,0:T(8,128)(2,1)S(1)} %pad_maximum_fusion.4.refs_0_), channel_id=1, source_target_pairs={{0,2},{1,3},{2,0},{3,1},{4,6},{5,7},{6,4},{7,5},{8,10},{9,11},{10,... | collective-permute-start | bytes 1572872 | tf_op jit(solution)/shard_map/ppermute | solution.py:263
  62.1 21.9 %collective-permute-start.17 = (bf16[112,2048]{1,0:T(8,128)(2,1)}, bf16[112,2048]{1,0:T(8,128)(2,1)}, u32[]{:S(2)}, u32[]{:S(2)}) collective-permute-start(bf16[112,2048]{1,0:T(8,128)(2,1)} %get-tuple-element.131), channel_id=1, source_target_pairs={{0,2},{1,3},{2,0},{3,1},{4,6},{5,7},{6,4},{7,5},{8,10},{9,11},{10,... | collective-permute-start | bytes 1376264 | tf_op jit(solution)/shard_map/ppermute | solution.py:263
  84.1 14.9 %collective-permute-start.27 = (bf16[128,2048]{1,0:T(8,128)(2,1)S(1)}, bf16[128,2048]{1,0:T(8,128)(2,1)S(1)}, u32[]{:S(2)}, u32[]{:S(2)}) collective-permute-start(bf16[128,2048]{1,0:T(8,128)(2,1)S(1)} %broadcast_select_fusion.3.d00), channel_id=1, source_target_pairs={{0,2},{1,3},{2,0},{3,1},{4,6},{5,7},{6,4},{7,5},{8,10},{9,11},{10,... | collective-permute-start | bytes 1572872 | tf_op jit(solution)/shard_map/ppermute | solution.py:263
  84.8 21.1 %collective-permute-start.26 = (bf16[128,2048]{1,0:T(8,128)(2,1)S(1)}, bf16[128,2048]{1,0:T(8,128)(2,1)S(1)}, u32[]{:S(2)}, u32[]{:S(2)}) collective-permute-start(bf16[128,2048]{1,0:T(8,128)(2,1)S(1)} %broadcast_select_fusion.3.d00), channel_id=1, source_target_pairs={{0,1},{1,0},{2,3},{3,2},{4,5},{5,4},{6,7},{7,6},{8,9},{9,8},{10,11... | collective-permute-start | bytes 1572872 | tf_op jit(solution)/shard_map/ppermute | solution.py:266
  85.9 17.2 %collective-permute-start.23 = (bf16[112,1408]{1,0:T(8,128)(2,1)S(1)}, bf16[112,1408]{1,0:T(8,128)(2,1)S(1)}, u32[]{:S(2)}, u32[]{:S(2)}) collective-permute-start(bf16[112,1408]{1,0:T(8,128)(2,1)S(1)} %get-tuple-element.227), channel_id=1, source_target_pairs={{0,2},{1,3},{2,0},{3,1},{4,6},{5,7},{6,4},{7,5},{8,10},{9,11},{10,... | collective-permute-start | bytes 946184 | tf_op jit(solution)/shard_map/ppermute | solution.py:263
  87.4 29.9 %collective-permute-start.21 = (bf16[2,112,1408]{2,1,0:T(8,128)(2,1)S(1)}, bf16[2,112,1408]{2,1,0:T(8,128)(2,1)S(1)}, u32[]{:S(2)}, u32[]{:S(2)}) collective-permute-start(bf16[2,112,1408]{2,1,0:T(8,128)(2,1)S(1)} %copy-done.26), channel_id=1, source_target_pairs={{0,12},{1,13},{2,14},{3,15},{4,8},{5,9},{6,10},{7,11},{8,4},{9,5},... | collective-permute-start | bytes 1892360 | tf_op jit(solution)/shard_map/ppermute | solution.py:257
  88.2 29.0 %collective-permute-start.25 = (bf16[224,1408]{1,0:T(8,128)(2,1)S(1)}, bf16[224,1408]{1,0:T(8,128)(2,1)S(1)}, u32[]{:S(2)}, u32[]{:S(2)}) collective-permute-start(bf16[224,1408]{1,0:T(8,128)(2,1)S(1)} %get-tuple-element.198.refs_18_), channel_id=1, source_target_pairs={{0,16},{16,0},{1,17},{17,1},{2,18},{18,2},{3,19},{19,3},{4,20},{20... | collective-permute-start | bytes 1892360 | tf_op jit(solution)/shard_map/ppermute | solution.py:269
  99.0 7.7 %collective-permute-start.28 = (bf16[128,2048]{1,0:T(8,128)(2,1)S(1)}, bf16[128,2048]{1,0:T(8,128)(2,1)S(1)}, u32[]{:S(2)}, u32[]{:S(2)}) collective-permute-start(bf16[128,2048]{1,0:T(8,128)(2,1)S(1)} %collective-permute-done.27.d10), channel_id=1, source_target_pairs={{0,1},{1,0},{2,3},{3,2},{4,5},{5,4},{6,7},{7,6},{8,9},{9,8},{10,11... | collective-permute-start | bytes 1572872 | tf_op jit(solution)/shard_map/ppermute | solution.py:266
  103.1 12.1 %collective-permute-start.22 = (bf16[128,2048]{1,0:T(8,128)(2,1)S(1)}, bf16[128,2048]{1,0:T(8,128)(2,1)S(1)}, u32[]{:S(2)}, u32[]{:S(2)}) collective-permute-start(bf16[128,2048]{1,0:T(8,128)(2,1)S(1)} %copy-done.29), channel_id=1, source_target_pairs={{4,0},{5,1},{6,2},{7,3},{8,12},{9,13},{10,14},{11,15},{20,16},{21,... | collective-permute-start | bytes 1572872 | tf_op jit(solution)/shard_map/ppermute | solution.py:260
  105.9 11.3 %collective-permute-start.24 = (bf16[112,2048]{1,0:T(8,128)(2,1)S(1)}, bf16[112,2048]{1,0:T(8,128)(2,1)S(1)}, u32[]{:S(2)}, u32[]{:S(2)}) collective-permute-start(bf16[112,2048]{1,0:T(8,128)(2,1)S(1)} %get-tuple-element.148), channel_id=1, source_target_pairs={{0,2},{1,3},{2,0},{3,1},{4,6},{5,7},{6,4},{7,5},{8,10},{9,11},{10,... | collective-permute-start | bytes 1376264 | tf_op jit(solution)/shard_map/ppermute | solution.py:263
  106.8 14.0 %collective-permute-start.35 = (bf16[56,2048]{1,0:T(8,128)(2,1)S(1)}, bf16[56,2048]{1,0:T(8,128)(2,1)S(1)}, u32[]{:S(2)}, u32[]{:S(2)}) collective-permute-start(bf16[56,2048]{1,0:T(8,128)(2,1)S(1)} %get-tuple-element.162), channel_id=1, source_target_pairs={{0,1},{1,0},{2,3},{3,2},{4,5},{5,4},{6,7},{7,6},{8,9},{9,8},{10,11... | collective-permute-start | bytes 688136 | tf_op jit(solution)/shard_map/ppermute | solution.py:266
  106.8 36.1 %copy-start.6 = (bf16[1,704,2048]{2,1,0:T(8,128)(2,1)S(1)}, bf16[1,704,2048]{2,1,0:T(8,128)(2,1)}, u32[]{:S(2)}) copy-start(bf16[1,704,2048]{2,1,0:T(8,128)(2,1)} %param.17) | copy-start | bytes 8650756
  117.3 10.4 %collective-permute-start.33 = (bf16[112,1408]{1,0:T(8,128)(2,1)S(1)}, bf16[112,1408]{1,0:T(8,128)(2,1)S(1)}, u32[]{:S(2)}, u32[]{:S(2)}) collective-permute-start(bf16[112,1408]{1,0:T(8,128)(2,1)S(1)} %get-tuple-element.225), channel_id=1, source_target_pairs={{0,2},{1,3},{2,0},{3,1},{4,6},{5,7},{6,4},{7,5},{8,10},{9,11},{10,... | collective-permute-start | bytes 946184 | tf_op jit(solution)/shard_map/ppermute | solution.py:263
  118.0 9.7 %collective-permute-start.36 = (bf16[112,2048]{1,0:T(8,128)(2,1)S(1)}, bf16[112,2048]{1,0:T(8,128)(2,1)S(1)}, u32[]{:S(2)}, u32[]{:S(2)}) collective-permute-start(bf16[112,2048]{1,0:T(8,128)(2,1)S(1)} %collective-permute-done.24.hop), channel_id=1, source_target_pairs={{0,1},{1,0},{2,3},{3,2},{4,5},{5,4},{6,7},{7,6},{8,9},{9,8},{10,11... | collective-permute-start | bytes 1376264 | tf_op jit(solution)/shard_map/ppermute | solution.py:266
  119.3 18.1 %collective-permute-start.39 = (bf16[128,2048]{1,0:T(8,128)(2,1)S(1)}, bf16[128,2048]{1,0:T(8,128)(2,1)S(1)}, u32[]{:S(2)}, u32[]{:S(2)}) collective-permute-start(bf16[128,2048]{1,0:T(8,128)(2,1)S(1)} %broadcast_select_fusion.2.d00), channel_id=1, source_target_pairs={{0,2},{1,3},{2,0},{3,1},{4,6},{5,7},{6,4},{7,5},{8,10},{9,11},{10,... | collective-permute-start | bytes 1572872 | tf_op jit(solution)/shard_map/ppermute | solution.py:263
  120.7 16.7 %collective-permute-start.29 = (bf16[256,1024]{1,0:T(8,128)(2,1)S(1)}, bf16[256,1024]{1,0:T(8,128)(2,1)S(1)}, u32[]{:S(2)}, u32[]{:S(2)}) collective-permute-start(bf16[256,1024]{1,0:T(8,128)(2,1)S(1)} %pad_maximum_fusion.4.refs_0_), channel_id=1, source_target_pairs={{0,4},{1,5},{2,6},{3,7},{4,0},{5,1},{6,2},{7,3},{8,12},{9,13},{10,... | collective-permute-start | bytes 1572872 | tf_op jit(solution)/shard_map/ppermute | solution.py:257
  120.7 19.4 %collective-permute-start.30 = (bf16[256,1024]{1,0:T(8,128)(2,1)S(1)}, bf16[256,1024]{1,0:T(8,128)(2,1)S(1)}, u32[]{:S(2)}, u32[]{:S(2)}) collective-permute-start(bf16[256,1024]{1,0:T(8,128)(2,1)S(1)} %pad_maximum_fusion.4.refs_0_), channel_id=1, source_target_pairs={{4,8},{5,9},{6,10},{7,11},{8,4},{9,5},{10,6},{11,7},{20,24},{21,25... | collective-permute-start | bytes 1572872 | tf_op jit(solution)/shard_map/ppermute | solution.py:260
  127.7 13.7 %collective-permute-start.38 = (bf16[128,2048]{1,0:T(8,128)(2,1)S(1)}, bf16[128,2048]{1,0:T(8,128)(2,1)S(1)}, u32[]{:S(2)}, u32[]{:S(2)}) collective-permute-start(bf16[128,2048]{1,0:T(8,128)(2,1)S(1)} %broadcast_select_fusion.2.d00), channel_id=1, source_target_pairs={{0,1},{1,0},{2,3},{3,2},{4,5},{5,4},{6,7},{7,6},{8,9},{9,8},{10,11... | collective-permute-start | bytes 1572872 | tf_op jit(solution)/shard_map/ppermute | solution.py:266
  127.7 20.6 %collective-permute-start.37 = (bf16[224,1408]{1,0:T(8,128)(2,1)S(1)}, bf16[224,1408]{1,0:T(8,128)(2,1)S(1)}, u32[]{:S(2)}, u32[]{:S(2)}) collective-permute-start(bf16[224,1408]{1,0:T(8,128)(2,1)S(1)} %get-tuple-element.200.refs_20_), channel_id=1, source_target_pairs={{0,16},{16,0},{1,17},{17,1},{2,18},{18,2},{3,19},{19,3},{4,20},{20... | collective-permute-start | bytes 1892360 | tf_op jit(solution)/shard_map/ppermute | solution.py:269
  137.4 5.3 %collective-permute-start.40 = (bf16[128,2048]{1,0:T(8,128)(2,1)S(1)}, bf16[128,2048]{1,0:T(8,128)(2,1)S(1)}, u32[]{:S(2)}, u32[]{:S(2)}) collective-permute-start(bf16[128,2048]{1,0:T(8,128)(2,1)S(1)} %collective-permute-done.39.d10), channel_id=1, source_target_pairs={{0,1},{1,0},{2,3},{3,2},{4,5},{5,4},{6,7},{7,6},{8,9},{9,8},{10,11... | collective-permute-start | bytes 1572872 | tf_op jit(solution)/shard_map/ppermute | solution.py:266
  137.4 16.7 %collective-permute-start.31 = (bf16[256,1024]{1,0:T(8,128)(2,1)S(1)}, bf16[256,1024]{1,0:T(8,128)(2,1)S(1)}, u32[]{:S(2)}, u32[]{:S(2)}) collective-permute-start(bf16[256,1024]{1,0:T(8,128)(2,1)S(1)} %collective-permute-done.29.refs_4_), channel_id=1, source_target_pairs={{4,8},{5,9},{6,10},{7,11},{8,4},{9,5},{10,6},{11,7},{20,24},{21,25... | collective-permute-start | bytes 1572872 | tf_op jit(solution)/shard_map/ppermute | solution.py:260
  140.1 14.1 %collective-permute-start.32 = (bf16[256,1024]{1,0:T(8,128)(2,1)S(1)}, bf16[256,1024]{1,0:T(8,128)(2,1)S(1)}, u32[]{:S(2)}, u32[]{:S(2)}) collective-permute-start(bf16[256,1024]{1,0:T(8,128)(2,1)S(1)} %collective-permute-done.30), channel_id=1, source_target_pairs={{4,0},{5,1},{6,2},{7,3},{8,12},{9,13},{10,14},{11,15},{20,16},{21,... | collective-permute-start | bytes 1572872 | tf_op jit(solution)/shard_map/ppermute | solution.py:260
  141.4 12.7 %collective-permute-start.34 = (bf16[112,2048]{1,0:T(8,128)(2,1)S(1)}, bf16[112,2048]{1,0:T(8,128)(2,1)S(1)}, u32[]{:S(2)}, u32[]{:S(2)}) collective-permute-start(bf16[112,2048]{1,0:T(8,128)(2,1)S(1)} %get-tuple-element.160), channel_id=1, source_target_pairs={{0,2},{1,3},{2,0},{3,1},{4,6},{5,7},{6,4},{7,5},{8,10},{9,11},{10,... | collective-permute-start | bytes 1376264 | tf_op jit(solution)/shard_map/ppermute | solution.py:263
  142.8 15.0 %collective-permute-start.49 = (bf16[256,1024]{1,0:T(8,128)(2,1)}, bf16[256,1024]{1,0:T(8,128)(2,1)S(1)}, u32[]{:S(2)}, u32[]{:S(2)}) collective-permute-start(bf16[256,1024]{1,0:T(8,128)(2,1)} %collective-permute-done.16.refs_2_), channel_id=1, source_target_pairs={{0,1},{1,0},{2,3},{3,2},{4,5},{5,4},{6,7},{7,6},{8,9},{9,8},{10,11... | collective-permute-start | bytes 1572872 | tf_op jit(solution)/shard_map/ppermute | solution.py:266
  148.3 13.1 %collective-permute-start.48 = (bf16[256,1024]{1,0:T(8,128)(2,1)S(1)}, bf16[256,1024]{1,0:T(8,128)(2,1)S(1)}, u32[]{:S(2)}, u32[]{:S(2)}) collective-permute-start(bf16[256,1024]{1,0:T(8,128)(2,1)S(1)} %pad_maximum_fusion.4.refs_0_), channel_id=1, source_target_pairs={{0,1},{1,0},{2,3},{3,2},{4,5},{5,4},{6,7},{7,6},{8,9},{9,8},{10,11... | collective-permute-start | bytes 1572872 | tf_op jit(solution)/shard_map/ppermute | solution.py:266
  154.2 14.9 %collective-permute-start.51 = (bf16[256,1024]{1,0:T(8,128)(2,1)S(1)}, bf16[256,1024]{1,0:T(8,128)(2,1)S(1)}, u32[]{:S(2)}, u32[]{:S(2)}) collective-permute-start(bf16[256,1024]{1,0:T(8,128)(2,1)S(1)} %collective-permute-done.29.refs_4_), channel_id=1, source_target_pairs={{0,2},{1,3},{2,0},{3,1},{4,6},{5,7},{6,4},{7,5},{8,10},{9,11},{10,... | collective-permute-start | bytes 1572872 | tf_op jit(solution)/shard_map/ppermute | solution.py:263
  154.7 22.6 %collective-permute-start.47 = (bf16[112,2048]{1,0:T(8,128)(2,1)S(1)}, bf16[112,2048]{1,0:T(8,128)(2,1)S(1)}, u32[]{:S(2)}, u32[]{:S(2)}) collective-permute-start(bf16[112,2048]{1,0:T(8,128)(2,1)S(1)} %get-tuple-element.179), channel_id=1, source_target_pairs={{0,2},{1,3},{2,0},{3,1},{4,6},{5,7},{6,4},{7,5},{8,10},{9,11},{10,... | collective-permute-start | bytes 1376264 | tf_op jit(solution)/shard_map/ppermute | solution.py:263
  156.3 23.1 %collective-permute-start.53 = (bf16[224,1408]{1,0:T(8,128)(2,1)S(1)}, bf16[224,1408]{1,0:T(8,128)(2,1)S(1)}, u32[]{:S(2)}, u32[]{:S(2)}) collective-permute-start(bf16[224,1408]{1,0:T(8,128)(2,1)S(1)} %get-tuple-element.202.refs_22_), channel_id=1, source_target_pairs={{0,16},{16,0},{1,17},{17,1},{2,18},{18,2},{3,19},{19,3},{4,20},{20... | collective-permute-start | bytes 1892360 | tf_op jit(solution)/shard_map/ppermute | solution.py:269
  157.8 21.0 %collective-permute-start.46 = (bf16[256,1024]{1,0:T(8,128)(2,1)S(1)}, bf16[256,1024]{1,0:T(8,128)(2,1)S(1)}, u32[]{:S(2)}, u32[]{:S(2)}) collective-permute-start(bf16[256,1024]{1,0:T(8,128)(2,1)S(1)} %collective-permute-done.31), channel_id=1, source_target_pairs={{4,0},{5,1},{6,2},{7,3},{8,12},{9,13},{10,14},{11,15},{20,16},{21,... | collective-permute-start | bytes 1572872 | tf_op jit(solution)/shard_map/ppermute | solution.py:260
  161.4 17.4 %collective-permute-start.50 = (bf16[256,1024]{1,0:T(8,128)(2,1)S(1)}, bf16[256,1024]{1,0:T(8,128)(2,1)S(1)}, u32[]{:S(2)}, u32[]{:S(2)}) collective-permute-start(bf16[256,1024]{1,0:T(8,128)(2,1)S(1)} %collective-permute-done.29.refs_4_), channel_id=1, source_target_pairs={{0,1},{1,0},{2,3},{3,2},{4,5},{5,4},{6,7},{7,6},{8,9},{9,8},{10,11... | collective-permute-start | bytes 1572872 | tf_op jit(solution)/shard_map/ppermute | solution.py:266
  169.1 10.3 %collective-permute-start.52 = (bf16[256,1024]{1,0:T(8,128)(2,1)S(1)}, bf16[256,1024]{1,0:T(8,128)(2,1)S(1)}, u32[]{:S(2)}, u32[]{:S(2)}) collective-permute-start(bf16[256,1024]{1,0:T(8,128)(2,1)S(1)} %collective-permute-done.51.refs_6_), channel_id=1, source_target_pairs={{0,1},{1,0},{2,3},{3,2},{4,5},{5,4},{6,7},{7,6},{8,9},{9,8},{10,11... | collective-permute-start | bytes 1572872 | tf_op jit(solution)/shard_map/ppermute | solution.py:266
  177.3 32.6 %collective-permute-start.62 = (bf16[704,1024]{1,0:T(8,128)(2,1)S(1)}, bf16[704,1024]{1,0:T(8,128)(2,1)S(1)}, u32[]{:S(2)}, u32[]{:S(2)}) collective-permute-start(bf16[704,1024]{1,0:T(8,128)(2,1)S(1)} %bitcast.71), channel_id=1, source_target_pairs={{0,16},{16,0},{1,17},{17,1},{2,18},{18,2},{3,19},{19,3},{4,20},{20... | collective-permute-start | bytes 4325384 | tf_op jit(solution)/shard_map/ppermute | solution.py:269
  178.8 3.3 %collective-permute-start.43 = (bf16[112,2048]{1,0:T(8,128)(2,1)S(1)}, bf16[112,2048]{1,0:T(8,128)(2,1)S(1)}, u32[]{:S(2)}, u32[]{:S(2)}) collective-permute-start(bf16[112,2048]{1,0:T(8,128)(2,1)S(1)} %collective-permute-done.34.hop), channel_id=1, source_target_pairs={{0,1},{1,0},{2,3},{3,2},{4,5},{5,4},{6,7},{7,6},{8,9},{9,8},{10,11... | collective-permute-start | bytes 1376264 | tf_op jit(solution)/shard_map/ppermute | solution.py:266
  178.8 4.4 %collective-permute-start.12 = (bf16[56,2048]{1,0:T(8,128)(2,1)S(1)}, bf16[56,2048]{1,0:T(8,128)(2,1)S(1)}, u32[]{:S(2)}, u32[]{:S(2)}) collective-permute-start(bf16[56,2048]{1,0:T(8,128)(2,1)S(1)} %copy-done.25), channel_id=1, source_target_pairs={{0,1},{1,0},{2,3},{3,2},{4,5},{5,4},{6,7},{7,6},{8,9},{9,8},{10,11... | collective-permute-start | bytes 688136 | tf_op jit(solution)/shard_map/ppermute | solution.py:266
  179.3 5.7 %collective-permute-start.20 = (bf16[112,2048]{1,0:T(8,128)(2,1)}, bf16[112,2048]{1,0:T(8,128)(2,1)S(1)}, u32[]{:S(2)}, u32[]{:S(2)}) collective-permute-start(bf16[112,2048]{1,0:T(8,128)(2,1)} %collective-permute-done.17.hop), channel_id=1, source_target_pairs={{0,1},{1,0},{2,3},{3,2},{4,5},{5,4},{6,7},{7,6},{8,9},{9,8},{10,11... | collective-permute-start | bytes 1376264 | tf_op jit(solution)/shard_map/ppermute | solution.py:266
  179.4 2.5 %collective-permute-start.42 = (bf16[56,2048]{1,0:T(8,128)(2,1)S(1)}, bf16[56,2048]{1,0:T(8,128)(2,1)S(1)}, u32[]{:S(2)}, u32[]{:S(2)}) collective-permute-start(bf16[56,2048]{1,0:T(8,128)(2,1)S(1)} %get-tuple-element.174), channel_id=1, source_target_pairs={{0,1},{1,0},{2,3},{3,2},{4,5},{5,4},{6,7},{7,6},{8,9},{9,8},{10,11... | collective-permute-start | bytes 688136 | tf_op jit(solution)/shard_map/ppermute | solution.py:266
  182.0 4.8 %collective-permute-start.54 = (bf16[112,2048]{1,0:T(8,128)(2,1)S(1)}, bf16[112,2048]{1,0:T(8,128)(2,1)S(1)}, u32[]{:S(2)}, u32[]{:S(2)}) collective-permute-start(bf16[112,2048]{1,0:T(8,128)(2,1)S(1)} %collective-permute-done.47.hop), channel_id=1, source_target_pairs={{0,1},{1,0},{2,3},{3,2},{4,5},{5,4},{6,7},{7,6},{8,9},{9,8},{10,11... | collective-permute-start | bytes 1376264 | tf_op jit(solution)/shard_map/ppermute | solution.py:266
  182.1 4.0 %collective-permute-start.45 = (bf16[56,2048]{1,0:T(8,128)(2,1)S(1)}, bf16[56,2048]{1,0:T(8,128)(2,1)S(1)}, u32[]{:S(2)}, u32[]{:S(2)}) collective-permute-start(bf16[56,2048]{1,0:T(8,128)(2,1)S(1)} %get-tuple-element.177), channel_id=1, source_target_pairs={{0,1},{1,0},{2,3},{3,2},{4,5},{5,4},{6,7},{7,6},{8,9},{9,8},{10,11... | collective-permute-start | bytes 688136 | tf_op jit(solution)/shard_map/ppermute | solution.py:266
  183.2 24.1 %collective-permute-start.41 = (bf16[128,2048]{1,0:T(8,128)(2,1)S(1)}, bf16[128,2048]{1,0:T(8,128)(2,1)S(1)}, u32[]{:S(2)}, u32[]{:S(2)}) collective-permute-start(bf16[128,2048]{1,0:T(8,128)(2,1)S(1)} %combine.5), channel_id=1, source_target_pairs={{0,4},{1,5},{2,6},{3,7},{4,0},{5,1},{6,2},{7,3},{8,12},{9,13},{10,... | collective-permute-start | bytes 1572872 | tf_op jit(solution)/shard_map/ppermute | solution.py:257
  185.1 24.7 %collective-permute-start.44 = (bf16[128,2048]{1,0:T(8,128)(2,1)S(1)}, bf16[128,2048]{1,0:T(8,128)(2,1)S(1)}, u32[]{:S(2)}, u32[]{:S(2)}) collective-permute-start(bf16[128,2048]{1,0:T(8,128)(2,1)S(1)} %combine.6), channel_id=1, source_target_pairs={{0,8},{1,9},{2,10},{3,11},{4,12},{5,13},{6,14},{7,15},{8,0},{9,1},... | collective-permute-start | bytes 1572872 | tf_op jit(solution)/shard_map/ppermute | solution.py:257
  186.1 24.3 %collective-permute-start.60 = (bf16[256,1024]{1,0:T(8,128)(2,1)S(1)}, bf16[256,1024]{1,0:T(8,128)(2,1)S(1)}, u32[]{:S(2)}, u32[]{:S(2)}) collective-permute-start(bf16[256,1024]{1,0:T(8,128)(2,1)S(1)} %broadcast_select_fusion.refs_12_), channel_id=1, source_target_pairs={{0,2},{1,3},{2,0},{3,1},{4,6},{5,7},{6,4},{7,5},{8,10},{9,11},{10,... | collective-permute-start | bytes 1572872 | tf_op jit(solution)/shard_map/ppermute | solution.py:263
  186.8 24.2 %collective-permute-start.57 = (bf16[256,1024]{1,0:T(8,128)(2,1)S(1)}, bf16[256,1024]{1,0:T(8,128)(2,1)S(1)}, u32[]{:S(2)}, u32[]{:S(2)}) collective-permute-start(bf16[256,1024]{1,0:T(8,128)(2,1)S(1)} %broadcast_select_fusion.1.refs_8_), channel_id=1, source_target_pairs={{0,2},{1,3},{2,0},{3,1},{4,6},{5,7},{6,4},{7,5},{8,10},{9,11},{10,... | collective-permute-start | bytes 1572872 | tf_op jit(solution)/shard_map/ppermute | solution.py:263
  207.3 25.0 %collective-permute-start.55 = (bf16[128,2048]{1,0:T(8,128)(2,1)S(1)}, bf16[128,2048]{1,0:T(8,128)(2,1)S(1)}, u32[]{:S(2)}, u32[]{:S(2)}) collective-permute-start(bf16[128,2048]{1,0:T(8,128)(2,1)S(1)} %combine.7), channel_id=1, source_target_pairs={{0,12},{1,13},{2,14},{3,15},{4,8},{5,9},{6,10},{7,11},{8,4},{9,5},... | collective-permute-start | bytes 1572872 | tf_op jit(solution)/shard_map/ppermute | solution.py:257
  209.8 23.6 %collective-permute-start.59 = (bf16[256,1024]{1,0:T(8,128)(2,1)S(1)}, bf16[256,1024]{1,0:T(8,128)(2,1)S(1)}, u32[]{:S(2)}, u32[]{:S(2)}) collective-permute-start(bf16[256,1024]{1,0:T(8,128)(2,1)S(1)} %broadcast_select_fusion.refs_12_), channel_id=1, source_target_pairs={{0,1},{1,0},{2,3},{3,2},{4,5},{5,4},{6,7},{7,6},{8,9},{9,8},{10,11... | collective-permute-start | bytes 1572872 | tf_op jit(solution)/shard_map/ppermute | solution.py:266
  209.9 23.5 %collective-permute-start.56 = (bf16[256,1024]{1,0:T(8,128)(2,1)S(1)}, bf16[256,1024]{1,0:T(8,128)(2,1)S(1)}, u32[]{:S(2)}, u32[]{:S(2)}) collective-permute-start(bf16[256,1024]{1,0:T(8,128)(2,1)S(1)} %broadcast_select_fusion.1.refs_8_), channel_id=1, source_target_pairs={{0,1},{1,0},{2,3},{3,2},{4,5},{5,4},{6,7},{7,6},{8,9},{9,8},{10,11... | collective-permute-start | bytes 1572872 | tf_op jit(solution)/shard_map/ppermute | solution.py:266
  210.4 23.1 %collective-permute-start.61 = (bf16[256,1024]{1,0:T(8,128)(2,1)S(1)}, bf16[256,1024]{1,0:T(8,128)(2,1)S(1)}, u32[]{:S(2)}, u32[]{:S(2)}) collective-permute-start(bf16[256,1024]{1,0:T(8,128)(2,1)S(1)} %collective-permute-done.60.refs_14_), channel_id=1, source_target_pairs={{0,1},{1,0},{2,3},{3,2},{4,5},{5,4},{6,7},{7,6},{8,9},{9,8},{10,11... | collective-permute-start | bytes 1572872 | tf_op jit(solution)/shard_map/ppermute | solution.py:266
  210.9 22.5 %collective-permute-start.58 = (bf16[256,1024]{1,0:T(8,128)(2,1)S(1)}, bf16[256,1024]{1,0:T(8,128)(2,1)S(1)}, u32[]{:S(2)}, u32[]{:S(2)}) collective-permute-start(bf16[256,1024]{1,0:T(8,128)(2,1)S(1)} %collective-permute-done.57.refs_10_), channel_id=1, source_target_pairs={{0,1},{1,0},{2,3},{3,2},{4,5},{5,4},{6,7},{7,6},{8,9},{9,8},{10,11... | collective-permute-start | bytes 1572872 | tf_op jit(solution)/shard_map/ppermute | solution.py:266
  (29 other events, 231.3 us)
